TPU v7x, 128 devices: a whole 4x4x4 slice. The times are simulated.
128 devices in a mesh: ta: 2 (over x_hi), ha: 8 (over y, x_lo), wa: 8 (over z, core).
Axes of the slice: x: 4 (x_hi: 2, x_lo: 2; x = x_hi * 2 + x_lo), y: 4, z: 4, core: 2. Of those that a mesh axis runs over, the one named last changes fastest.
Arguments:
- tokens: bfloat16 [8, 56, 56, 384], P('ta', 'ha', 'wa'), may hold values from -6 to 6
- upstream: bfloat16 [8, 56, 56, 384], P('ta', 'ha', 'wa'), may hold values from -6 to 6
- qkv_one: bfloat16 [384, 1152], replicated, may hold values from -0.3125 to 0.3125
- proj_one: bfloat16 [384, 384], replicated, may hold values from -0.3125 to 0.3125
- table_one: float32 [12, 1183], replicated, may hold values from -4 to 320
- expand_one: bfloat16 [384, 1536], replicated, may hold values from -0.3125 to 0.3125
- contract_one: bfloat16 [1536, 384], replicated, may hold values from -0.15625 to 0.15625
- qkv_two: bfloat16 [384, 1152], replicated, may hold values from -0.3125 to 0.3125
- proj_two: bfloat16 [384, 384], replicated, may hold values from -0.3125 to 0.3125
- table_two: float32 [12, 1183], replicated, may hold values from -4 to 320
- expand_two: bfloat16 [384, 1536], replicated, may hold values from -0.3125 to 0.3125
- contract_two: bfloat16 [1536, 384], replicated, may hold values from -0.15625 to 0.15625
Outputs:
- grad_tokens: bfloat16 [8, 56, 56, 384], P('ta', 'ha', 'wa')
- grad_qkv_one: float32 [384, 1152], P(('ta', 'ha', 'wa'))
- grad_proj_one: float32 [384, 384], P(('ta', 'ha', 'wa'))
- grad_table_one: float32 [12, 1183], replicated
- grad_expand_one: float32 [384, 1536], P(('ta', 'ha', 'wa'))
- grad_contract_one: float32 [1536, 384], P(('ta', 'ha', 'wa'))
- grad_qkv_two: float32 [384, 1152], P(('ta', 'ha', 'wa'))
- grad_proj_two: float32 [384, 384], P(('ta', 'ha', 'wa'))
- grad_table_two: float32 [12, 1183], replicated
- grad_expand_two: float32 [384, 1536], P(('ta', 'ha', 'wa'))
- grad_contract_two: float32 [1536, 384], P(('ta', 'ha', 'wa'))
All inputs are finite; a program needn't handle non-finite values.
Results may differ from a plain program's by a relative error of at most 0.04.
Values may be sent and summed in bfloat16 or wider, within the bound.
No kernel may reach another device: no remote copies, remote signals or barrier semaphores. Data moves between devices by JAX's collectives and lax.ppermute only.
A program may use at most 256 MiB of HBM per device.

v0:
```python
import jax
import jax.numpy as jnp
from jax import lax
from jax.sharding import PartitionSpec as P

HEADS = 12
WT = 4
WH = 7
WW = 7


epsilon = 1e-05


def for_sending(shard):

    def short(part):
        return part.astype(jnp.bfloat16) if part.dtype == jnp.float32 else part

    return jax.tree.map(short, shard)


def passed_along(block, axis, distance):
    devices = range(lax.axis_size(axis))
    route = [((i - distance) % len(devices), i) for i in devices]
    return lax.ppermute(block, axis, route)


def layer_norm(values_in):
    widened = values_in.astype(jnp.float32)
    average = jnp.mean(widened, axis=-1, keepdims=True)
    centred = widened - average
    spread = jnp.mean(centred * centred, axis=-1, keepdims=True)
    return (centred * lax.rsqrt(spread + epsilon)).astype(jnp.bfloat16)


def offset_onehot(extent):
    places = jnp.arange(extent, dtype=jnp.int32)
    offsets = places[:, None] - places[None, :] + (extent - 1)
    entries = jnp.arange(2 * extent - 1, dtype=jnp.int32)
    return (entries[:, None, None] == offsets[None]).astype(jnp.float32)


def position_table(table):
    shaped = table.reshape(HEADS, 2 * WT - 1, 2 * WH - 1, 2 * WW - 1)
    along_w = jnp.einsum(
        "htrc,cab->htrab", shaped, offset_onehot(WW), precision=lax.Precision.HIGHEST
    )
    along_h = jnp.einsum(
        "htrab,rij->htiajb", along_w, offset_onehot(WH), precision=lax.Precision.HIGHEST
    )
    full_bias = jnp.einsum(
        "htiajb,tkl->hkialjb", along_h, offset_onehot(WT), precision=lax.Precision.HIGHEST
    )
    return full_bias.reshape(HEADS, WT * WH * WW, WT * WH * WW)


def into_windows(grid):
    frames, height, width, depth = grid.shape
    blocks = grid.reshape(frames // WT, WT, height // WH, WH, width // WW, WW, depth)
    return blocks.transpose(0, 2, 4, 1, 3, 5, 6).reshape(-1, WT * WH * WW, depth)


def from_windows(windows, grid_shape):
    frames, height, width, depth = grid_shape
    blocks = windows.reshape(frames // WT, height // WH, width // WW, WT, WH, WW, depth)
    return blocks.transpose(0, 3, 1, 4, 2, 5, 6).reshape(grid_shape)


def window_attention(windows, weight_qkv, weight_proj, table, probe_qkv, probe_proj):
    window_count, length, depth = windows.shape
    head_size = depth // HEADS
    flat_rows = windows.reshape(window_count * length, depth)
    projected = (
        jnp.dot(flat_rows, weight_qkv, preferred_element_type=jnp.float32) + probe_qkv
    ).astype(jnp.bfloat16)
    projected = projected.reshape(window_count, length, 3, HEADS, head_size)
    queries = projected[:, :, 0]
    keys_all = projected[:, :, 1]
    values_all = projected[:, :, 2]
    position_bias = position_table(table)
    scores = jnp.einsum(
        "blhe,bmhe->bhlm", queries, keys_all, preferred_element_type=jnp.float32
    ) * head_size ** (-0.5)
    scores = scores + position_bias[None]
    weights_soft = jax.nn.softmax(scores, axis=-1).astype(jnp.bfloat16)
    context = jnp.einsum(
        "bhlm,bmhe->blhe", weights_soft, values_all, preferred_element_type=jnp.float32
    ).astype(jnp.bfloat16)
    context = context.reshape(window_count * length, depth)
    result = (
        jnp.dot(context, weight_proj, preferred_element_type=jnp.float32) + probe_proj
    ).astype(jnp.bfloat16)
    return (result.reshape(window_count, length, depth), (flat_rows, context))


def feed_forward(hidden_in, weight_expand, weight_contract, probe_expand, probe_contract):
    normed = layer_norm(hidden_in).reshape(-1, hidden_in.shape[-1])
    expanded = jnp.dot(normed, weight_expand, preferred_element_type=jnp.float32) + probe_expand
    activated = jax.nn.gelu(expanded, approximate=False).astype(jnp.bfloat16)
    contracted = (
        jnp.dot(activated, weight_contract, preferred_element_type=jnp.float32) + probe_contract
    )
    result = (hidden_in.astype(jnp.float32) + contracted.reshape(hidden_in.shape)).astype(
        jnp.bfloat16
    )
    return (result, (normed, activated))


def outer_sum(stored, cotangent):
    return lax.dot_general(
        stored,
        cotangent.astype(jnp.bfloat16),
        (((0,), (0,)), ((), ())),
        preferred_element_type=jnp.float32,
    )


def edge_of(grid, dim, width, direction):
    extent = grid.shape[dim]
    if direction < 0:
        return lax.slice_in_dim(grid, 0, width, axis=dim)
    return lax.slice_in_dim(grid, extent - width, extent, axis=dim)


def rejoin(grid, dim, width, direction, arrived):
    extent = grid.shape[dim]
    if direction < 0:
        return jnp.concatenate([lax.slice_in_dim(grid, width, extent, axis=dim), arrived], axis=dim)
    return jnp.concatenate([arrived, lax.slice_in_dim(grid, 0, extent - width, axis=dim)], axis=dim)


def roll_grid(grid, direction):
    grid = rejoin(
        grid,
        0,
        WT // 2,
        direction,
        passed_along(for_sending(edge_of(grid, 0, WT // 2, direction)), "ta", direction),
    )
    grid = rejoin(
        grid,
        1,
        WH // 2,
        direction,
        passed_along(for_sending(edge_of(grid, 1, WH // 2, direction)), "ha", direction),
    )
    grid = rejoin(
        grid,
        2,
        WW // 2,
        direction,
        passed_along(for_sending(edge_of(grid, 2, WW // 2, direction)), "wa", direction),
    )
    return grid


def body(
    tokens,
    upstream,
    qkv_one,
    proj_one,
    table_one,
    expand_one,
    contract_one,
    qkv_two,
    proj_two,
    table_two,
    expand_two,
    contract_two,
):
    grid_shape = tokens.shape
    depth = grid_shape[3]
    hidden_units = expand_one.shape[1]
    row_count = grid_shape[0] * grid_shape[1] * grid_shape[2]

    def zeros_for(columns):
        return jnp.zeros((row_count, columns), jnp.float32)

    def part_one(inputs, table, probe_set):
        attended, stored = window_attention(
            into_windows(layer_norm(inputs)), qkv_one, proj_one, table, probe_set[0], probe_set[1]
        )
        mixed = (
            inputs.astype(jnp.float32) + from_windows(attended, grid_shape).astype(jnp.float32)
        ).astype(jnp.bfloat16)
        after, kept = feed_forward(mixed, expand_one, contract_one, probe_set[2], probe_set[3])
        return ((after, layer_norm(after)), stored + kept)

    probes_one = (zeros_for(3 * depth), zeros_for(depth), zeros_for(hidden_units), zeros_for(depth))
    (after_one, normed), pull_one, stored_one = jax.vjp(
        part_one, tokens, table_one, probes_one, has_aux=True
    )
    rolled = roll_grid(normed, -1)

    def part_two(shifted, table, probe_set):
        attended, stored = window_attention(
            into_windows(shifted), qkv_two, proj_two, table, probe_set[0], probe_set[1]
        )
        return (from_windows(attended, grid_shape), stored)

    attended_two, pull_two, stored_two = jax.vjp(
        part_two, rolled, table_two, (zeros_for(3 * depth), zeros_for(depth)), has_aux=True
    )
    returned = roll_grid(attended_two, 1)

    def part_three(carried, branch, probe_set):
        mixed = (carried.astype(jnp.float32) + branch.astype(jnp.float32)).astype(jnp.bfloat16)
        return feed_forward(mixed, expand_two, contract_two, probe_set[0], probe_set[1])

    final_out, pull_three, stored_three = jax.vjp(
        part_three, after_one, returned, (zeros_for(hidden_units), zeros_for(depth)), has_aux=True
    )
    grad_carried, grad_branch, probe_three = pull_three(upstream)
    grad_attended = roll_grid(grad_branch, -1)
    grad_shifted, table_part_two, probe_two = pull_two(grad_attended)
    second_grads = (
        outer_sum(stored_two[0], probe_two[0]),
        outer_sum(stored_two[1], probe_two[1]),
        outer_sum(stored_three[0], probe_three[0]),
        outer_sum(stored_three[1], probe_three[1]),
    )
    grad_normed = roll_grid(grad_shifted, 1)
    grad_tokens, table_part_one, probe_one = pull_one((grad_carried, grad_normed))
    first_grads = (
        outer_sum(stored_one[0], probe_one[0]),
        outer_sum(stored_one[1], probe_one[1]),
        outer_sum(stored_one[2], probe_one[2]),
        outer_sum(stored_one[3], probe_one[3]),
    )
    summed = (
        lax.psum_scatter(first_grads[0], ("ta", "ha", "wa"), scatter_dimension=0, tiled=True),
        lax.psum_scatter(first_grads[1], ("ta", "ha", "wa"), scatter_dimension=0, tiled=True),
        lax.psum_scatter(first_grads[2], ("ta", "ha", "wa"), scatter_dimension=0, tiled=True),
        lax.psum_scatter(first_grads[3], ("ta", "ha", "wa"), scatter_dimension=0, tiled=True),
        lax.psum_scatter(second_grads[0], ("ta", "ha", "wa"), scatter_dimension=0, tiled=True),
        lax.psum_scatter(second_grads[1], ("ta", "ha", "wa"), scatter_dimension=0, tiled=True),
        lax.psum_scatter(second_grads[2], ("ta", "ha", "wa"), scatter_dimension=0, tiled=True),
        lax.psum_scatter(second_grads[3], ("ta", "ha", "wa"), scatter_dimension=0, tiled=True),
    )
    first_grads = tuple(summed[:4])
    second_grads = tuple(summed[4:])
    table_grad_one, table_grad_two = lax.psum((table_part_one, table_part_two), ("ta", "ha", "wa"))
    return (
        grad_tokens,
        first_grads[0],
        first_grads[1],
        table_grad_one,
        first_grads[2],
        first_grads[3],
        second_grads[0],
        second_grads[1],
        table_grad_two,
        second_grads[2],
        second_grads[3],
    )


def solution(mesh):
    placed = (
        P("ta", "ha", "wa", None),
        P("ta", "ha", "wa", None),
        P(),
        P(),
        P(),
        P(),
        P(),
        P(),
        P(),
        P(),
        P(),
        P(),
    )
    return jax.shard_map(
        body,
        mesh=mesh,
        in_specs=placed,
        out_specs=(
            P("ta", "ha", "wa", None),
            P(("ta", "ha", "wa"), None),
            P(("ta", "ha", "wa"), None),
            P(),
            P(("ta", "ha", "wa"), None),
            P(("ta", "ha", "wa"), None),
            P(("ta", "ha", "wa"), None),
            P(("ta", "ha", "wa"), None),
            P(),
            P(("ta", "ha", "wa"), None),
            P(("ta", "ha", "wa"), None),
        ),
        check_vma=False,
    )
```

profile of v0, /device:TPU:1, one launch (start us, length us, event | category | flops | bytes accessed | tf_op | source)
XLA Modules:
  0.0 1419.8 jit_solution(3367892516801581992)
XLA Ops:
  11.8 23.9 %convolution_bitcast_fusion.1 = f32[12,7,7,7,7,7]{0,4,5,3,1,2:T(8,128)} fusion(f32[12,7,13,7,7]{2,4,1,0,3:T(8,128)S(1)} %convolution_bitcast_fusion.3, s32[7,7]{1,0:T(8,128)S(1)} %subtract_add_fusion), kind=kOutput, calls=%fused_computation.17 | convolution fusion | flops 31463340 | bytes 1020964 | tf_op jit(solution)/shard_map/jvp(htrab,rij->htiajb)/dot_general | solution.py:49
  35.7 30.5 %fusion.14 = f32[12,4,7,7,4,7,7]{0,4,6,5,3,2,1:T(4,128)} fusion(f32[12,7,7,7,7,7]{0,4,5,3,1,2:T(8,128)} %convolution_bitcast_fusion.1, s32[4,4]{1,0:T(4,128)S(1)} %subtract_add_fusion.1), kind=kOutput, calls=%fused_computation.12 | convolution fusion | flops 38723440 | bytes 2650768 | tf_op jit(solution)/shard_map/jvp(htiajb,tkl->hkialjb)/dot_general | solution.py:52
  66.1 49.7 %copy.125 = f32[12,4,7,7,4,7,7]{3,2,1,6,5,4,0:T(8,128)} copy(f32[12,4,7,7,4,7,7]{0,4,6,5,3,2,1:T(4,128)} %fusion.14) | data formatting | bytes 3687936 | tf_op jit(solution)/shard_map/jvp()/broadcast_in_dim;jvp()/reshape | solution.py:85
  115.9 31.9 %reshape.468 = f32[12,196,196]{1,2,0:T(8,128)} reshape(f32[12,4,7,7,4,7,7]{3,2,1,6,5,4,0:T(8,128)} %copy.125) | data formatting | bytes 3687936 | tf_op jit(solution)/shard_map/jvp()/broadcast_in_dim;jvp()/reshape | solution.py:85
  176.6 24.3 %convolution_bitcast_fusion = f32[12,7,7,7,7,7]{0,4,5,3,1,2:T(8,128)} fusion(f32[12,7,13,7,7]{2,4,1,0,3:T(8,128)S(1)} %convolution_bitcast_fusion.2, s32[7,7]{1,0:T(8,128)S(1)} %subtract_add_fusion), kind=kOutput, calls=%fused_computation.16 | convolution fusion | flops 31463340 | bytes 1020964 | tf_op jit(solution)/shard_map/jvp(htrab,rij->htiajb)/dot_general | solution.py:49
  200.9 30.4 %fusion.17 = f32[12,4,7,7,4,7,7]{0,4,6,5,3,2,1:T(4,128)} fusion(f32[12,7,7,7,7,7]{0,4,5,3,1,2:T(8,128)} %convolution_bitcast_fusion, s32[4,4]{1,0:T(4,128)S(1)} %subtract_add_fusion.1), kind=kOutput, calls=%fused_computation.13 | convolution fusion | flops 38723440 | bytes 2650768 | tf_op jit(solution)/shard_map/jvp(htiajb,tkl->hkialjb)/dot_general | solution.py:52
  232.0 49.7 %copy.126 = f32[12,4,7,7,4,7,7]{3,2,1,6,5,4,0:T(8,128)} copy(f32[12,4,7,7,4,7,7]{0,4,6,5,3,2,1:T(4,128)} %fusion.17) | data formatting | bytes 3687936 | tf_op jit(solution)/shard_map/jvp()/broadcast_in_dim;jvp()/reshape | solution.py:85
  281.7 31.6 %reshape.470 = f32[12,196,196]{1,2,0:T(8,128)} reshape(f32[12,4,7,7,4,7,7]{3,2,1,6,5,4,0:T(8,128)} %copy.126) | data formatting | bytes 3687936 | tf_op jit(solution)/shard_map/jvp()/broadcast_in_dim;jvp()/reshape | solution.py:85
  372.6 5.6 collective-permute-start.8
  413.6 38.9 %reshape.446 = f32[12,4,7,7,4,7,7]{6,5,4,3,2,1,0:T(8,128)} reshape(f32[12,196,196]{2,1,0:T(8,128)} %copy.101) | data formatting | bytes 3687936 | tf_op jit(solution)/shard_map/transpose(jvp())/reshape | solution.py:55
  474.9 353.6 %fusion.198 = (f32[16,384]{1,0:T(8,128)}, f32[16,384]{1,0:T(8,128)}) fusion(f32[1536,384]{1,0:T(8,128)} %fusion.212, f32[1536,384]{1,0:T(8,128)S(1)} %copy-done.7), kind=kCustom, calls=%all-reduce-scatter.2 | all-reduce-scatter fusion | flops 1572865 | bytes 4767744
  835.0 6.8 collective-permute-start.43
  841.8 9.5 collective-permute-start.75
  851.6 51.6 %fusion.23 = f32[7,7,12,7,7,7]{3,5,1,4,0,2:T(8,128)} fusion(f32[4,4,12,7,7,7,7]{6,5,1,4,3,0,2:T(8,128)} %bitcast.259, pred[7,4,4,1,1,1,1]{0,2,1,6,5,4,3:T(4,128)(4,1)S(1)} %copy-done.79), kind=kOutput, calls=%fused_computation.15 | convolution fusion | flops 38723328 | bytes 2650816 | tf_op jit(solution)/shard_map/transpose(jvp(htiajb,tkl->hkialjb))/dot_general | solution.py:52
  903.2 35.1 %copy.103 = f32[7,7,12,7,7,7]{1,5,0,4,3,2:T(8,128)} copy(f32[7,7,12,7,7,7]{3,5,1,4,0,2:T(8,128)} %fusion.23) | data formatting | bytes 1613472 | tf_op jit(solution)/shard_map/transpose(jvp(htrab,rij->htiajb))/transpose;transpose(jvp(htiajb,tkl->hkialjb))/transpose | solution.py:49
  938.3 7.3 collective-permute-start.40
  949.2 6.8 collective-permute-start.38
  956.0 4.9 collective-permute-start.37
  962.5 23.7 %fusion.163 = f32[12,7,7,7,13,1]{4,3,5,2,1,0:T(8,128)S(1)} fusion(f32[7,7,12,7,7,7]{1,5,0,4,3,2:T(8,128)} %copy.103, s32[7,7]{1,0:T(8,128)S(1)} %copy-done.57), kind=kOutput, calls=%fused_computation.234 | convolution fusion | flops 31463340 | bytes 1020964 | tf_op jit(solution)/shard_map/transpose(jvp(htrab,rij->htiajb))/dot_general | solution.py:49
  1003.9 38.9 %reshape.444 = f32[12,4,7,7,4,7,7]{6,5,4,3,2,1,0:T(8,128)} reshape(f32[12,196,196]{2,1,0:T(8,128)} %copy.98) | data formatting | bytes 3687936 | tf_op jit(solution)/shard_map/transpose(jvp())/reshape | solution.py:55
  1053.3 51.6 %fusion.20 = f32[7,7,12,7,7,7]{3,5,1,4,0,2:T(8,128)} fusion(f32[4,4,12,7,7,7,7]{6,5,1,4,3,0,2:T(8,128)} %bitcast.260, pred[7,4,4,1,1,1,1]{0,2,1,6,5,4,3:T(4,128)(4,1)S(1)} %copy-done.78), kind=kOutput, calls=%fused_computation.14 | convolution fusion | flops 38723328 | bytes 2650816 | tf_op jit(solution)/shard_map/transpose(jvp(htiajb,tkl->hkialjb))/dot_general | solution.py:52
  1104.9 35.0 %copy.100 = f32[7,7,12,7,7,7]{1,5,0,4,3,2:T(8,128)} copy(f32[7,7,12,7,7,7]{3,5,1,4,0,2:T(8,128)} %fusion.20) | data formatting | bytes 1613472 | tf_op jit(solution)/shard_map/transpose(jvp(htrab,rij->htiajb))/transpose;transpose(jvp(htiajb,tkl->hkialjb))/transpose | solution.py:49
  1155.2 27.2 %fusion.165 = f32[12,7,7,7,13,1]{4,3,5,2,1,0:T(8,128)} fusion(f32[7,7,12,7,7,7]{1,5,0,4,3,2:T(8,128)} %copy.100, s32[7,7]{1,0:T(8,128)S(1)} %copy-done.57), kind=kOutput, calls=%fused_computation.235 | convolution fusion | flops 31463340 | bytes 1020964 | tf_op jit(solution)/shard_map/transpose(jvp(htrab,rij->htiajb))/dot_general | solution.py:49
  1300.9 108.5 %all-reduce.22.cloned.1.call-done = (f32[12,1183]{1,0:T(8,128)}, f32[12,1183]{1,0:T(8,128)}) async-done(((f32[12,1183]{1,0:T(8,128)}, f32[12,1183]{1,0:T(8,128)}), (f32[12,1183]{1,0:T(8,128)}, f32[12,1183]{1,0:T(8,128)})) %all-reduce.22.cloned.1.call-update) | async-done | bytes 113584 | tf_op jit(solution)/shard_map/psum | solution.py:243
  (470 shorter events, 325.9 us)
Async XLA Ops:
  7.2 1289.3 %all-reduce.24.cloned.1.call-start = ((), (), s32[]{:S(2)}) async-start(), calls=%async_computation.1 | async-start | bytes 18874368
  168.5 144.7 %collective-permute-start = (bf16[2,7,7,384]{3,2,1,0:T(8,128)(2,1)}, bf16[2,7,7,384]{3,2,1,0:T(8,128)(2,1)}, u32[]{:S(2)}, u32[]{:S(2)}) collective-permute-start(bf16[2,7,7,384]{3,2,1,0:T(8,128)(2,1)} %get-tuple-element.56), channel_id=1, source_target_pairs={{64,0},{0,64},{65,1},{1,65},{66,2},{2,66},{67,3},{3,67},{68,4},{4,... | collective-permute-start | bytes 225800 | tf_op jit(solution)/shard_map/ppermute | solution.py:26
  408.3 44.2 %collective-permute-start.11 = (bf16[4,7,3,384]{3,2,1,0:T(4,128)(2,1)S(1)}, bf16[4,7,3,384]{3,2,1,0:T(4,128)(2,1)S(1)}, u32[]{:S(2)}, u32[]{:S(2)}) collective-permute-start(bf16[4,7,3,384]{3,2,1,0:T(4,128)(2,1)S(1)} %fusion.153), channel_id=1, source_target_pairs={{7,0},{0,1},{1,2},{2,3},{3,4},{4,5},{5,6},{6,7},{15,8},{8,9},{9,10... | collective-permute-start | bytes 193544 | tf_op jit(solution)/shard_map/ppermute | solution.py:26
  829.3 126.7 %collective-permute-start.42 = (f32[16,384]{1,0:T(8,128)}, f32[16,384]{1,0:T(8,128)S(1)}, u32[]{:S(2)}, u32[]{:S(2)}) collective-permute-start(f32[16,384]{1,0:T(8,128)} %get-tuple-element.43), channel_id=1, source_target_pairs={{0,31},{1,32},{2,33},{3,34},{4,35},{5,36},{6,37},{7,38},{8,39},{9,... | collective-permute-start | bytes 73736
  830.6 130.3 %collective-permute-start.41 = (f32[16,384]{1,0:T(8,128)}, f32[16,384]{1,0:T(8,128)S(1)}, u32[]{:S(2)}, u32[]{:S(2)}) collective-permute-start(f32[16,384]{1,0:T(8,128)} %get-tuple-element.43), channel_id=1, source_target_pairs={{0,30},{1,31},{2,32},{3,33},{4,34},{5,35},{6,36},{7,37},{8,38},{9,... | collective-permute-start | bytes 73736
  835.0 110.6 %collective-permute-start.43 = (f32[12,384]{1,0:T(8,128)S(1)}, f32[12,384]{1,0:T(8,128)S(1)}, u32[]{:S(2)}, u32[]{:S(2)}) collective-permute-start(f32[12,384]{1,0:T(8,128)S(1)} %slice.166), channel_id=1, source_target_pairs={{0,32},{1,33},{2,34},{3,35},{4,36},{5,37},{6,38},{7,39},{8,40},{9,... | collective-permute-start | bytes 55304
  841.8 107.3 %collective-permute-start.75 = (f32[12,384]{1,0:T(8,128)S(1)}, f32[12,384]{1,0:T(8,128)S(1)}, u32[]{:S(2)}, u32[]{:S(2)}) collective-permute-start(f32[12,384]{1,0:T(8,128)S(1)} %slice.167), channel_id=1, source_target_pairs={{0,32},{1,33},{2,34},{3,35},{4,36},{5,37},{6,38},{7,39},{8,40},{9,... | collective-permute-start | bytes 55304
  851.4 558.1 %all-reduce.22.cloned.1.call-start = ((), (), s32[]{:S(2)}) async-start(), calls=%async_computation | async-start | bytes 327680 | tf_op jit(solution)/shard_map/psum | solution.py:243
  938.3 48.0 %collective-permute-start.40 = (f32[16,384]{1,0:T(8,128)S(1)}, f32[16,384]{1,0:T(8,128)S(1)}, u32[]{:S(2)}, u32[]{:S(2)}) collective-permute-start(f32[16,384]{1,0:T(8,128)S(1)} %copy-done.70), channel_id=1, source_target_pairs={{0,29},{1,30},{2,31},{3,32},{4,33},{5,34},{6,35},{7,36},{8,37},{9,... | collective-permute-start | bytes 73736
  945.6 42.1 %collective-permute-start.39 = (f32[16,384]{1,0:T(8,128)S(1)}, f32[16,384]{1,0:T(8,128)S(1)}, u32[]{:S(2)}, u32[]{:S(2)}) collective-permute-start(f32[16,384]{1,0:T(8,128)S(1)} %copy-done.70), channel_id=1, source_target_pairs={{0,28},{1,29},{2,30},{3,31},{4,32},{5,33},{6,34},{7,35},{8,36},{9,... | collective-permute-start | bytes 73736
  949.2 39.8 %collective-permute-start.38 = (f32[16,384]{1,0:T(8,128)S(1)}, f32[16,384]{1,0:T(8,128)S(1)}, u32[]{:S(2)}, u32[]{:S(2)}) collective-permute-start(f32[16,384]{1,0:T(8,128)S(1)} %copy-done.70), channel_id=1, source_target_pairs={{0,27},{1,28},{2,29},{3,30},{4,31},{5,32},{6,33},{7,34},{8,35},{9,... | collective-permute-start | bytes 73736
  986.2 56.6 %collective-permute-start.35 = (f32[16,384]{1,0:T(8,128)S(1)}, f32[16,384]{1,0:T(8,128)S(1)}, u32[]{:S(2)}, u32[]{:S(2)}) collective-permute-start(f32[16,384]{1,0:T(8,128)S(1)} %copy-done.70), channel_id=1, source_target_pairs={{0,24},{1,25},{2,26},{3,27},{4,28},{5,29},{6,30},{7,31},{8,32},{9,... | collective-permute-start | bytes 73736
  987.7 58.5 %collective-permute-start.34 = (f32[16,384]{1,0:T(8,128)S(1)}, f32[16,384]{1,0:T(8,128)S(1)}, u32[]{:S(2)}, u32[]{:S(2)}) collective-permute-start(f32[16,384]{1,0:T(8,128)S(1)} %copy-done.70), channel_id=1, source_target_pairs={{0,23},{1,24},{2,25},{3,26},{4,27},{5,28},{6,29},{7,30},{8,31},{9,... | collective-permute-start | bytes 73736
  989.0 58.4 %collective-permute-start.33 = (f32[16,384]{1,0:T(8,128)S(1)}, f32[16,384]{1,0:T(8,128)S(1)}, u32[]{:S(2)}, u32[]{:S(2)}) collective-permute-start(f32[16,384]{1,0:T(8,128)S(1)} %copy-done.70), channel_id=1, source_target_pairs={{0,22},{1,23},{2,24},{3,25},{4,26},{5,27},{6,28},{7,29},{8,30},{9,... | collective-permute-start | bytes 73736
  992.4 57.1 %collective-permute-start.32 = (f32[16,384]{1,0:T(8,128)S(1)}, f32[16,384]{1,0:T(8,128)S(1)}, u32[]{:S(2)}, u32[]{:S(2)}) collective-permute-start(f32[16,384]{1,0:T(8,128)S(1)} %copy-done.70), channel_id=1, source_target_pairs={{0,21},{1,22},{2,23},{3,24},{4,25},{5,26},{6,27},{7,28},{8,29},{9,... | collective-permute-start | bytes 73736
  994.9 56.4 %collective-permute-start.31 = (f32[16,384]{1,0:T(8,128)S(1)}, f32[16,384]{1,0:T(8,128)S(1)}, u32[]{:S(2)}, u32[]{:S(2)}) collective-permute-start(f32[16,384]{1,0:T(8,128)S(1)} %copy-done.70), channel_id=1, source_target_pairs={{0,20},{1,21},{2,22},{3,23},{4,24},{5,25},{6,26},{7,27},{8,28},{9,... | collective-permute-start | bytes 73736
  1042.8 97.1 %collective-permute-start.30 = (f32[16,384]{1,0:T(8,128)S(1)}, f32[16,384]{1,0:T(8,128)S(1)}, u32[]{:S(2)}, u32[]{:S(2)}) collective-permute-start(f32[16,384]{1,0:T(8,128)S(1)} %copy-done.70), channel_id=1, source_target_pairs={{0,19},{1,20},{2,21},{3,22},{4,23},{5,24},{6,25},{7,26},{8,27},{9,... | collective-permute-start | bytes 73736
  1046.1 98.6 %collective-permute-start.29 = (f32[16,384]{1,0:T(8,128)S(1)}, f32[16,384]{1,0:T(8,128)S(1)}, u32[]{:S(2)}, u32[]{:S(2)}) collective-permute-start(f32[16,384]{1,0:T(8,128)S(1)} %copy-done.70), channel_id=1, source_target_pairs={{0,18},{1,19},{2,20},{3,21},{4,22},{5,23},{6,24},{7,25},{8,26},{9,... | collective-permute-start | bytes 73736
  1047.4 99.4 %collective-permute-start.28 = (f32[16,384]{1,0:T(8,128)S(1)}, f32[16,384]{1,0:T(8,128)S(1)}, u32[]{:S(2)}, u32[]{:S(2)}) collective-permute-start(f32[16,384]{1,0:T(8,128)S(1)} %copy-done.70), channel_id=1, source_target_pairs={{0,17},{1,18},{2,19},{3,20},{4,21},{5,22},{6,23},{7,24},{8,25},{9,... | collective-permute-start | bytes 73736
  1049.5 100.0 %collective-permute-start.27 = (f32[16,384]{1,0:T(8,128)S(1)}, f32[16,384]{1,0:T(8,128)S(1)}, u32[]{:S(2)}, u32[]{:S(2)}) collective-permute-start(f32[16,384]{1,0:T(8,128)S(1)} %copy-done.70), channel_id=1, source_target_pairs={{0,16},{1,17},{2,18},{3,19},{4,20},{5,21},{6,22},{7,23},{8,24},{9,... | collective-permute-start | bytes 73736
  1051.4 102.3 %collective-permute-start.26 = (f32[16,384]{1,0:T(8,128)S(1)}, f32[16,384]{1,0:T(8,128)S(1)}, u32[]{:S(2)}, u32[]{:S(2)}) collective-permute-start(f32[16,384]{1,0:T(8,128)S(1)} %copy-done.70), channel_id=1, source_target_pairs={{0,15},{1,16},{2,17},{3,18},{4,19},{5,20},{6,21},{7,22},{8,23},{9,... | collective-permute-start | bytes 73736
  1139.9 42.5 %collective-permute-start.25 = (f32[16,384]{1,0:T(8,128)S(1)}, f32[16,384]{1,0:T(8,128)S(1)}, u32[]{:S(2)}, u32[]{:S(2)}) collective-permute-start(f32[16,384]{1,0:T(8,128)S(1)} %copy-done.70), channel_id=1, source_target_pairs={{0,14},{1,15},{2,16},{3,17},{4,18},{5,19},{6,20},{7,21},{8,22},{9,... | collective-permute-start | bytes 73736
  1146.9 40.7 %collective-permute-start.23 = (f32[16,384]{1,0:T(8,128)S(1)}, f32[16,384]{1,0:T(8,128)S(1)}, u32[]{:S(2)}, u32[]{:S(2)}) collective-permute-start(f32[16,384]{1,0:T(8,128)S(1)} %copy-done.70), channel_id=1, source_target_pairs={{0,12},{1,13},{2,14},{3,15},{4,16},{5,17},{6,18},{7,19},{8,20},{9,... | collective-permute-start | bytes 73736
  1149.5 40.1 %collective-permute-start.22 = (f32[16,384]{1,0:T(8,128)S(1)}, f32[16,384]{1,0:T(8,128)S(1)}, u32[]{:S(2)}, u32[]{:S(2)}) collective-permute-start(f32[16,384]{1,0:T(8,128)S(1)} %copy-done.70), channel_id=1, source_target_pairs={{0,11},{1,12},{2,13},{3,14},{4,15},{5,16},{6,17},{7,18},{8,19},{9,... | collective-permute-start | bytes 73736
  (135 other events, 1893.9 us)
Sparse Core Ops, SparseCore 0:
  851.5 166.7 all-reduce.23
  1272.8 136.6 all-reduce.21
where the time goes:
time: 1430 us; the launch traced here: 1420 us
  local copies, waits for them, and re-layouts  367 us (26%)
  blocking collectives  354 us (25%)
  matrix products  333 us (23%)
  starting transfers between devices  204 us (14%)
  waiting for transfers between devices  128 us (9%)
  other arithmetic  17.2 us (1%)
  between operations  16.9 us (1%)
    unnamed x1, blocking collectives  354 us
    unnamed x65, starting transfers between devices  177 us
    dot_general x4, matrix products, position_table(): jnp.einsum('htiajb,tkl->hkialjb', along_h, offset_onehot(WT), precision=l...  164 us
    reshape x4, local copies, waits for them, and re-layouts, window_attention(): scores = scores + position_bias[None]  163 us
    psum x1, waiting for transfers between devices, body(): lax.psum((table_part_one, table_part_two), ('ta', 'ha', 'wa'))  109 us
    dot_general x4, matrix products, position_table(): jnp.einsum('htrab,rij->htiajb', along_w, offset_onehot(WH), precision=lax...  99.1 us
    reshape x2, local copies, waits for them, and re-layouts, position_table(): return full_bias.reshape(HEADS, WT * WH * WW, WT * WH * WW)  77.8 us
    transpose x2, local copies, waits for them, and re-layouts, position_table(): jnp.einsum('htrab,rij->htiajb', along_w, offset_onehot(WH), precision=lax...  70.1 us
  transfers between devices with their start and end apart: 78, of which 11 were waited for; matrix products, arithmetic and copies ran while one was open for 34% of the time, Pallas kernels for 0%

commit v1 on v0

v1 whole, which is shorter than its diff:
```python
import jax
import jax.numpy as jnp
from jax import lax
from jax.experimental import pallas as pl
from jax.experimental.pallas import tpu as pltpu
from jax.sharding import PartitionSpec as P

HEADS = 12
WT = 4
WH = 7
WW = 7
PITCH = 8
ROWS = WT * WH * PITCH
D = 384
FF = 1536
HD = 32
TABLE = 1183
TPAD = 1280
UPAD = 768
STEP = 32
CHUNK = 112
epsilon = 1e-05
f32 = jnp.float32
bf16 = jnp.bfloat16
NN = ((1,), (0,))
NT = ((1,), (1,))
AXES = ("ta", "ha", "wa")


def dot(a, b, dims):
    return lax.dot_general(a, b, (dims, ((), ())), preferred_element_type=f32)


def call(kernel, outs, scratch, *args):
    return pl.pallas_call(
        kernel,
        out_shape=outs,
        in_specs=[pl.BlockSpec(memory_space=pltpu.VMEM)] * len(args),
        out_specs=[pl.BlockSpec(memory_space=pltpu.VMEM)] * len(outs),
        scratch_shapes=scratch,
        compiler_params=pltpu.CompilerParams(vmem_limit_bytes=48 * 1024 * 1024),
    )(*args)


def out(shape, dtype):
    return jax.ShapeDtypeStruct(shape, dtype)


def row_steps():
    return range(0, ROWS, STEP)


def standardized(x):
    average = jnp.sum(x, axis=-1, keepdims=True) * (1.0 / D)
    centred = x - average
    spread = jnp.sum(centred * centred, axis=-1, keepdims=True) * (1.0 / D)
    scale = lax.rsqrt(spread + epsilon)
    return centred * scale, scale


def norm_pull(x, grad):
    unit, scale = standardized(x)
    mean_grad = jnp.sum(grad, axis=-1, keepdims=True) * (1.0 / D)
    mean_both = jnp.sum(grad * unit, axis=-1, keepdims=True) * (1.0 / D)
    return scale * (grad - mean_grad - unit * mean_both)


def norm_into(src, dst):
    for i in row_steps():
        rows = pl.ds(i, STEP)
        dst[rows, :] = standardized(src[rows, :].astype(f32))[0].astype(bf16)


def split3(x):
    hi = x.astype(bf16)
    rest = x - hi.astype(f32)
    mid = rest.astype(bf16)
    return hi, mid, (rest - mid.astype(f32)).astype(bf16)


def spread_onehot():
    col = lax.broadcasted_iota(jnp.int32, (1, UPAD), 1)
    group = lax.shift_right_logical(col, 3)
    w = jnp.bitwise_and(col, 7)
    valid = (w < WW) & (group < 91)
    target = jnp.where(valid, group * 13 + w + 6, -1)
    row = lax.broadcasted_iota(jnp.int32, (TPAD, UPAD), 0)
    return jnp.where(row == target, 1.0, 0.0).astype(bf16)


def build_bias(table_ref, bias_ref):
    sheared = []
    for h in range(HEADS):
        line = jnp.broadcast_to(table_ref[h : h + 1, :], (8, TPAD))
        sheared.append(pltpu.roll(line, 0, 1, stride=1, stride_axis=0))
    sheared = jnp.concatenate(sheared, axis=0)
    onehot = spread_onehot()
    hi, mid, lo = split3(sheared)
    u = dot(hi, onehot, NN) + dot(mid, onehot, NN) + dot(lo, onehot, NN)
    sub = lax.broadcasted_iota(jnp.int32, u.shape, 0)
    u = jnp.where(jnp.bitwise_and(sub, 7) == 7, -1e30, u)
    for hj in range(WH):
        base = (6 - hj) * 8
        y = jnp.concatenate([u[:, dt * 104 + base : dt * 104 + base + 56] for dt in range(7)], axis=1)
        for tj in range(WT):
            z = y[:, (3 - tj) * 56 : (3 - tj) * 56 + ROWS]
            bias_ref[:, tj * 56 + hj * 8 : tj * 56 + hj * 8 + 8, :] = z.reshape(HEADS, 8, ROWS)


def bias_kernel(table_ref, bias_ref):
    build_bias(table_ref, bias_ref)


def table_pull(ds_ref):
    du = jnp.zeros((HEADS * 8, UPAD), f32)
    for hj in range(WH):
        dy = jnp.zeros((HEADS * 8, 392), f32)
        for tj in range(WT):
            z = ds_ref[:, tj * 56 + hj * 8 : tj * 56 + hj * 8 + 8, :].reshape(HEADS * 8, ROWS)
            parts = []
            if tj < 3:
                parts.append(jnp.zeros((HEADS * 8, (3 - tj) * 56), f32))
            parts.append(z)
            if tj > 0:
                parts.append(jnp.zeros((HEADS * 8, tj * 56), f32))
            dy = dy + (jnp.concatenate(parts, axis=1) if len(parts) > 1 else parts[0])
        parts = []
        at = 0
        for dt in range(7):
            start = dt * 104 + (6 - hj) * 8
            if start > at:
                parts.append(jnp.zeros((HEADS * 8, start - at), f32))
            parts.append(dy[:, dt * 56 : dt * 56 + 56])
            at = start + 56
        parts.append(jnp.zeros((HEADS * 8, UPAD - at), f32))
        du = du + jnp.concatenate(parts, axis=1)
    onehot = spread_onehot()
    hi = du.astype(bf16)
    lo = (du - hi.astype(f32)).astype(bf16)
    return dot(hi, onehot, NT) + dot(lo, onehot, NT)


def unsheared(sheared):
    sub = jnp.bitwise_and(lax.broadcasted_iota(jnp.int32, sheared.shape, 0), 7)
    total = jnp.zeros_like(sheared)
    for wj in range(WW):
        moved = pltpu.roll(sheared, TPAD - wj, 1) if wj else sheared
        total = jnp.where(sub == wj, moved, total)
    return [jnp.sum(total[8 * h : 8 * h + 8], axis=0, keepdims=True) for h in range(HEADS)]


def head_mask(hh):
    lane = lax.broadcasted_iota(jnp.int32, (1, 128), 1)
    return (lane >= hh * HD) & (lane < hh * HD + HD)


def masked(value, hh):
    return jnp.where(head_mask(hh), value, jnp.zeros_like(value))


def attention_forward(n_ref, wqkv_ref, bias_ref, qkv_ref, p_ref, ctxt_ref, ctx_ref):
    for c in range(3):
        cols = slice(c * D, c * D + D)
        qkv_ref[:, cols] = dot(n_ref[...], wqkv_ref[:, cols], NN).astype(bf16)
    for g in range(3):
        lanes = slice(g * 128, g * 128 + 128)
        q = qkv_ref[:, g * 128 : g * 128 + 128]
        k = qkv_ref[:, D + g * 128 : D + g * 128 + 128]
        v = qkv_ref[:, 2 * D + g * 128 : 2 * D + g * 128 + 128]
        vt = v.astype(f32).T.astype(bf16)
        for hh in range(4):
            h = 4 * g + hh
            s = dot(k, masked(q, hh), NT) * (HD**-0.5) + bias_ref[h]
            top = jnp.max(s, axis=0, keepdims=True)
            e = jnp.exp(s - top)
            p = (e * (1.0 / jnp.sum(e, axis=0, keepdims=True))).astype(bf16)
            p_ref[h] = p
            ctxt_ref[h * HD : h * HD + HD, :] = dot(vt[hh * HD : hh * HD + HD], p, NN)
        ctx_ref[:, lanes] = ctxt_ref[g * 128 : g * 128 + 128, :].T.astype(bf16)


def attention_backward(dctx, qkv_ref, p_ref, ds_ref, dqt_ref, dqkv_ref):
    for g in range(3):
        q = qkv_ref[:, g * 128 : g * 128 + 128]
        k = qkv_ref[:, D + g * 128 : D + g * 128 + 128]
        v = qkv_ref[:, 2 * D + g * 128 : 2 * D + g * 128 + 128]
        dc = dctx[:, g * 128 : g * 128 + 128]
        kt = k.astype(f32).T.astype(bf16)
        dk = jnp.zeros((ROWS, 128), f32)
        dv = jnp.zeros((ROWS, 128), f32)
        for hh in range(4):
            h = 4 * g + hh
            dch = masked(dc, hh)
            p = p_ref[h]
            p32 = p.astype(f32)
            dp = dot(v, dch, NT)
            delta = jnp.sum(p32 * dp, axis=0, keepdims=True)
            ds = p32 * (dp - delta)
            ds_ref[h] = ds.astype(ds_ref.dtype)
            dsb = ds.astype(bf16)
            dv = dv + dot(p, dch, NN)
            dk = dk + dot(dsb, masked(q, hh), NN)
            dqt_ref[h * HD : h * HD + HD, :] = dot(kt[hh * HD : hh * HD + HD], dsb, NN)
        dq = dqt_ref[g * 128 : g * 128 + 128, :].T
        dqkv_ref[:, g * 128 : g * 128 + 128] = (dq * (HD**-0.5)).astype(bf16)
        dqkv_ref[:, D + g * 128 : D + g * 128 + 128] = (dk * (HD**-0.5)).astype(bf16)
        dqkv_ref[:, 2 * D + g * 128 : 2 * D + g * 128 + 128] = dv.astype(bf16)


def expand_gelu(n2_ref, we_ref, e_ref, act_ref, slope_ref):
    for c in range(4):
        cols = slice(c * D, c * D + D)
        e_ref[...] = dot(n2_ref[...], we_ref[:, cols], NN)
        for i in row_steps():
            rows = slice(i, i + STEP)
            x = e_ref[rows, :]
            cdf = 0.5 + 0.5 * lax.erf(x * 0.7071067811865476)
            act_ref[rows, cols] = (x * cdf).astype(bf16)
            slope = cdf + x * (jnp.exp(x * x * -0.5) * 0.3989422804014327)
            slope_ref[rows, cols] = slope.astype(slope_ref.dtype)


def first_forward(
    x_ref, table_ref, wqkv_ref, wp_ref, we_ref, wc_ref,
    n1_ref, qkv_ref, p_ref, ctx_ref, h1_ref, n2_ref, act_ref, slope_ref, y_ref,
    bias_ref, ctxt_ref, big_ref,
):
    build_bias(table_ref, bias_ref)
    norm_into(x_ref, n1_ref)
    attention_forward(n1_ref, wqkv_ref, bias_ref, qkv_ref, p_ref, ctxt_ref, ctx_ref)
    big_ref[...] = dot(ctx_ref[...], wp_ref[...], NN)
    for i in row_steps():
        rows = slice(i, i + STEP)
        a = big_ref[rows, :].astype(bf16).astype(f32)
        h = (x_ref[rows, :].astype(f32) + a).astype(bf16)
        h1_ref[rows, :] = h
        n2_ref[rows, :] = standardized(h.astype(f32))[0].astype(bf16)
    expand_gelu(n2_ref, we_ref, big_ref, act_ref, slope_ref)
    big_ref[...] = dot(act_ref[...], wc_ref[...], NN)
    for i in row_steps():
        rows = slice(i, i + STEP)
        y_ref[rows, :] = (h1_ref[rows, :].astype(f32) + big_ref[rows, :]).astype(bf16)


def feed_backward(gy_ref, act_unused, slope_ref, h_ref, we_ref, wc_ref, de_ref, big_ref, dh_ref):
    for c in range(4):
        cols = slice(c * D, c * D + D)
        big_ref[...] = dot(gy_ref[...], wc_ref[cols, :], NT)
        for i in row_steps():
            rows = slice(i, i + STEP)
            da = big_ref[rows, :].astype(bf16).astype(f32)
            de_ref[rows, cols] = (da * slope_ref[rows, cols].astype(f32)).astype(bf16)
    big_ref[...] = dot(de_ref[...], we_ref[...], NT)
    for i in row_steps():
        rows = slice(i, i + STEP)
        g = big_ref[rows, :].astype(bf16).astype(f32)
        back = norm_pull(h_ref[rows, :].astype(f32), g).astype(bf16)
        dh_ref[rows, :] = (gy_ref[rows, :].astype(f32) + back.astype(f32)).astype(bf16)


def second_whole(
    y_ref, up_ref, bias_ref, wqkv_ref, wp_ref, we_ref, wc_ref,
    n1_ref, ctx_ref, n2_ref, act_ref, dqkv_ref, dh_ref, de_ref, ds_ref, gy_ref,
    qkv_ref, p_ref, ctxt_ref, h2_ref, slope_ref, dctx_ref, big_ref,
):
    norm_into(y_ref, n1_ref)
    attention_forward(n1_ref, wqkv_ref, bias_ref, qkv_ref, p_ref, ctxt_ref, ctx_ref)
    big_ref[...] = dot(ctx_ref[...], wp_ref[...], NN)
    for i in row_steps():
        rows = slice(i, i + STEP)
        a = big_ref[rows, :].astype(bf16).astype(f32)
        h = (y_ref[rows, :].astype(f32) + a).astype(bf16)
        h2_ref[rows, :] = h
        n2_ref[rows, :] = standardized(h.astype(f32))[0].astype(bf16)
    expand_gelu(n2_ref, we_ref, big_ref, act_ref, slope_ref)
    feed_backward(up_ref, act_ref, slope_ref, h2_ref, we_ref, wc_ref, de_ref, big_ref, dh_ref)
    dctx_ref[...] = dot(dh_ref[...], wp_ref[...], NT).astype(bf16)
    attention_backward(dctx_ref, qkv_ref, p_ref, ds_ref, ctxt_ref, dqkv_ref)
    attention_input_pull(y_ref, dqkv_ref, wqkv_ref, big_ref, dh_ref, gy_ref)


def attention_input_pull(x_ref, dqkv_ref, wqkv_ref, big_ref, dh_ref, dx_ref):
    big_ref[...] = dot(dqkv_ref[...], wqkv_ref[...], NT)
    for i in row_steps():
        rows = slice(i, i + STEP)
        g = big_ref[rows, :].astype(bf16).astype(f32)
        back = norm_pull(x_ref[rows, :].astype(f32), g).astype(bf16)
        dx_ref[rows, :] = (dh_ref[rows, :].astype(f32) + back.astype(f32)).astype(bf16)


def first_backward(
    gy_ref, x_ref, qkv_ref, p_ref, h1_ref, slope_ref, wqkv_ref, wp_ref, we_ref, wc_ref,
    dqkv_ref, dh_ref, de_ref, ds_ref, dx_ref,
    dqt_ref, dctx_ref, big_ref,
):
    feed_backward(gy_ref, None, slope_ref, h1_ref, we_ref, wc_ref, de_ref, big_ref, dh_ref)
    dctx_ref[...] = dot(dh_ref[...], wp_ref[...], NT).astype(bf16)
    attention_backward(dctx_ref, qkv_ref, p_ref, ds_ref, dqt_ref, dqkv_ref)
    attention_input_pull(x_ref, dqkv_ref, wqkv_ref, big_ref, dh_ref, dx_ref)


def picker(columns, per):
    row = lax.broadcasted_iota(jnp.int32, (128, columns), 0)
    col = lax.broadcasted_iota(jnp.int32, (128, columns), 1)
    return [jnp.where(col == row * per + r, 1.0, 0.0).astype(bf16) for r in range(per)]


def weights_kernel(
    n1_ref, ctx_ref, n2_ref, act_ref, dqkv_ref, da_ref, de_ref, gy_ref, ds_ref,
    out_ref, f_ref,
):
    pick3 = picker(D, 3)

    def place(first, x_ref, g_ref, picks):
        width = g_ref.shape[1] // 128
        for r, pick in enumerate(picks):
            xt = dot(pick, x_ref[...], NT).astype(bf16)
            dw = dot(xt, g_ref[...], NN)
            for c in range(width):
                f_ref[pl.ds(first + r * width + c, 128, stride=CHUNK), :] = dw[:, c * 128 : c * 128 + 128]

    place(0, n1_ref, dqkv_ref, pick3)
    place(27, ctx_ref, da_ref, pick3)
    place(36, n2_ref, de_ref, pick3)
    place(72, act_ref, gy_ref, picker(FF, 12))
    lines = unsheared(table_pull(ds_ref))
    zero = jnp.zeros((128, 128), f32)
    for j in range(108, CHUNK):
        f_ref[pl.ds(j, 128, stride=CHUNK), :] = zero
    for h in range(HEADS):
        for c in range(10):
            at = (h * 10 + c) * CHUNK + 108
            f_ref[at : at + 1, :] = lines[h][:, c * 128 : c * 128 + 128]

    def step(i, carry):
        rows = pl.ds(pl.multiple_of(i * 256, 256), 256)
        out_ref[rows, :] = f_ref[rows, :].astype(bf16)
        return carry

    lax.fori_loop(0, 128 * CHUNK // 256, step, 0)


def run_bias(table):
    return call(bias_kernel, [out((HEADS, ROWS, ROWS), f32)], [], table)[0]


def rows(width, dtype=bf16):
    return out((ROWS, width), dtype)


def scr(shape, dtype):
    return pltpu.VMEM(shape, dtype)


def run_first_forward(x, table, wqkv, wp, we, wc):
    return call(
        first_forward,
        [rows(D), rows(3 * D), out((HEADS, ROWS, ROWS), bf16), rows(D), rows(D), rows(D), rows(FF), rows(FF), rows(D)],
        [scr((HEADS, ROWS, ROWS), f32), scr((D, ROWS), f32), scr((ROWS, D), f32)],
        x, table, wqkv, wp, we, wc,
    )


def run_second(y, up, bias, wqkv, wp, we, wc):
    return call(
        second_whole,
        [rows(D), rows(D), rows(D), rows(FF), rows(3 * D), rows(D), rows(FF), out((HEADS, ROWS, ROWS), f32), rows(D)],
        [
            scr((ROWS, 3 * D), bf16), scr((HEADS, ROWS, ROWS), bf16), scr((D, ROWS), f32), scr((ROWS, D), bf16),
            scr((ROWS, FF), bf16), scr((ROWS, D), bf16), scr((ROWS, D), f32),
        ],
        y, up, bias, wqkv, wp, we, wc,
    )


def run_first_backward(gy, x, qkv, p, h1, slope, wqkv, wp, we, wc):
    return call(
        first_backward,
        [rows(3 * D), rows(D), rows(FF), out((HEADS, ROWS, ROWS), f32), rows(D)],
        [scr((D, ROWS), f32), scr((ROWS, D), bf16), scr((ROWS, D), f32)],
        gy, x, qkv, p, h1, slope, wqkv, wp, we, wc,
    )


def run_weights(n1, ctx, n2, act, dqkv, da, de, gy, ds):
    return call(
        weights_kernel, [out((128 * CHUNK, 128), bf16)], [scr((128 * CHUNK, 128), f32)],
        n1, ctx, n2, act, dqkv, da, de, gy, ds,
    )[0]


def passed_along(block, axis, distance):
    devices = range(lax.axis_size(axis))
    route = [((i - distance) % len(devices), i) for i in devices]
    return lax.ppermute(block, axis, route)


def edge_of(grid, dim, width, direction):
    extent = grid.shape[dim]
    if direction < 0:
        return lax.slice_in_dim(grid, 0, width, axis=dim)
    return lax.slice_in_dim(grid, extent - width, extent, axis=dim)


def rejoin(grid, dim, width, direction, arrived):
    extent = grid.shape[dim]
    if direction < 0:
        return jnp.concatenate([lax.slice_in_dim(grid, width, extent, axis=dim), arrived], axis=dim)
    return jnp.concatenate([arrived, lax.slice_in_dim(grid, 0, extent - width, axis=dim)], axis=dim)


def roll_grid(grid, direction):
    for dim, (axis, width) in enumerate(zip(AXES, (WT // 2, WH // 2, WW // 2))):
        moved = passed_along(edge_of(grid, dim, width, direction), axis, direction)
        grid = rejoin(grid, dim, width, direction, moved)
    return grid


def to_rows(grid):
    return jnp.pad(grid, ((0, 0), (0, 0), (0, 1), (0, 0))).reshape(ROWS, D)


def to_grid(flat):
    return flat.reshape(WT, WH, PITCH, D)[:, :, :WW]


def scattered(buffer):
    spread = lax.all_to_all(buffer.reshape(128, CHUNK, 128), AXES, 0, 0, tiled=True)
    return jnp.sum(spread.astype(f32), axis=0)


def weight_parts(chunk):
    return (
        chunk[0:27].reshape(3, 3 * D),
        chunk[27:36].reshape(3, D),
        chunk[36:72].reshape(3, FF),
        chunk[72:108].reshape(12, D),
    )


def body(
    tokens, upstream, qkv_one, proj_one, table_one, expand_one, contract_one,
    qkv_two, proj_two, table_two, expand_two, contract_two,
):
    def padded(table):
        return jnp.pad(table, ((0, 16 - HEADS), (0, TPAD - TABLE)))

    x = to_rows(tokens)
    n1, qkv, p, ctx, h1, n2, act, slope, y = run_first_forward(
        x, padded(table_one), qkv_one, proj_one, expand_one, contract_one
    )
    bias = run_bias(padded(table_two))
    up = to_rows(roll_grid(upstream, -1))
    rolled = to_rows(roll_grid(to_grid(y), -1))
    n1b, ctxb, n2b, actb, dqkvb, dhb, deb, dsb, gyb = run_second(
        rolled, up, bias, qkv_two, proj_two, expand_two, contract_two
    )
    gy = to_rows(roll_grid(to_grid(gyb), 1))
    second = scattered(run_weights(n1b, ctxb, n2b, actb, dqkvb, dhb, deb, up, dsb))
    dqkv, dh, de, ds, dx = run_first_backward(
        gy, x, qkv, p, h1, slope, qkv_one, proj_one, expand_one, contract_one
    )
    first = scattered(run_weights(n1, ctx, n2, act, dqkv, dh, de, gy, ds))
    lines = jnp.concatenate([first[108:109], second[108:109]], axis=0)
    tables = lax.all_to_all(jnp.broadcast_to(lines[None], (128, 2, 128)), AXES, 0, 0, tiled=True)

    def table_of(which):
        return tables[:120, which].reshape(HEADS, TPAD)[:, :TABLE]

    g1, g2 = weight_parts(first), weight_parts(second)
    return (
        to_grid(dx), g1[0], g1[1], table_of(0), g1[2], g1[3],
        g2[0], g2[1], table_of(1), g2[2], g2[3],
    )


def solution(mesh):
    grid = P("ta", "ha", "wa", None)
    rows_split = P(AXES, None)
    return jax.shard_map(
        body,
        mesh=mesh,
        in_specs=(grid, grid) + (P(),) * 10,
        out_specs=(
            grid, rows_split, rows_split, P(), rows_split, rows_split,
            rows_split, rows_split, P(), rows_split, rows_split,
        ),
        check_vma=False,
    )
```

time: 1430 us -> 246 us (0.17)
  blocking collectives: 354 us -> 0 us
  local copies, waits for them, and re-layouts: 367 us -> 24.8 us
  matrix products: 333 us -> 0 us
  starting transfers between devices: 204 us -> 41.1 us
  Pallas kernels: 0 us -> 71.7 us
  waiting for transfers between devices: 128 us -> 99.1 us
  between operations: 16.9 us -> 1.23 us
    unnamed x1 -> x0, blocking collectives: 354 us -> none
    dot_general x45 -> x0, matrix products: 324 us -> none  [the longest x4 164 us: position_table(): jnp.einsum('htiajb,tkl->hkialjb', along_h, offset_onehot(WT), precision=l...]
    reshape x19 -> x8, local copies, waits for them, and re-layouts: 246 us -> 4.9 us  [the longest x2 1.24 us: weight_parts(): chunk[36:72].reshape(3, FF)]
    unnamed x65 -> x0, starting transfers between devices: 177 us -> none
    psum x1 -> x0, waiting for transfers between devices: 109 us -> none  [body(): lax.psum((table_part_one, table_part_two), ('ta', 'ha', 'wa'))]
    pallas_call x0 -> x6, Pallas kernels: none -> 71.7 us  [call(): pl.pallas_call(kernel, out_shape=outs, in_specs=[pl.BlockSpec(memory_spac...]
    transpose x2 -> x0, local copies, waits for them, and re-layouts: 70.1 us -> none  [position_table(): jnp.einsum('htrab,rij->htiajb', along_w, offset_onehot(WH), precision=lax...]
    all_to_all x0 -> x3, waiting for transfers between devices: none -> 48.7 us  [the longest x2 40.9 us: scattered(): lax.all_to_all(buffer.reshape(128, CHUNK, 128), AXES, 0, 0, tiled=True)]
  transfers between devices with their start and end apart: 78 -> 12, of which waited for: 11 -> 7; matrix products, arithmetic and copies ran while one was open for 34% -> 4% of each run, Pallas kernels for 0% -> 10%
where the time goes in v1:
time: 246 us; the launch traced here: 244 us
  waiting for transfers between devices  99.1 us (40%)
  Pallas kernels  71.7 us (29%)
  starting transfers between devices  41.1 us (17%)
  local copies, waits for them, and re-layouts  24.8 us (10%)
  other arithmetic  6.07 us (2%)
    pallas_call x6, Pallas kernels, call(): pl.pallas_call(kernel, out_shape=outs, in_specs=[pl.BlockSpec(memory_spac...  71.7 us
    ppermute x9, waiting for transfers between devices, passed_along(): return lax.ppermute(block, axis, route)  50.4 us
    all_to_all x2, waiting for transfers between devices, scattered(): lax.all_to_all(buffer.reshape(128, CHUNK, 128), AXES, 0, 0, tiled=True)  40.9 us
    ppermute x9, starting transfers between devices, passed_along(): return lax.ppermute(block, axis, route)  19.5 us
    all_to_all x2, starting transfers between devices, scattered(): lax.all_to_all(buffer.reshape(128, CHUNK, 128), AXES, 0, 0, tiled=True)  16.5 us
    unnamed x57, local copies, waits for them, and re-layouts  15.5 us
    all_to_all x1, waiting for transfers between devices, body(): lax.all_to_all(jnp.broadcast_to(lines[None], (128, 2, 128)), AXES, 0, 0,...  7.75 us
    reduce_sum x2, other arithmetic, scattered(): return jnp.sum(spread.astype(f32), axis=0)  5.2 us
  transfers between devices with their start and end apart: 12, of which 7 were waited for; matrix products, arithmetic and copies ran while one was open for 4% of the time, Pallas kernels for 10%

profile of v1, /device:TPU:1, one launch (start us, length us, event | category | flops | bytes accessed | tf_op | source)
XLA Modules:
  0.0 244.0 jit_solution(7416567054689780265)
XLA Ops:
  6.0 7.9 %shard_map.203 = (bf16[224,384]{1,0:T(8,128)(2,1)S(1)}, bf16[224,1152]{1,0:T(8,128)(2,1)S(1)}, bf16[12,224,224]{2,1,0:T(8,128)(2,1)}, bf16[224,384]{1,0:T(8,128)...) custom-call(bf16[224,384]{1,0:T(8,128)(2,1)S(1)} %bitcast.12, ...), custom_call_target="tpu_custom_call" | custom-call | tf_op jit(solution)/shard_map/pallas_call | solution.py:35
  16.8 3.7 %collective-permute-start = (bf16[2,7,7,384]{3,2,1,0:T(8,128)(2,1)S(1)}, bf16[2,7,7,384]{3,2,1,0:T(8,128)(2,1)S(1)}, u32[]{:S(2)}, u32[]{:S(2)}) collective-permute-start(bf16[2,7,7,384]{3,2,1,0:T(8,128)(2,1)S(1)} %get-tuple-element.62), channel_id=1, source_target_pairs={{64,0},{0,64},{65,1},{1,65},{66,2},{2,66},{67,3},{3,67},{68,4},{4,... | collective-permute-start | bytes 225800 | tf_op jit(solution)/shard_map/ppermute | solution.py:395
  20.7 2.8 %shard_map.204.bias_ref = f32[12,224,224]{2,1,0:T(8,128)S(1)} custom-call(f32[16,1280]{1,0:T(8,128)S(1)} %pad.24.table_ref), custom_call_target="tpu_custom_call" | custom-call | tf_op jit(solution)/shard_map/pallas_call | solution.py:35
  25.1 3.9 %collective-permute-start.1 = (bf16[4,3,7,384]{3,2,1,0:T(8,128)(2,1)S(1)}, bf16[4,3,7,384]{3,2,1,0:T(8,128)(2,1)S(1)}, u32[]{:S(2)}, u32[]{:S(2)}) collective-permute-start(bf16[4,3,7,384]{3,2,1,0:T(8,128)(2,1)S(1)} %pad_maximum_fusion.4), channel_id=1, source_target_pairs={{8,0},{16,8},{24,16},{32,24},{40,32},{48,40},{56,48},{0,56},{9,1},... | collective-permute-start | bytes 193544 | tf_op jit(solution)/shard_map/ppermute | solution.py:395
  30.5 2.1 collective-permute-start.2
  32.7 2.6 %collective-permute-start.5 = (bf16[4,7,3,384]{3,0,2,1:T(4,128)(2,1)S(1)}, bf16[4,7,3,384]{3,0,2,1:T(4,128)(2,1)S(1)}, u32[]{:S(2)}, u32[]{:S(2)}) collective-permute-start(bf16[4,7,3,384]{3,0,2,1:T(4,128)(2,1)S(1)} %pad_maximum_fusion.5), channel_id=1, source_target_pairs={{1,0},{2,1},{3,2},{4,3},{5,4},{6,5},{7,6},{0,7},{9,8},{10,9},{11,1... | collective-permute-start | bytes 193544 | tf_op jit(solution)/shard_map/ppermute | solution.py:395
  35.5 3.3 %collective-permute-done.5 = bf16[4,7,3,384]{3,0,2,1:T(4,128)(2,1)S(1)} collective-permute-done((bf16[4,7,3,384]{3,0,2,1:T(4,128)(2,1)S(1)}, bf16[4,7,3,384]{3,0,2,1:T(4,128)(2,1)S(1)}, u32[]{:S(2)}, u32[]{:S(2)}) %collective-permute-start.5) | collective-permute-done | bytes 64544 | tf_op jit(solution)/shard_map/ppermute | solution.py:395
  39.1 12.1 %shard_map.205 = (bf16[224,384]{1,0:T(8,128)(2,1)S(1)}, bf16[224,384]{1,0:T(8,128)(2,1)S(1)}, bf16[224,384]{1,0:T(8,128)(2,1)S(1)}, bf16[224,1536]{1,0:T(8,128)(...) custom-call(bf16[224,384]{1,0:T(8,128)(2,1)S(1)} %bitcast.18, ...), custom_call_target="tpu_custom_call" | custom-call | tf_op jit(solution)/shard_map/pallas_call | solution.py:35
  51.9 1.8 copy-done.6
  53.6 26.5 %shard_map.208 = bf16[14336,128]{1,0:T(8,128)(2,1)} custom-call(bf16[224,384]{1,0:T(8,128)(2,1)S(1)} %get-tuple-element.49.n1_ref, bf16[224,384]{1,0:T(8,128)(2,1)S(1)} %get-tuple-element.50.ctx_ref, bf16[224,384]{1,0:T(8,128)(2,1)S(1)} %get-tuple-element.51.n2_ref, bf16[224,1536]{1,0:T(8,128)(2,1)S(1)} %get-tuple-element.52.act_ref, ...), custom_call_target="tpu_custom_call" | custom-call | tf_op jit(solution)/shard_map/pallas_call | solution.py:35
  80.2 9.4 %all-to-all-start.1 = ((bf16[128,112,128]{2,1,0:T(8,128)(2,1)}), bf16[128,112,128]{2,1,0:T(8,128)(2,1)}, u32[]{:S(2)}, u32[]{:S(2)}) async-start(bf16[128,112,128]{2,1,0:T(8,128)(2,1)} %bitcast.22), calls=%async_computation.1 | async-start | bytes 7340032 | tf_op jit(solution)/shard_map/all_to_all | solution.py:428
  90.5 3.0 %collective-permute-start.6 = (bf16[2,7,7,384]{3,2,1,0:T(8,128)(2,1)S(1)}, bf16[2,7,7,384]{3,2,1,0:T(8,128)(2,1)S(1)}, u32[]{:S(2)}, u32[]{:S(2)}) collective-permute-start(bf16[2,7,7,384]{3,2,1,0:T(8,128)(2,1)S(1)} %get-tuple-element.59), channel_id=1, source_target_pairs={{64,0},{0,64},{65,1},{1,65},{66,2},{2,66},{67,3},{3,67},{68,4},{4,... | collective-permute-start | bytes 225800 | tf_op jit(solution)/shard_map/ppermute | solution.py:395
  93.5 39.9 %collective-permute-done.6 = bf16[2,7,7,384]{3,2,1,0:T(8,128)(2,1)S(1)} collective-permute-done((bf16[2,7,7,384]{3,2,1,0:T(8,128)(2,1)S(1)}, bf16[2,7,7,384]{3,2,1,0:T(8,128)(2,1)S(1)}, u32[]{:S(2)}, u32[]{:S(2)}) %collective-permute-start.6) | collective-permute-done | bytes 75296 | tf_op jit(solution)/shard_map/ppermute | solution.py:395
  133.8 5.0 %collective-permute-done.7 = bf16[4,3,7,384]{3,2,1,0:T(8,128)(2,1)S(1)} collective-permute-done((bf16[4,3,7,384]{3,2,1,0:T(8,128)(2,1)S(1)}, bf16[4,3,7,384]{3,2,1,0:T(8,128)(2,1)S(1)}, u32[]{:S(2)}, u32[]{:S(2)}) %collective-permute-start.7) | collective-permute-done | bytes 64544 | tf_op jit(solution)/shard_map/ppermute | solution.py:395
  139.0 3.2 %collective-permute-start.8 = (bf16[4,7,3,384]{3,2,1,0:T(4,128)(2,1)S(1)}, bf16[4,7,3,384]{3,2,1,0:T(4,128)(2,1)S(1)}, u32[]{:S(2)}, u32[]{:S(2)}) collective-permute-start(bf16[4,7,3,384]{3,2,1,0:T(4,128)(2,1)S(1)} %slice.150), channel_id=1, source_target_pairs={{7,0},{0,1},{1,2},{2,3},{3,4},{4,5},{5,6},{6,7},{15,8},{8,9},{9,10... | collective-permute-start | bytes 193544 | tf_op jit(solution)/shard_map/ppermute | solution.py:395
  144.9 7.8 %shard_map.206 = (bf16[224,1152]{1,0:T(8,128)(2,1)S(1)}, bf16[224,384]{1,0:T(8,128)(2,1)S(1)}, bf16[224,1536]{1,0:T(8,128)(2,1)S(1)}, f32[12,224,224]{2,1,0:T(8,128)}, bf16[224,384]{1,0:T(8,128)(2,1)S(1)}) custom-call(bf16[224,384]{1,0:T(8,128)(2,1)S(1)} %bitcast.16, bf16[224,384]{1,0:T(8,128)(2,1)S(1)} %bitcast.13, bf16[224,1152]{1,0:T(8,128)(2,1)S(1)} %copy-done.14, ...), custom_call_target="tpu_custom_call" | custom-call | tf_op jit(solution)/shard_map/pallas_call | solution.py:35
  153.4 1.8 copy-done.5
  155.1 14.5 %shard_map.207 = bf16[14336,128]{1,0:T(8,128)(2,1)} custom-call(bf16[224,384]{1,0:T(8,128)(2,1)S(1)} %copy-done.20, bf16[224,384]{1,0:T(8,128)(2,1)S(1)} %copy-done.22, bf16[224,384]{1,0:T(8,128)(2,1)S(1)} %copy-done.24, bf16[224,1536]{1,0:T(8,128)(2,1)S(1)} %copy-done.12, bf16[224,1152]{1,0:T(8,128)(2,1)S(1)} %get-tuple-element.45.dqkv_ref, ...), custom_call_target="tpu_custom_call" | custom-call | tf_op jit(solution)/shard_map/pallas_call | solution.py:35
  169.6 7.1 %all-to-all-start = ((bf16[128,112,128]{2,1,0:T(8,128)(2,1)}), bf16[128,112,128]{2,1,0:T(8,128)(2,1)}, u32[]{:S(2)}, u32[]{:S(2)}) async-start(bf16[128,112,128]{2,1,0:T(8,128)(2,1)} %bitcast.23), calls=%async_computation | async-start | bytes 7340032 | tf_op jit(solution)/shard_map/all_to_all | solution.py:428
  177.5 2.6 %convert_reduce_fusion = f32[112,128]{1,0:T(8,128)S(1)} fusion(bf16[128,112,128]{2,1,0:T(8,128)(2,1)} %all-to-all-done.1), kind=kLoop, calls=%fused_computation | loop fusion | flops 3655680 | bytes 3727360 | tf_op jit(solution)/shard_map/reduce_sum | solution.py:429
  182.6 40.9 %all-to-all-done = bf16[128,112,128]{2,1,0:T(8,128)(2,1)} async-done(((bf16[128,112,128]{2,1,0:T(8,128)(2,1)}), bf16[128,112,128]{2,1,0:T(8,128)(2,1)}, u32[]{:S(2)}, u32[]{:S(2)}) %all-to-all-start) | async-done | bytes 3670048 | tf_op jit(solution)/shard_map/all_to_all | solution.py:428
  223.5 2.6 %convert_reduce_fusion.1 = f32[112,128]{1,0:T(8,128)S(1)} fusion(bf16[128,112,128]{2,1,0:T(8,128)(2,1)} %all-to-all-done), kind=kLoop, calls=%fused_computation.1 | loop fusion | flops 3655680 | bytes 3727360 | tf_op jit(solution)/shard_map/reduce_sum | solution.py:429
  226.8 5.1 %all-to-all-start.2 = ((f32[128,2,128]{2,1,0:T(2,128)}), f32[128,2,128]{2,1,0:T(2,128)S(1)}, u32[]{:S(2)}, u32[]{:S(2)}) async-start(f32[128,2,128]{2,1,0:T(2,128)} %broadcast_in_dim.2), calls=%async_computation.2 | async-start | bytes 262144 | tf_op jit(solution)/shard_map/all_to_all | solution.py:465
  234.4 7.8 %all-to-all-done.2 = f32[128,2,128]{2,1,0:T(2,128)S(1)} async-done(((f32[128,2,128]{2,1,0:T(2,128)}), f32[128,2,128]{2,1,0:T(2,128)S(1)}, u32[]{:S(2)}, u32[]{:S(2)}) %all-to-all-start.2) | async-done | bytes 131104 | tf_op jit(solution)/shard_map/all_to_all | solution.py:465
  (108 shorter events, 25.3 us)
Async XLA Ops:
  0.6 19.8 %copy-start.25 = (bf16[4,7,7,384]{3,0,2,1:T(4,128)(2,1)S(1)}, bf16[4,7,7,384]{3,0,2,1:T(4,128)(2,1)}, u32[]{:S(2)}) copy-start(bf16[4,7,7,384]{3,0,2,1:T(4,128)(2,1)} %param.13) | copy-start | bytes 451588
  0.7 20.0 %copy-start.26 = (f32[12,1183]{1,0:T(8,128)S(1)}, f32[12,1183]{1,0:T(8,128)}, u32[]{:S(2)}) copy-start(f32[12,1183]{1,0:T(8,128)} %param.21) | copy-start | bytes 170356
  16.8 22.2 %copy-start.11 = (bf16[224,1536]{1,0:T(8,128)(2,1)}, bf16[224,1536]{1,0:T(8,128)(2,1)S(1)}, u32[]{:S(2)}) copy-start(bf16[224,1536]{1,0:T(8,128)(2,1)S(1)} %get-tuple-element.44.act_ref) | copy-start | bytes 2064388
  16.8 22.3 %copy-start.7 = (bf16[384,1536]{1,0:T(8,128)(2,1)S(1)}, bf16[384,1536]{1,0:T(8,128)(2,1)}, u32[]{:S(2)}) copy-start(bf16[384,1536]{1,0:T(8,128)(2,1)} %we_ref.4) | copy-start | bytes 3538948
  16.8 22.3 %copy-start.10 = (bf16[384,1152]{1,0:T(8,128)(2,1)S(1)}, bf16[384,1152]{1,0:T(8,128)(2,1)}, u32[]{:S(2)}) copy-start(bf16[384,1152]{1,0:T(8,128)(2,1)} %wqkv_ref.4) | copy-start | bytes 2654212
  16.8 22.3 %copy-start.15 = (bf16[384,384]{1,0:T(8,128)(2,1)S(1)}, bf16[384,384]{1,0:T(8,128)(2,1)}, u32[]{:S(2)}) copy-start(bf16[384,384]{1,0:T(8,128)(2,1)} %wp_ref.4) | copy-start | bytes 884740
  16.8 8.3 %collective-permute-start = (bf16[2,7,7,384]{3,2,1,0:T(8,128)(2,1)S(1)}, bf16[2,7,7,384]{3,2,1,0:T(8,128)(2,1)S(1)}, u32[]{:S(2)}, u32[]{:S(2)}) collective-permute-start(bf16[2,7,7,384]{3,2,1,0:T(8,128)(2,1)S(1)} %get-tuple-element.62), channel_id=1, source_target_pairs={{64,0},{0,64},{65,1},{1,65},{66,2},{2,66},{67,3},{3,67},{68,4},{4,... | collective-permute-start | bytes 225800 | tf_op jit(solution)/shard_map/ppermute | solution.py:395
  20.6 8.5 %collective-permute-start.3 = (bf16[2,7,7,384]{3,0,2,1:T(2,128)(2,1)S(1)}, bf16[2,7,7,384]{3,0,2,1:T(2,128)(2,1)S(1)}, u32[]{:S(2)}, u32[]{:S(2)}) collective-permute-start(bf16[2,7,7,384]{3,0,2,1:T(2,128)(2,1)S(1)} %get-tuple-element.64), channel_id=1, source_target_pairs={{64,0},{0,64},{65,1},{1,65},{66,2},{2,66},{67,3},{3,67},{68,4},{4,... | collective-permute-start | bytes 225800 | tf_op jit(solution)/shard_map/ppermute | solution.py:395
  25.1 5.3 %collective-permute-start.1 = (bf16[4,3,7,384]{3,2,1,0:T(8,128)(2,1)S(1)}, bf16[4,3,7,384]{3,2,1,0:T(8,128)(2,1)S(1)}, u32[]{:S(2)}, u32[]{:S(2)}) collective-permute-start(bf16[4,3,7,384]{3,2,1,0:T(8,128)(2,1)S(1)} %pad_maximum_fusion.4), channel_id=1, source_target_pairs={{8,0},{16,8},{24,16},{32,24},{40,32},{48,40},{56,48},{0,56},{9,1},... | collective-permute-start | bytes 193544 | tf_op jit(solution)/shard_map/ppermute | solution.py:395
  29.1 3.5 %collective-permute-start.4 = (bf16[4,3,7,384]{3,0,2,1:T(4,128)(2,1)S(1)}, bf16[4,3,7,384]{3,0,2,1:T(4,128)(2,1)S(1)}, u32[]{:S(2)}, u32[]{:S(2)}) collective-permute-start(bf16[4,3,7,384]{3,0,2,1:T(4,128)(2,1)S(1)} %pad_maximum_fusion.6), channel_id=1, source_target_pairs={{8,0},{16,8},{24,16},{32,24},{40,32},{48,40},{56,48},{0,56},{9,1},... | collective-permute-start | bytes 193544 | tf_op jit(solution)/shard_map/ppermute | solution.py:395
  30.5 8.4 %collective-permute-start.2 = (bf16[4,7,3,384]{3,2,1,0:T(4,128)(2,1)S(1)}, bf16[4,7,3,384]{3,2,1,0:T(4,128)(2,1)S(1)}, u32[]{:S(2)}, u32[]{:S(2)}) collective-permute-start(bf16[4,7,3,384]{3,2,1,0:T(4,128)(2,1)S(1)} %pad_maximum_fusion.2), channel_id=1, source_target_pairs={{1,0},{2,1},{3,2},{4,3},{5,4},{6,5},{7,6},{0,7},{9,8},{10,9},{11,1... | collective-permute-start | bytes 193544 | tf_op jit(solution)/shard_map/ppermute | solution.py:395
  32.7 6.1 %collective-permute-start.5 = (bf16[4,7,3,384]{3,0,2,1:T(4,128)(2,1)S(1)}, bf16[4,7,3,384]{3,0,2,1:T(4,128)(2,1)S(1)}, u32[]{:S(2)}, u32[]{:S(2)}) collective-permute-start(bf16[4,7,3,384]{3,0,2,1:T(4,128)(2,1)S(1)} %pad_maximum_fusion.5), channel_id=1, source_target_pairs={{1,0},{2,1},{3,2},{4,3},{5,4},{6,5},{7,6},{0,7},{9,8},{10,9},{11,1... | collective-permute-start | bytes 193544 | tf_op jit(solution)/shard_map/ppermute | solution.py:395
  80.2 63.6 %copy-start.2 = (bf16[384,1536]{1,0:T(8,128)(2,1)S(1)}, bf16[384,1536]{1,0:T(8,128)(2,1)}, u32[]{:S(2)}) copy-start(bf16[384,1536]{1,0:T(8,128)(2,1)} %we_ref.5) | copy-start | bytes 3538948
  80.2 63.6 %copy-start.4 = (bf16[384,1152]{1,0:T(8,128)(2,1)S(1)}, bf16[384,1152]{1,0:T(8,128)(2,1)}, u32[]{:S(2)}) copy-start(bf16[384,1152]{1,0:T(8,128)(2,1)} %wqkv_ref.5) | copy-start | bytes 2654212
  80.2 63.6 %copy-start.9 = (bf16[384,384]{1,0:T(8,128)(2,1)S(1)}, bf16[384,384]{1,0:T(8,128)(2,1)}, u32[]{:S(2)}) copy-start(bf16[384,384]{1,0:T(8,128)(2,1)} %wp_ref.5) | copy-start | bytes 884740
  80.2 89.4 %all-to-all-start.1 = ((bf16[128,112,128]{2,1,0:T(8,128)(2,1)}), bf16[128,112,128]{2,1,0:T(8,128)(2,1)}, u32[]{:S(2)}, u32[]{:S(2)}) async-start(bf16[128,112,128]{2,1,0:T(8,128)(2,1)} %bitcast.22), calls=%async_computation.1 | async-start | bytes 7340032 | tf_op jit(solution)/shard_map/all_to_all | solution.py:428
  90.5 42.9 %collective-permute-start.6 = (bf16[2,7,7,384]{3,2,1,0:T(8,128)(2,1)S(1)}, bf16[2,7,7,384]{3,2,1,0:T(8,128)(2,1)S(1)}, u32[]{:S(2)}, u32[]{:S(2)}) collective-permute-start(bf16[2,7,7,384]{3,2,1,0:T(8,128)(2,1)S(1)} %get-tuple-element.59), channel_id=1, source_target_pairs={{64,0},{0,64},{65,1},{1,65},{66,2},{2,66},{67,3},{3,67},{68,4},{4,... | collective-permute-start | bytes 225800 | tf_op jit(solution)/shard_map/ppermute | solution.py:395
  133.5 19.9 %copy-start.24 = (bf16[224,384]{1,0:T(8,128)(2,1)S(1)}, bf16[224,384]{1,0:T(8,128)(2,1)}, u32[]{:S(2)}) copy-start(bf16[224,384]{1,0:T(8,128)(2,1)} %copy-done.23) | copy-start | bytes 516100
  133.5 5.4 %collective-permute-start.7 = (bf16[4,3,7,384]{3,2,1,0:T(8,128)(2,1)S(1)}, bf16[4,3,7,384]{3,2,1,0:T(8,128)(2,1)S(1)}, u32[]{:S(2)}, u32[]{:S(2)}) collective-permute-start(bf16[4,3,7,384]{3,2,1,0:T(8,128)(2,1)S(1)} %pad_maximum_fusion.3), channel_id=1, source_target_pairs={{56,0},{0,8},{8,16},{16,24},{24,32},{32,40},{40,48},{48,56},{57,1}... | collective-permute-start | bytes 193544 | tf_op jit(solution)/shard_map/ppermute | solution.py:395
  138.9 14.5 %copy-start.20 = (bf16[224,384]{1,0:T(8,128)(2,1)S(1)}, bf16[224,384]{1,0:T(8,128)(2,1)}, u32[]{:S(2)}) copy-start(bf16[224,384]{1,0:T(8,128)(2,1)} %copy-done.19) | copy-start | bytes 516100
  138.9 14.5 %copy-start.22 = (bf16[224,384]{1,0:T(8,128)(2,1)S(1)}, bf16[224,384]{1,0:T(8,128)(2,1)}, u32[]{:S(2)}) copy-start(bf16[224,384]{1,0:T(8,128)(2,1)} %copy-done.21) | copy-start | bytes 516100
  139.0 4.7 %collective-permute-start.8 = (bf16[4,7,3,384]{3,2,1,0:T(4,128)(2,1)S(1)}, bf16[4,7,3,384]{3,2,1,0:T(4,128)(2,1)S(1)}, u32[]{:S(2)}, u32[]{:S(2)}) collective-permute-start(bf16[4,7,3,384]{3,2,1,0:T(4,128)(2,1)S(1)} %slice.150), channel_id=1, source_target_pairs={{7,0},{0,1},{1,2},{2,3},{3,4},{4,5},{5,6},{6,7},{15,8},{8,9},{9,10... | collective-permute-start | bytes 193544 | tf_op jit(solution)/shard_map/ppermute | solution.py:395
  169.6 53.9 %all-to-all-start = ((bf16[128,112,128]{2,1,0:T(8,128)(2,1)}), bf16[128,112,128]{2,1,0:T(8,128)(2,1)}, u32[]{:S(2)}, u32[]{:S(2)}) async-start(bf16[128,112,128]{2,1,0:T(8,128)(2,1)} %bitcast.23), calls=%async_computation | async-start | bytes 7340032 | tf_op jit(solution)/shard_map/all_to_all | solution.py:428
  226.8 15.3 %all-to-all-start.2 = ((f32[128,2,128]{2,1,0:T(2,128)}), f32[128,2,128]{2,1,0:T(2,128)S(1)}, u32[]{:S(2)}, u32[]{:S(2)}) async-start(f32[128,2,128]{2,1,0:T(2,128)} %broadcast_in_dim.2), calls=%async_computation.2 | async-start | bytes 262144 | tf_op jit(solution)/shard_map/all_to_all | solution.py:465
  (15 other events, 35.3 us)

commit v2 on v1

--- a/solution.py
+++ b/solution.py
@@ -19,6 +19,7 @@
 UPAD = 768
 STEP = 32
 CHUNK = 112
+VMEM_LIMIT = 32 * 1024 * 1024
 epsilon = 1e-05
 f32 = jnp.float32
 bf16 = jnp.bfloat16
@@ -31,19 +32,65 @@
     return lax.dot_general(a, b, (dims, ((), ())), preferred_element_type=f32)
 
 
-def call(kernel, outs, scratch, *args):
-    return pl.pallas_call(
-        kernel,
-        out_shape=outs,
-        in_specs=[pl.BlockSpec(memory_space=pltpu.VMEM)] * len(args),
-        out_specs=[pl.BlockSpec(memory_space=pltpu.VMEM)] * len(outs),
-        scratch_shapes=scratch,
-        compiler_params=pltpu.CompilerParams(vmem_limit_bytes=48 * 1024 * 1024),
-    )(*args)
-
-
-def out(shape, dtype):
-    return jax.ShapeDtypeStruct(shape, dtype)
+class Held:
+    def __init__(self, refs, incoming, outgoing):
+        self.__dict__.update(refs)
+        self.incoming = dict(incoming)
+        self.outgoing = dict(outgoing)
+
+    def need(self, *names):
+        for name in names:
+            if name in self.incoming:
+                self.incoming.pop(name).wait()
+
+    def ready(self, *names):
+        for name in names:
+            if name in self.outgoing:
+                self.outgoing.pop(name).start()
+
+
+def launch(kernel, ins, outs, scratch=()):
+    places = {"far": pltpu.HBM, "near": pltpu.VMEM, "flag": pltpu.SMEM}
+    far_ins = [n for n, (_, space) in ins.items() if space == "far"]
+    far_outs = [n for n, (_, _, space) in outs.items() if space == "far"]
+    scratch = dict(scratch)
+    buffers = {n: pltpu.VMEM(ins[n][0].shape, ins[n][0].dtype) for n in far_ins}
+    buffers.update({n: pltpu.VMEM(outs[n][0], outs[n][1]) for n in far_outs})
+
+    def wrapped(*refs):
+        named = dict(zip(list(ins) + list(outs), refs))
+        rest = refs[len(named) :]
+        near = dict(zip(list(scratch) + list(buffers), rest))
+        sems = rest[-1]
+        incoming, outgoing = {}, {}
+        for i, n in enumerate(far_ins):
+            incoming[n] = pltpu.make_async_copy(named[n], near[n], sems.at[i])
+            incoming[n].start()
+        for i, n in enumerate(far_outs):
+            outgoing[n] = pltpu.make_async_copy(near[n], named[n], sems.at[len(far_ins) + i])
+        kernel(Held({**named, **near}, incoming, outgoing))
+        for n in far_outs:
+            outgoing[n].wait()
+
+    results = pl.pallas_call(
+        wrapped,
+        out_shape=[
+            pltpu.HBM(shape, dtype) if space == "far" else jax.ShapeDtypeStruct(shape, dtype)
+            for shape, dtype, space in outs.values()
+        ],
+        in_specs=[pl.BlockSpec(memory_space=places[space]) for _, space in ins.values()],
+        out_specs=[pl.BlockSpec(memory_space=places[space]) for _, _, space in outs.values()],
+        scratch_shapes=list(scratch.values())
+        + list(buffers.values())
+        + [pltpu.SemaphoreType.DMA((max(1, len(far_ins) + len(far_outs)),))],
+        compiler_params=pltpu.CompilerParams(vmem_limit_bytes=VMEM_LIMIT),
+    )(
+        *[
+            pltpu.with_memory_space_constraint(array, pltpu.HBM) if space == "far" else array
+            for array, space in ins.values()
+        ]
+    )
+    return dict(zip(outs, results))
 
 
 def row_steps():
@@ -88,10 +135,12 @@
     return jnp.where(row == target, 1.0, 0.0).astype(bf16)
 
 
-def build_bias(table_ref, bias_ref):
+def build_bias(table_ref, bias_ref, wide_ref):
+    wide_ref[...] = jnp.zeros_like(wide_ref)
+    wide_ref[:HEADS, :TABLE] = table_ref[...]
     sheared = []
     for h in range(HEADS):
-        line = jnp.broadcast_to(table_ref[h : h + 1, :], (8, TPAD))
+        line = jnp.broadcast_to(wide_ref[h : h + 1, :], (8, TPAD))
         sheared.append(pltpu.roll(line, 0, 1, stride=1, stride_axis=0))
     sheared = jnp.concatenate(sheared, axis=0)
     onehot = spread_onehot()
@@ -107,16 +156,12 @@
             bias_ref[:, tj * 56 + hj * 8 : tj * 56 + hj * 8 + 8, :] = z.reshape(HEADS, 8, ROWS)
 
 
-def bias_kernel(table_ref, bias_ref):
-    build_bias(table_ref, bias_ref)
-
-
 def table_pull(ds_ref):
     du = jnp.zeros((HEADS * 8, UPAD), f32)
     for hj in range(WH):
         dy = jnp.zeros((HEADS * 8, 392), f32)
         for tj in range(WT):
-            z = ds_ref[:, tj * 56 + hj * 8 : tj * 56 + hj * 8 + 8, :].reshape(HEADS * 8, ROWS)
+            z = ds_ref[:, tj * 56 + hj * 8 : tj * 56 + hj * 8 + 8, :].astype(f32).reshape(HEADS * 8, ROWS)
             parts = []
             if tj < 3:
                 parts.append(jnp.zeros((HEADS * 8, (3 - tj) * 56), f32))
@@ -220,29 +265,33 @@
             slope_ref[rows, cols] = slope.astype(slope_ref.dtype)
 
 
-def first_forward(
-    x_ref, table_ref, wqkv_ref, wp_ref, we_ref, wc_ref,
-    n1_ref, qkv_ref, p_ref, ctx_ref, h1_ref, n2_ref, act_ref, slope_ref, y_ref,
-    bias_ref, ctxt_ref, big_ref,
-):
-    build_bias(table_ref, bias_ref)
-    norm_into(x_ref, n1_ref)
-    attention_forward(n1_ref, wqkv_ref, bias_ref, qkv_ref, p_ref, ctxt_ref, ctx_ref)
-    big_ref[...] = dot(ctx_ref[...], wp_ref[...], NN)
+def attention_and_feed(m, x):
+    m.need("wqkv")
+    build_bias(m.table, m.bias, m.wide)
+    norm_into(x, m.n1)
+    attention_forward(m.n1, m.wqkv, m.bias, m.qkv, m.p, m.turned, m.ctx)
+    m.need("wp", "we", "wc")
+    m.ready("n1", "qkv", "p", "ctx")
+    m.big[...] = dot(m.ctx[...], m.wp[...], NN)
     for i in row_steps():
         rows = slice(i, i + STEP)
-        a = big_ref[rows, :].astype(bf16).astype(f32)
-        h = (x_ref[rows, :].astype(f32) + a).astype(bf16)
-        h1_ref[rows, :] = h
-        n2_ref[rows, :] = standardized(h.astype(f32))[0].astype(bf16)
-    expand_gelu(n2_ref, we_ref, big_ref, act_ref, slope_ref)
-    big_ref[...] = dot(act_ref[...], wc_ref[...], NN)
+        a = m.big[rows, :].astype(bf16).astype(f32)
+        h = (x[rows, :].astype(f32) + a).astype(bf16)
+        m.h[rows, :] = h
+        m.n2[rows, :] = standardized(h.astype(f32))[0].astype(bf16)
+    expand_gelu(m.n2, m.we, m.big, m.act, m.slope)
+    m.ready("h", "n2", "act", "slope")
+
+
+def first_forward(m):
+    attention_and_feed(m, m.x)
+    m.big[...] = dot(m.act[...], m.wc[...], NN)
     for i in row_steps():
         rows = slice(i, i + STEP)
-        y_ref[rows, :] = (h1_ref[rows, :].astype(f32) + big_ref[rows, :]).astype(bf16)
-
-
-def feed_backward(gy_ref, act_unused, slope_ref, h_ref, we_ref, wc_ref, de_ref, big_ref, dh_ref):
+        m.y[rows, :] = (m.h[rows, :].astype(f32) + m.big[rows, :]).astype(bf16)
+
+
+def feed_backward(gy_ref, slope_ref, h_ref, we_ref, wc_ref, de_ref, big_ref, dh_ref):
     for c in range(4):
         cols = slice(c * D, c * D + D)
         big_ref[...] = dot(gy_ref[...], wc_ref[cols, :], NT)
@@ -258,27 +307,6 @@
         dh_ref[rows, :] = (gy_ref[rows, :].astype(f32) + back.astype(f32)).astype(bf16)
 
 
-def second_whole(
-    y_ref, up_ref, bias_ref, wqkv_ref, wp_ref, we_ref, wc_ref,
-    n1_ref, ctx_ref, n2_ref, act_ref, dqkv_ref, dh_ref, de_ref, ds_ref, gy_ref,
-    qkv_ref, p_ref, ctxt_ref, h2_ref, slope_ref, dctx_ref, big_ref,
-):
-    norm_into(y_ref, n1_ref)
-    attention_forward(n1_ref, wqkv_ref, bias_ref, qkv_ref, p_ref, ctxt_ref, ctx_ref)
-    big_ref[...] = dot(ctx_ref[...], wp_ref[...], NN)
-    for i in row_steps():
-        rows = slice(i, i + STEP)
-        a = big_ref[rows, :].astype(bf16).astype(f32)
-        h = (y_ref[rows, :].astype(f32) + a).astype(bf16)
-        h2_ref[rows, :] = h
-        n2_ref[rows, :] = standardized(h.astype(f32))[0].astype(bf16)
-    expand_gelu(n2_ref, we_ref, big_ref, act_ref, slope_ref)
-    feed_backward(up_ref, act_ref, slope_ref, h2_ref, we_ref, wc_ref, de_ref, big_ref, dh_ref)
-    dctx_ref[...] = dot(dh_ref[...], wp_ref[...], NT).astype(bf16)
-    attention_backward(dctx_ref, qkv_ref, p_ref, ds_ref, ctxt_ref, dqkv_ref)
-    attention_input_pull(y_ref, dqkv_ref, wqkv_ref, big_ref, dh_ref, gy_ref)
-
-
 def attention_input_pull(x_ref, dqkv_ref, wqkv_ref, big_ref, dh_ref, dx_ref):
     big_ref[...] = dot(dqkv_ref[...], wqkv_ref[...], NT)
     for i in row_steps():
@@ -288,42 +316,66 @@
         dx_ref[rows, :] = (dh_ref[rows, :].astype(f32) + back.astype(f32)).astype(bf16)
 
 
-def first_backward(
-    gy_ref, x_ref, qkv_ref, p_ref, h1_ref, slope_ref, wqkv_ref, wp_ref, we_ref, wc_ref,
-    dqkv_ref, dh_ref, de_ref, ds_ref, dx_ref,
-    dqt_ref, dctx_ref, big_ref,
-):
-    feed_backward(gy_ref, None, slope_ref, h1_ref, we_ref, wc_ref, de_ref, big_ref, dh_ref)
-    dctx_ref[...] = dot(dh_ref[...], wp_ref[...], NT).astype(bf16)
-    attention_backward(dctx_ref, qkv_ref, p_ref, ds_ref, dqt_ref, dqkv_ref)
-    attention_input_pull(x_ref, dqkv_ref, wqkv_ref, big_ref, dh_ref, dx_ref)
-
-
-def picker(columns, per):
-    row = lax.broadcasted_iota(jnp.int32, (128, columns), 0)
-    col = lax.broadcasted_iota(jnp.int32, (128, columns), 1)
-    return [jnp.where(col == row * per + r, 1.0, 0.0).astype(bf16) for r in range(per)]
-
-
-def weights_kernel(
-    n1_ref, ctx_ref, n2_ref, act_ref, dqkv_ref, da_ref, de_ref, gy_ref, ds_ref,
-    out_ref, f_ref,
-):
-    pick3 = picker(D, 3)
-
-    def place(first, x_ref, g_ref, picks):
+def backward(m, x, gy, dx):
+    m.need("wc", "slope", "we", "h")
+    feed_backward(gy, m.slope, m.h, m.we, m.wc, m.de, m.big, m.dh)
+    m.need("wp", "qkv", "p", "wqkv")
+    m.dctx[...] = dot(m.dh[...], m.wp[...], NT).astype(bf16)
+    attention_backward(m.dctx, m.qkv, m.p, m.ds, m.turned, m.dqkv)
+    attention_input_pull(x, m.dqkv, m.wqkv, m.big, m.dh, dx)
+    m.ready("ds", "dqkv", "de", "dh")
+
+
+def second_whole(m):
+    attention_and_feed(m, m.y)
+    backward(m, m.y, m.up, m.gy)
+
+
+def first_backward(m):
+    backward(m, m.x, m.gy, m.dx)
+    m.need("n1", "ctx", "n2", "act")
+    weight_sums(m)
+
+
+def picker(per):
+    count = D // per
+    row = lax.broadcasted_iota(jnp.int32, (D, 1), 0)
+    r = jnp.zeros((D, 1), jnp.int32)
+    for step in range(1, per):
+        r = r + jnp.where(row >= step * count, 1, 0)
+    target = (row - r * count) * per + r
+    col = lax.broadcasted_iota(jnp.int32, (D, D), 1)
+    return jnp.where(col == target, 1.0, 0.0).astype(bf16)
+
+
+def weights_kernel(m):
+    m.passed[...] = m.carried[...]
+    m.need("n1", "dqkv", "ctx", "dh", "n2", "de", "act", "ds")
+    weight_sums(m)
+
+
+def weight_sums(m):
+    f_ref = m.f
+    pick = picker(3)
+
+    def place(first, x, g_ref, pick, per, owner):
         width = g_ref.shape[1] // 128
-        for r, pick in enumerate(picks):
-            xt = dot(pick, x_ref[...], NT).astype(bf16)
-            dw = dot(xt, g_ref[...], NN)
-            for c in range(width):
-                f_ref[pl.ds(first + r * width + c, 128, stride=CHUNK), :] = dw[:, c * 128 : c * 128 + 128]
-
-    place(0, n1_ref, dqkv_ref, pick3)
-    place(27, ctx_ref, da_ref, pick3)
-    place(36, n2_ref, de_ref, pick3)
-    place(72, act_ref, gy_ref, picker(FF, 12))
-    lines = unsheared(table_pull(ds_ref))
+        count = D // per
+        xt = dot(pick, x, NT).astype(bf16)
+        for c in range(0, width, 3):
+            dw = dot(xt, g_ref[:, c * 128 : c * 128 + 384], NN)
+            for r in range(per):
+                for k in range(3):
+                    at = owner * CHUNK + first + r * width + c + k
+                    f_ref[pl.ds(at, count, stride=CHUNK), :] = dw[r * count : r * count + count, k * 128 : k * 128 + 128]
+
+    place(0, m.n1[...], m.dqkv, pick, 3, 0)
+    place(27, m.ctx[...], m.dh, pick, 3, 0)
+    place(36, m.n2[...], m.de, pick, 3, 0)
+    pick = picker(12)
+    for b in range(4):
+        place(72, m.act[:, b * D : b * D + D], m.gy, pick, 12, b * 32)
+    lines = unsheared(table_pull(m.ds))
     zero = jnp.zeros((128, 128), f32)
     for j in range(108, CHUNK):
         f_ref[pl.ds(j, 128, stride=CHUNK), :] = zero
@@ -331,62 +383,94 @@
         for c in range(10):
             at = (h * 10 + c) * CHUNK + 108
             f_ref[at : at + 1, :] = lines[h][:, c * 128 : c * 128 + 128]
-
-    def step(i, carry):
-        rows = pl.ds(pl.multiple_of(i * 256, 256), 256)
-        out_ref[rows, :] = f_ref[rows, :].astype(bf16)
-        return carry
-
-    lax.fori_loop(0, 128 * CHUNK // 256, step, 0)
-
-
-def run_bias(table):
-    return call(bias_kernel, [out((HEADS, ROWS, ROWS), f32)], [], table)[0]
-
-
-def rows(width, dtype=bf16):
-    return out((ROWS, width), dtype)
+    mine = m.mine[0]
+
+    def half(ref, offset):
+        def step(i, carry):
+            to = pl.ds(pl.multiple_of(i * CHUNK, CHUNK), CHUNK)
+            ref[to, :] = f_ref[pl.ds(pl.multiple_of((2 * i + offset) * CHUNK, CHUNK), CHUNK), :].astype(bf16)
+            return carry
+
+        lax.fori_loop(0, 64, step, 0, unroll=8)
+
+    half(m.give, 1 - mine)
+    m.ready("give")
+    half(m.keep, mine)
+    m.ready("keep")
+
+
+SQUARE = (HEADS, ROWS, ROWS)
 
 
 def scr(shape, dtype):
     return pltpu.VMEM(shape, dtype)
 
 
-def run_first_forward(x, table, wqkv, wp, we, wc):
-    return call(
+def rows(width, space):
+    return (ROWS, width), bf16, space
+
+
+def run_first_forward(x, table, weights):
+    return launch(
         first_forward,
-        [rows(D), rows(3 * D), out((HEADS, ROWS, ROWS), bf16), rows(D), rows(D), rows(D), rows(FF), rows(FF), rows(D)],
-        [scr((HEADS, ROWS, ROWS), f32), scr((D, ROWS), f32), scr((ROWS, D), f32)],
-        x, table, wqkv, wp, we, wc,
-    )
-
-
-def run_second(y, up, bias, wqkv, wp, we, wc):
-    return call(
+        {"x": (x, "near"), "table": (table, "near")} | weights,
+        {
+            "n1": rows(D, "far"), "qkv": rows(3 * D, "far"), "p": (SQUARE, bf16, "far"), "ctx": rows(D, "far"),
+            "h": rows(D, "far"), "n2": rows(D, "far"), "act": rows(FF, "far"), "slope": rows(FF, "far"),
+            "y": rows(D, "near"),
+        },
+        {
+            "bias": scr(SQUARE, f32), "turned": scr((D, ROWS), f32), "big": scr((ROWS, D), f32),
+            "wide": scr((16, TPAD), f32),
+        },
+    )
+
+
+def run_second(y, up, table, weights):
+    return launch(
         second_whole,
-        [rows(D), rows(D), rows(D), rows(FF), rows(3 * D), rows(D), rows(FF), out((HEADS, ROWS, ROWS), f32), rows(D)],
-        [
-            scr((ROWS, 3 * D), bf16), scr((HEADS, ROWS, ROWS), bf16), scr((D, ROWS), f32), scr((ROWS, D), bf16),
-            scr((ROWS, FF), bf16), scr((ROWS, D), bf16), scr((ROWS, D), f32),
-        ],
-        y, up, bias, wqkv, wp, we, wc,
-    )
-
-
-def run_first_backward(gy, x, qkv, p, h1, slope, wqkv, wp, we, wc):
-    return call(
+        {"y": (y, "near"), "up": (up, "near"), "table": (table, "near")} | weights,
+        {
+            "n1": rows(D, "far"), "ctx": rows(D, "far"), "n2": rows(D, "far"), "act": rows(FF, "far"),
+            "dqkv": rows(3 * D, "far"), "dh": rows(D, "far"), "de": rows(FF, "far"), "ds": (SQUARE, bf16, "far"),
+            "gy": rows(D, "near"),
+        },
+        {
+            "bias": scr(SQUARE, f32), "wide": scr((16, TPAD), f32),
+            "qkv": scr((ROWS, 3 * D), bf16), "p": scr(SQUARE, bf16), "turned": scr((D, ROWS), f32),
+            "h": scr((ROWS, D), bf16), "slope": scr((ROWS, FF), bf16), "dctx": scr((ROWS, D), bf16),
+            "big": scr((ROWS, D), f32),
+        },
+    )
+
+
+HALF = ((64 * CHUNK, 128), bf16, "far")
+
+
+def run_first_backward(mine, gy, x, kept, weights):
+    return launch(
         first_backward,
-        [rows(3 * D), rows(D), rows(FF), out((HEADS, ROWS, ROWS), f32), rows(D)],
-        [scr((D, ROWS), f32), scr((ROWS, D), bf16), scr((ROWS, D), f32)],
-        gy, x, qkv, p, h1, slope, wqkv, wp, we, wc,
-    )
-
-
-def run_weights(n1, ctx, n2, act, dqkv, da, de, gy, ds):
-    return call(
-        weights_kernel, [out((128 * CHUNK, 128), bf16)], [scr((128 * CHUNK, 128), f32)],
-        n1, ctx, n2, act, dqkv, da, de, gy, ds,
-    )[0]
+        {"mine": (mine, "flag"), "gy": (gy, "near"), "x": (x, "near"), "wc": weights["wc"]}
+        | {"slope": (kept["slope"], "far"), "we": weights["we"], "h": (kept["h"], "far"), "wp": weights["wp"]}
+        | {"qkv": (kept["qkv"], "far"), "p": (kept["p"], "far"), "wqkv": weights["wqkv"]}
+        | {name: (kept[name], "far") for name in ("n1", "ctx", "n2", "act")},
+        {"dx": rows(D, "near"), "keep": HALF, "give": HALF},
+        {
+            "turned": scr((D, ROWS), f32), "dctx": scr((ROWS, D), bf16), "big": scr((ROWS, D), f32),
+            "dqkv": scr((ROWS, 3 * D), bf16), "dh": scr((ROWS, D), bf16), "de": scr((ROWS, FF), bf16),
+            "ds": scr(SQUARE, bf16), "f": scr((128 * CHUNK, 128), f32),
+        },
+    )
+
+
+def run_weights(mine, sums, gy, carried):
+    return launch(
+        weights_kernel,
+        {"mine": (mine, "flag"), "gy": (gy, "near"), "carried": (carried, "near")}
+        | {name: (sums[name], "far") for name in ("n1", "ctx", "n2", "act", "dqkv", "dh", "de", "ds")},
+        {"keep": HALF, "give": HALF, "passed": (carried.shape, carried.dtype, "near")},
+        {"f": scr((128 * CHUNK, 128), f32)},
+    )
 
 
 def passed_along(block, axis, distance):
@@ -409,11 +493,11 @@
     return jnp.concatenate([arrived, lax.slice_in_dim(grid, 0, extent - width, axis=dim)], axis=dim)
 
 
-def roll_grid(grid, direction):
-    for dim, (axis, width) in enumerate(zip(AXES, (WT // 2, WH // 2, WW // 2))):
-        moved = passed_along(edge_of(grid, dim, width, direction), axis, direction)
-        grid = rejoin(grid, dim, width, direction, moved)
-    return grid
+def rolled_along(grid, dim, direction):
+    width = (WT // 2, WH // 2, WW // 2)[dim]
+    at = grid.ndim - 4 + dim
+    moved = passed_along(edge_of(grid, at, width, direction), AXES[dim], direction)
+    return rejoin(grid, at, width, direction, moved)
 
 
 def to_rows(grid):
@@ -424,8 +508,18 @@
     return flat.reshape(WT, WH, PITCH, D)[:, :, :WW]
 
 
-def scattered(buffer):
-    spread = lax.all_to_all(buffer.reshape(128, CHUNK, 128), AXES, 0, 0, tiled=True)
+def swapped(block):
+    return lax.ppermute(block, "wa", [(i, i ^ 1) for i in range(lax.axis_size("wa"))])
+
+
+def scattered(kept, arrived):
+    both = [
+        (a.astype(f32) + b.astype(f32)).astype(bf16).reshape(64, CHUNK, 128) for a, b in zip(kept, arrived)
+    ]
+    groups = [[i for i in range(128) if i % 2 == side] for side in range(2)]
+    spread = lax.all_to_all(
+        jnp.concatenate(both, axis=1), AXES, 0, 0, axis_index_groups=groups, tiled=True
+    )
     return jnp.sum(spread.astype(f32), axis=0)
 
 
@@ -442,25 +536,29 @@
     tokens, upstream, qkv_one, proj_one, table_one, expand_one, contract_one,
     qkv_two, proj_two, table_two, expand_two, contract_two,
 ):
-    def padded(table):
-        return jnp.pad(table, ((0, 16 - HEADS), (0, TPAD - TABLE)))
-
+    mine = (lax.axis_index("wa") % 2).astype(jnp.int32).reshape(1)
     x = to_rows(tokens)
-    n1, qkv, p, ctx, h1, n2, act, slope, y = run_first_forward(
-        x, padded(table_one), qkv_one, proj_one, expand_one, contract_one
-    )
-    bias = run_bias(padded(table_two))
-    up = to_rows(roll_grid(upstream, -1))
-    rolled = to_rows(roll_grid(to_grid(y), -1))
-    n1b, ctxb, n2b, actb, dqkvb, dhb, deb, dsb, gyb = run_second(
-        rolled, up, bias, qkv_two, proj_two, expand_two, contract_two
-    )
-    gy = to_rows(roll_grid(to_grid(gyb), 1))
-    second = scattered(run_weights(n1b, ctxb, n2b, actb, dqkvb, dhb, deb, up, dsb))
-    dqkv, dh, de, ds, dx = run_first_backward(
-        gy, x, qkv, p, h1, slope, qkv_one, proj_one, expand_one, contract_one
-    )
-    first = scattered(run_weights(n1, ctx, n2, act, dqkv, dh, de, gy, ds))
+
+    def far(wqkv, wp, we, wc):
+        return {"wqkv": (wqkv, "far"), "wp": (wp, "far"), "we": (we, "far"), "wc": (wc, "far")}
+
+    weights_one = far(qkv_one, proj_one, expand_one, contract_one)
+    weights_two = far(qkv_two, proj_two, expand_two, contract_two)
+    one = run_first_forward(x, table_one, weights_one)
+    up = rolled_along(upstream, 0, -1)
+    both = jnp.stack([rolled_along(to_grid(one["y"]), 0, -1), up])
+    both = rolled_along(rolled_along(both, 1, -1), 2, -1)
+    rolled, up = to_rows(both[0]), to_rows(both[1])
+    two = run_second(rolled, up, table_two, weights_two)
+    sent = passed_along(edge_of(to_grid(two["gy"]), 0, WT // 2, 1), "ta", 1)
+    sums_two = run_weights(mine, two, up, two["gy"])
+    gy = rejoin(to_grid(sums_two["passed"]), 0, WT // 2, 1, sent)
+    gy = to_rows(rolled_along(rolled_along(gy, 1, 1), 2, 1))
+    arrived_two = swapped(lax.dynamic_update_slice(sums_two["give"], gy[:1, :128], (CHUNK - 1, 0)))
+    sums_one = run_first_backward(mine, gy, x, one, weights_one)
+    keep_one, keep_two, give_one, dx = sums_one["keep"], sums_two["keep"], sums_one["give"], sums_one["dx"]
+    total = scattered((keep_one, keep_two), (swapped(give_one), arrived_two))
+    first, second = total[:CHUNK], total[CHUNK:]
     lines = jnp.concatenate([first[108:109], second[108:109]], axis=0)
     tables = lax.all_to_all(jnp.broadcast_to(lines[None], (128, 2, 128)), AXES, 0, 0, tiled=True)
 

time: 246 us -> 185 us (0.75); the launches traced: 244 us -> 186 us
  Pallas kernels: 71.7 us -> 44.7 us
  waiting for transfers between devices: 99.1 us -> 72.8 us
  local copies, waits for them, and re-layouts: 24.8 us -> 12.6 us
  starting transfers between devices: 41.1 us -> 46 us
    ppermute x9 -> x7, waiting for transfers between devices: 50.4 us -> 18.1 us  [passed_along(): return lax.ppermute(block, axis, route)]
    pallas_call x6 -> x4, Pallas kernels: 71.7 us -> 44.7 us  [launch(): pl.pallas_call(wrapped, out_shape=[pltpu.HBM(shape, dtype) if space == 'f...]
    unnamed x57 -> x12, local copies, waits for them, and re-layouts: 15.5 us -> 2.72 us
    all_to_all x2 -> x1, starting transfers between devices: 16.5 us -> 5.9 us  [scattered(): lax.all_to_all(jnp.concatenate(both, axis=1), AXES, 0, 0, axis_index_grou...]
    ppermute x9 -> x7, starting transfers between devices: 19.5 us -> 25.5 us  [passed_along(): return lax.ppermute(block, axis, route)]
    all_to_all x1, starting transfers between devices: 5.11 us -> 10.6 us  [body(): lax.all_to_all(jnp.broadcast_to(lines[None], (128, 2, 128)), AXES, 0, 0,...]
    ppermute x0 -> x2, starting transfers between devices: none -> 3.99 us  [swapped(): lax.ppermute(block, 'wa', [(i, i ^ 1) for i in range(lax.axis_size('wa'))])]
    all_to_all x2 -> x1, waiting for transfers between devices: 40.9 us -> 44.8 us  [scattered(): lax.all_to_all(jnp.concatenate(both, axis=1), AXES, 0, 0, axis_index_grou...]
  transfers between devices with their start and end apart: 12 -> 11, of which waited for: 7 -> 9; matrix products, arithmetic and copies ran while one was open for 4% -> 5% of each run, Pallas kernels for 10% -> 10%
where the time goes in v2:
time: 185 us; the launch traced here: 186 us
  waiting for transfers between devices  72.8 us (39%)
  starting transfers between devices  46 us (25%)
  Pallas kernels  44.7 us (24%)
  local copies, waits for them, and re-layouts  12.6 us (7%)
  other arithmetic  8.4 us (5%)
    all_to_all x1, waiting for transfers between devices, scattered(): lax.all_to_all(jnp.concatenate(both, axis=1), AXES, 0, 0, axis_index_grou...  44.8 us
    pallas_call x4, Pallas kernels, launch(): pl.pallas_call(wrapped, out_shape=[pltpu.HBM(shape, dtype) if space == 'f...  44.7 us
    ppermute x7, starting transfers between devices, passed_along(): return lax.ppermute(block, axis, route)  25.5 us
    ppermute x7, waiting for transfers between devices, passed_along(): return lax.ppermute(block, axis, route)  18.1 us
    all_to_all x1, starting transfers between devices, body(): lax.all_to_all(jnp.broadcast_to(lines[None], (128, 2, 128)), AXES, 0, 0,...  10.6 us
    all_to_all x1, waiting for transfers between devices, body(): lax.all_to_all(jnp.broadcast_to(lines[None], (128, 2, 128)), AXES, 0, 0,...  7.12 us
    all_to_all x1, starting transfers between devices, scattered(): lax.all_to_all(jnp.concatenate(both, axis=1), AXES, 0, 0, axis_index_grou...  5.9 us
    ppermute x2, starting transfers between devices, swapped(): lax.ppermute(block, 'wa', [(i, i ^ 1) for i in range(lax.axis_size('wa'))])  3.99 us
  transfers between devices with their start and end apart: 11, of which 9 were waited for; matrix products, arithmetic and copies ran while one was open for 5% of the time, Pallas kernels for 10%

profile of v2, /device:TPU:1, one launch (start us, length us, event | category | flops | bytes accessed | tf_op | source)
XLA Modules:
  0.0 185.7 jit_solution(4099174060584772591)
XLA Ops:
  0.6 1.1 fusion.10
  1.8 3.7 %collective-permute-start.1 = (bf16[2,7,7,384]{3,0,2,1:T(2,128)(2,1)S(1)}, bf16[2,7,7,384]{3,0,2,1:T(2,128)(2,1)S(1)}, u32[]{:S(2)}, u32[]{:S(2)}) collective-permute-start(bf16[2,7,7,384]{3,0,2,1:T(2,128)(2,1)S(1)} %get-tuple-element.66), channel_id=1, source_target_pairs={{64,0},{0,64},{65,1},{1,65},{66,2},{2,66},{67,3},{3,67},{68,4},{4,... | collective-permute-start | bytes 225800 | tf_op jit(solution)/shard_map/ppermute | solution.py:479
  7.3 8.0 %shard_map.203 = (bf16[224,384]{1,0:T(8,128)(2,1)}, bf16[224,1152]{1,0:T(8,128)(2,1)}, bf16[12,224,224]{2,1,0:T(8,128)(2,1)}, bf16[224,384]{1,0:T(8,128)(2,1)}, ...) custom-call(bf16[224,384]{1,0:T(8,128)(2,1)S(1)} %bitcast.22, ...), custom_call_target="tpu_custom_call" | custom-call | tf_op jit(solution)/shard_map/pallas_call | solution.py:75
  15.8 4.5 %collective-permute-done = bf16[2,7,7,384]{3,0,2,1:T(2,128)(2,1)S(1)} collective-permute-done((bf16[2,7,7,384]{3,0,2,1:T(2,128)(2,1)S(1)}, bf16[2,7,7,384]{3,0,2,1:T(2,128)(2,1)S(1)}, u32[]{:S(2)}, u32[]{:S(2)}) %collective-permute-start) | collective-permute-done | bytes 75296 | tf_op jit(solution)/shard_map/ppermute | solution.py:479
  20.5 3.1 %collective-permute-start.2 = (bf16[2,4,3,7,384]{4,1,3,2,0:T(4,128)(2,1)S(1)}, bf16[2,4,3,7,384]{4,1,3,2,0:T(4,128)(2,1)S(1)}, u32[]{:S(2)}, u32[]{:S(2)}) collective-permute-start(bf16[2,4,3,7,384]{4,1,3,2,0:T(4,128)(2,1)S(1)} %pad_maximum_fusion.4), channel_id=1, source_target_pairs={{8,0},{16,8},{24,16},{32,24},{40,32},{48,40},{56,48},{0,56},{9,1},... | collective-permute-start | bytes 387080 | tf_op jit(solution)/shard_map/ppermute | solution.py:479
  23.7 1.8 collective-permute-done.2
  25.6 3.0 %collective-permute-start.3 = (bf16[2,4,7,3,384]{4,1,3,2,0:T(4,128)(2,1)S(1)}, bf16[2,4,7,3,384]{4,1,3,2,0:T(4,128)(2,1)S(1)}, u32[]{:S(2)}, u32[]{:S(2)}) collective-permute-start(bf16[2,4,7,3,384]{4,1,3,2,0:T(4,128)(2,1)S(1)} %pad_maximum_fusion.3), channel_id=1, source_target_pairs={{1,0},{2,1},{3,2},{4,3},{5,4},{6,5},{7,6},{0,7},{9,8},{10,9},{11,1... | collective-permute-start | bytes 387080 | tf_op jit(solution)/shard_map/ppermute | solution.py:479
  28.7 4.0 %collective-permute-done.3 = bf16[2,4,7,3,384]{4,1,3,2,0:T(4,128)(2,1)S(1)} collective-permute-done((bf16[2,4,7,3,384]{4,1,3,2,0:T(4,128)(2,1)S(1)}, bf16[2,4,7,3,384]{4,1,3,2,0:T(4,128)(2,1)S(1)}, u32[]{:S(2)}, u32[]{:S(2)}) %collective-permute-start.3) | collective-permute-done | bytes 129056 | tf_op jit(solution)/shard_map/ppermute | solution.py:479
  33.1 12.3 %shard_map.204 = (bf16[224,384]{1,0:T(8,128)(2,1)}, bf16[224,384]{1,0:T(8,128)(2,1)}, bf16[224,384]{1,0:T(8,128)(2,1)}, bf16[224,1536]{1,0:T(8,128)(2,1)}, bf16[...) custom-call(bf16[224,384]{1,0:T(8,128)(2,1)S(1)} %bitcast.28, ...), custom_call_target="tpu_custom_call" | custom-call | tf_op jit(solution)/shard_map/pallas_call | solution.py:75
  45.4 15.3 %collective-permute-start.4 = (bf16[2,7,7,384]{3,2,1,0:T(8,128)(2,1)S(1)}, bf16[2,7,7,384]{3,2,1,0:T(8,128)(2,1)S(1)}, u32[]{:S(2)}, u32[]{:S(2)}) collective-permute-start(bf16[2,7,7,384]{3,2,1,0:T(8,128)(2,1)S(1)} %slice.155), channel_id=1, source_target_pairs={{64,0},{0,64},{65,1},{1,65},{66,2},{2,66},{67,3},{3,67},{68,4},{4,... | collective-permute-start | bytes 225800 | tf_op jit(solution)/shard_map/ppermute | solution.py:479
  60.7 9.9 %shard_map.205 = (bf16[7168,128]{1,0:T(8,128)(2,1)}, bf16[7168,128]{1,0:T(8,128)(2,1)}, bf16[224,384]{1,0:T(8,128)(2,1)S(1)}) custom-call(s32[1]{0:T(128)} %bitcast.refs_0_, bf16[224,384]{1,0:T(8,128)(2,1)S(1)} %bitcast.25, bf16[224,384]{1,0:T(8,128)(2,1)S(1)} %get-tuple-element.36.refs_2_, bf16[224,384]{1,0:T(8,128)(2,1)} %get-tuple-element.37.refs_3_, ...), custom_call_target="tpu_custom_call" | custom-call | tf_op jit(solution)/shard_map/pallas_call | solution.py:75
  70.8 6.3 %collective-permute-done.5 = bf16[4,3,7,384]{3,2,1,0:T(8,128)(2,1)S(1)} collective-permute-done((bf16[4,3,7,384]{3,2,1,0:T(8,128)(2,1)S(1)}, bf16[4,3,7,384]{3,2,1,0:T(8,128)(2,1)S(1)}, u32[]{:S(2)}, u32[]{:S(2)}) %collective-permute-start.5) | collective-permute-done | bytes 64544 | tf_op jit(solution)/shard_map/ppermute | solution.py:479
  77.5 1.5 collective-permute-done.6
  79.2 14.5 %shard_map.206 = (bf16[224,384]{1,0:T(8,128)(2,1)S(1)}, bf16[7168,128]{1,0:T(8,128)(2,1)}, bf16[7168,128]{1,0:T(8,128)(2,1)}) custom-call(s32[1]{0:T(128)} %bitcast.refs_0_, bf16[224,384]{1,0:T(8,128)(2,1)S(1)} %bitcast.26, bf16[224,384]{1,0:T(8,128)(2,1)S(1)} %bitcast.23, bf16[1536,384]{1,0:T(8,128)(2,1)} %refs_3_.5, ...), custom_call_target="tpu_custom_call" | custom-call | tf_op jit(solution)/shard_map/pallas_call | solution.py:75
  93.7 4.0 %collective-permute-start.7 = (bf16[7168,128]{1,0:T(8,128)(2,1)}, bf16[7168,128]{1,0:T(8,128)(2,1)S(1)}, u32[]{:S(2)}, u32[]{:S(2)}) collective-permute-start(bf16[7168,128]{1,0:T(8,128)(2,1)} %get-tuple-element.56), channel_id=1, source_target_pairs={{0,1},{1,0},{2,3},{3,2},{4,5},{5,4},{6,7},{7,6},{8,9},{9,8},{10,11... | collective-permute-start | bytes 5505032 | tf_op jit(solution)/shard_map/ppermute | solution.py:512
  97.6 1.3 dynamic_update_slice.3
  99.0 2.3 %collective-permute-done.7 = bf16[7168,128]{1,0:T(8,128)(2,1)S(1)} collective-permute-done((bf16[7168,128]{1,0:T(8,128)(2,1)}, bf16[7168,128]{1,0:T(8,128)(2,1)S(1)}, u32[]{:S(2)}, u32[]{:S(2)}) %collective-permute-start.7) | collective-permute-done | bytes 1835040 | tf_op jit(solution)/shard_map/ppermute | solution.py:512
  101.3 2.1 %add_convert_fusion.1 = bf16[7168,128]{1,0:T(8,128)(2,1)S(1)} fusion(bf16[7168,128]{1,0:T(8,128)(2,1)S(1)} %collective-permute-done.7, bf16[7168,128]{1,0:T(8,128)(2,1)} %get-tuple-element.55), kind=kLoop, calls=%fused_computation.3 | loop fusion | flops 3670016 | bytes 5505024 | tf_op jit(solution)/shard_map/convert_element_type | solution.py:517
  104.4 2.1 %pad_maximum_fusion = bf16[64,224,128]{2,1,0:T(8,128)(2,1)} fusion(bf16[64,112,128]{2,1,0:T(8,128)(2,1)S(1)} %bitcast.34, bf16[64,112,128]{2,1,0:T(8,128)(2,1)S(1)} %bitcast.33), kind=kLoop, calls=%fused_computation.1 | loop fusion | flops 7340032 | bytes 7340032 | tf_op jit(solution)/shard_map/concatenate | solution.py:521
  106.5 5.9 %all-to-all-start = ((bf16[64,224,128]{2,1,0:T(8,128)(2,1)}), bf16[64,224,128]{2,1,0:T(8,128)(2,1)}, u32[]{:S(2)}, u32[]{:S(2)}) async-start(bf16[64,224,128]{2,1,0:T(8,128)(2,1)} %pad_maximum_fusion), calls=%async_computation | async-start | bytes 7340032 | tf_op jit(solution)/shard_map/all_to_all | solution.py:520
  113.1 44.8 %all-to-all-done = bf16[64,224,128]{2,1,0:T(8,128)(2,1)} async-done(((bf16[64,224,128]{2,1,0:T(8,128)(2,1)}), bf16[64,224,128]{2,1,0:T(8,128)(2,1)}, u32[]{:S(2)}, u32[]{:S(2)}) %all-to-all-start) | async-done | bytes 3670048 | tf_op jit(solution)/shard_map/all_to_all | solution.py:520
  157.9 2.6 %convert_reduce_fusion = f32[224,128]{1,0:T(8,128)S(1)} fusion(bf16[64,224,128]{2,1,0:T(8,128)(2,1)} %all-to-all-done), kind=kLoop, calls=%fused_computation | loop fusion | flops 3641344 | bytes 3784704 | tf_op jit(solution)/shard_map/reduce_sum | solution.py:523
  163.0 10.6 %all-to-all-start.1 = ((f32[128,2,128]{2,1,0:T(2,128)}), f32[128,2,128]{2,1,0:T(2,128)S(1)}, u32[]{:S(2)}, u32[]{:S(2)}) async-start(f32[128,2,128]{2,1,0:T(2,128)} %broadcast_in_dim.2), calls=%async_computation.1 | async-start | bytes 262144 | tf_op jit(solution)/shard_map/all_to_all | solution.py:563
  176.8 7.1 %all-to-all-done.1 = f32[128,2,128]{2,1,0:T(2,128)S(1)} async-done(((f32[128,2,128]{2,1,0:T(2,128)}), f32[128,2,128]{2,1,0:T(2,128)S(1)}, u32[]{:S(2)}, u32[]{:S(2)}) %all-to-all-start.1) | async-done | bytes 131104 | tf_op jit(solution)/shard_map/all_to_all | solution.py:563
  (56 shorter events, 12.8 us)
Async XLA Ops:
  1.8 13.8 %collective-permute-start.1 = (bf16[2,7,7,384]{3,0,2,1:T(2,128)(2,1)S(1)}, bf16[2,7,7,384]{3,0,2,1:T(2,128)(2,1)S(1)}, u32[]{:S(2)}, u32[]{:S(2)}) collective-permute-start(bf16[2,7,7,384]{3,0,2,1:T(2,128)(2,1)S(1)} %get-tuple-element.66), channel_id=1, source_target_pairs={{64,0},{0,64},{65,1},{1,65},{66,2},{2,66},{67,3},{3,67},{68,4},{4,... | collective-permute-start | bytes 225800 | tf_op jit(solution)/shard_map/ppermute | solution.py:479
  6.4 0.9 copy-start.1
  15.4 4.8 %collective-permute-start = (bf16[2,7,7,384]{3,0,2,1:T(2,128)(2,1)S(1)}, bf16[2,7,7,384]{3,0,2,1:T(2,128)(2,1)S(1)}, u32[]{:S(2)}, u32[]{:S(2)}) collective-permute-start(bf16[2,7,7,384]{3,0,2,1:T(2,128)(2,1)S(1)} %copy.36), channel_id=1, source_target_pairs={{64,0},{0,64},{65,1},{1,65},{66,2},{2,66},{67,3},{3,67},{68,4},{4,... | collective-permute-start | bytes 225800 | tf_op jit(solution)/shard_map/ppermute | solution.py:479
  20.4 12.7 %copy-start = (f32[12,1183]{1,0:T(8,128)S(1)}, f32[12,1183]{1,0:T(8,128)}, u32[]{:S(2)}) copy-start(f32[12,1183]{1,0:T(8,128)} %refs_2_.3) | copy-start | bytes 170356
  20.5 5.0 %collective-permute-start.2 = (bf16[2,4,3,7,384]{4,1,3,2,0:T(4,128)(2,1)S(1)}, bf16[2,4,3,7,384]{4,1,3,2,0:T(4,128)(2,1)S(1)}, u32[]{:S(2)}, u32[]{:S(2)}) collective-permute-start(bf16[2,4,3,7,384]{4,1,3,2,0:T(4,128)(2,1)S(1)} %pad_maximum_fusion.4), channel_id=1, source_target_pairs={{8,0},{16,8},{24,16},{32,24},{40,32},{48,40},{56,48},{0,56},{9,1},... | collective-permute-start | bytes 387080 | tf_op jit(solution)/shard_map/ppermute | solution.py:479
  25.6 7.1 %collective-permute-start.3 = (bf16[2,4,7,3,384]{4,1,3,2,0:T(4,128)(2,1)S(1)}, bf16[2,4,7,3,384]{4,1,3,2,0:T(4,128)(2,1)S(1)}, u32[]{:S(2)}, u32[]{:S(2)}) collective-permute-start(bf16[2,4,7,3,384]{4,1,3,2,0:T(4,128)(2,1)S(1)} %pad_maximum_fusion.3), channel_id=1, source_target_pairs={{1,0},{2,1},{3,2},{4,3},{5,4},{6,5},{7,6},{0,7},{9,8},{10,9},{11,1... | collective-permute-start | bytes 387080 | tf_op jit(solution)/shard_map/ppermute | solution.py:479
  45.4 25.2 %collective-permute-start.4 = (bf16[2,7,7,384]{3,2,1,0:T(8,128)(2,1)S(1)}, bf16[2,7,7,384]{3,2,1,0:T(8,128)(2,1)S(1)}, u32[]{:S(2)}, u32[]{:S(2)}) collective-permute-start(bf16[2,7,7,384]{3,2,1,0:T(8,128)(2,1)S(1)} %slice.155), channel_id=1, source_target_pairs={{64,0},{0,64},{65,1},{1,65},{66,2},{2,66},{67,3},{3,67},{68,4},{4,... | collective-permute-start | bytes 225800 | tf_op jit(solution)/shard_map/ppermute | solution.py:479
  70.7 6.4 %collective-permute-start.5 = (bf16[4,3,7,384]{3,2,1,0:T(8,128)(2,1)S(1)}, bf16[4,3,7,384]{3,2,1,0:T(8,128)(2,1)S(1)}, u32[]{:S(2)}, u32[]{:S(2)}) collective-permute-start(bf16[4,3,7,384]{3,2,1,0:T(8,128)(2,1)S(1)} %pad_maximum_fusion.5), channel_id=1, source_target_pairs={{56,0},{0,8},{8,16},{16,24},{24,32},{32,40},{40,48},{48,56},{57,1}... | collective-permute-start | bytes 193544 | tf_op jit(solution)/shard_map/ppermute | solution.py:479
  77.2 1.8 collective-permute-start.6
  93.7 7.6 %collective-permute-start.7 = (bf16[7168,128]{1,0:T(8,128)(2,1)}, bf16[7168,128]{1,0:T(8,128)(2,1)S(1)}, u32[]{:S(2)}, u32[]{:S(2)}) collective-permute-start(bf16[7168,128]{1,0:T(8,128)(2,1)} %get-tuple-element.56), channel_id=1, source_target_pairs={{0,1},{1,0},{2,3},{3,2},{4,5},{5,4},{6,7},{7,6},{8,9},{9,8},{10,11... | collective-permute-start | bytes 5505032 | tf_op jit(solution)/shard_map/ppermute | solution.py:512
  98.9 5.0 %collective-permute-start.8 = (bf16[7168,128]{1,0:T(8,128)(2,1)}, bf16[7168,128]{1,0:T(8,128)(2,1)S(1)}, u32[]{:S(2)}, u32[]{:S(2)}) collective-permute-start(bf16[7168,128]{1,0:T(8,128)(2,1)} %dynamic_update_slice.3), channel_id=1, source_target_pairs={{0,1},{1,0},{2,3},{3,2},{4,5},{5,4},{6,7},{7,6},{8,9},{9,8},{10,11... | collective-permute-start | bytes 5505032 | tf_op jit(solution)/shard_map/ppermute | solution.py:512
  101.3 2.6 %copy-start.2 = (bf16[7168,128]{1,0:T(8,128)(2,1)S(1)}, bf16[7168,128]{1,0:T(8,128)(2,1)}, u32[]{:S(2)}) copy-start(bf16[7168,128]{1,0:T(8,128)(2,1)} %get-tuple-element.57) | copy-start | bytes 5505028
  106.5 51.4 %all-to-all-start = ((bf16[64,224,128]{2,1,0:T(8,128)(2,1)}), bf16[64,224,128]{2,1,0:T(8,128)(2,1)}, u32[]{:S(2)}, u32[]{:S(2)}) async-start(bf16[64,224,128]{2,1,0:T(8,128)(2,1)} %pad_maximum_fusion), calls=%async_computation | async-start | bytes 7340032 | tf_op jit(solution)/shard_map/all_to_all | solution.py:520
  163.0 20.9 %all-to-all-start.1 = ((f32[128,2,128]{2,1,0:T(2,128)}), f32[128,2,128]{2,1,0:T(2,128)S(1)}, u32[]{:S(2)}, u32[]{:S(2)}) async-start(f32[128,2,128]{2,1,0:T(2,128)} %broadcast_in_dim.2), calls=%async_computation.1 | async-start | bytes 262144 | tf_op jit(solution)/shard_map/all_to_all | solution.py:563

commit v3 on v2

--- a/solution.py
+++ b/solution.py
@@ -50,24 +50,38 @@
 
 
 def launch(kernel, ins, outs, scratch=()):
-    places = {"far": pltpu.HBM, "near": pltpu.VMEM, "flag": pltpu.SMEM}
-    far_ins = [n for n, (_, space) in ins.items() if space == "far"]
-    far_outs = [n for n, (_, _, space) in outs.items() if space == "far"]
+    places = {"parts": pltpu.HBM, "far": pltpu.HBM, "near": pltpu.VMEM, "flag": pltpu.SMEM, "pass": pltpu.HBM}
+    passed = [n for n, (_, space) in ins.items() if space == "pass"]
+    outs = dict(outs) | {n: (ins[n][0].shape, ins[n][0].dtype, "pass") for n in passed}
     scratch = dict(scratch)
-    buffers = {n: pltpu.VMEM(ins[n][0].shape, ins[n][0].dtype) for n in far_ins}
-    buffers.update({n: pltpu.VMEM(outs[n][0], outs[n][1]) for n in far_outs})
+    buffers = {}
+
+    def copied(named, space, shape, dtype):
+        cuts = {"far": 1, "parts": PIECES}.get(space, 0)
+        size = shape[0] // max(cuts, 1)
+        names = [named] if cuts == 1 else [f"{named}{i}" for i in range(cuts)]
+        for name in names:
+            buffers[name] = pltpu.VMEM((size,) + tuple(shape[1:]), dtype)
+        return {name: (named, i * size, size) for i, name in enumerate(names)}
+
+    far_ins, far_outs = {}, {}
+    for n, (array, space) in ins.items():
+        far_ins |= copied(n, space, array.shape, array.dtype)
+    for n, (shape, dtype, space) in outs.items():
+        far_outs |= copied(n, space, shape, dtype)
 
     def wrapped(*refs):
         named = dict(zip(list(ins) + list(outs), refs))
-        rest = refs[len(named) :]
+        rest = refs[len(ins) + len(outs) :]
         near = dict(zip(list(scratch) + list(buffers), rest))
         sems = rest[-1]
         incoming, outgoing = {}, {}
-        for i, n in enumerate(far_ins):
-            incoming[n] = pltpu.make_async_copy(named[n], near[n], sems.at[i])
+        for i, (n, (whole, first, size)) in enumerate(far_ins.items()):
+            incoming[n] = pltpu.make_async_copy(named[whole].at[pl.ds(first, size)], near[n], sems.at[i])
             incoming[n].start()
-        for i, n in enumerate(far_outs):
-            outgoing[n] = pltpu.make_async_copy(near[n], named[n], sems.at[len(far_ins) + i])
+        for i, (n, (whole, first, size)) in enumerate(far_outs.items()):
+            cut = named[whole].at[pl.ds(first, size)]
+            outgoing[n] = pltpu.make_async_copy(near[n], cut, sems.at[len(far_ins) + i])
         kernel(Held({**named, **near}, incoming, outgoing))
         for n in far_outs:
             outgoing[n].wait()
@@ -75,18 +89,19 @@
     results = pl.pallas_call(
         wrapped,
         out_shape=[
-            pltpu.HBM(shape, dtype) if space == "far" else jax.ShapeDtypeStruct(shape, dtype)
+            pltpu.HBM(shape, dtype) if space in ("far", "parts", "pass") else jax.ShapeDtypeStruct(shape, dtype)
             for shape, dtype, space in outs.values()
         ],
         in_specs=[pl.BlockSpec(memory_space=places[space]) for _, space in ins.values()],
         out_specs=[pl.BlockSpec(memory_space=places[space]) for _, _, space in outs.values()],
+        input_output_aliases={list(ins).index(n): list(outs).index(n) for n in passed},
         scratch_shapes=list(scratch.values())
         + list(buffers.values())
         + [pltpu.SemaphoreType.DMA((max(1, len(far_ins) + len(far_outs)),))],
         compiler_params=pltpu.CompilerParams(vmem_limit_bytes=VMEM_LIMIT),
     )(
         *[
-            pltpu.with_memory_space_constraint(array, pltpu.HBM) if space == "far" else array
+            pltpu.with_memory_space_constraint(array, pltpu.HBM) if space in ("far", "parts", "pass") else array
             for array, space in ins.values()
         ]
     )
@@ -447,13 +462,14 @@
 HALF = ((64 * CHUNK, 128), bf16, "far")
 
 
-def run_first_backward(mine, gy, x, kept, weights):
+def run_first_backward(mine, gy, x, kept, weights, give_two):
     return launch(
         first_backward,
         {"mine": (mine, "flag"), "gy": (gy, "near"), "x": (x, "near"), "wc": weights["wc"]}
         | {"slope": (kept["slope"], "far"), "we": weights["we"], "h": (kept["h"], "far"), "wp": weights["wp"]}
         | {"qkv": (kept["qkv"], "far"), "p": (kept["p"], "far"), "wqkv": weights["wqkv"]}
-        | {name: (kept[name], "far") for name in ("n1", "ctx", "n2", "act")},
+        | {name: (kept[name], "far") for name in ("n1", "ctx", "n2", "act")}
+        | {"give_two": (give_two, "pass")},
         {"dx": rows(D, "near"), "keep": HALF, "give": HALF},
         {
             "turned": scr((D, ROWS), f32), "dctx": scr((ROWS, D), bf16), "big": scr((ROWS, D), f32),
@@ -473,6 +489,75 @@
     )
 
 
+PIECES = 4
+
+
+def merge_kernel(m):
+    per = 64 // PIECES
+    for piece in range(PIECES):
+        m.need(f"keep_one{piece}", f"keep_two{piece}")
+        keeps = m.__dict__[f"keep_one{piece}"], m.__dict__[f"keep_two{piece}"]
+
+        def step(j, carry):
+            chunk = pl.ds(pl.multiple_of((piece * per + j) * CHUNK, CHUNK), CHUNK)
+            own = pl.ds(pl.multiple_of(j * CHUNK, CHUNK), CHUNK)
+            for b, (kept, arrived) in enumerate(zip(keeps, (m.arrived_one, m.arrived_two))):
+                total = kept[own, :].astype(f32) + arrived[chunk, :].astype(f32)
+                to = pl.ds(pl.multiple_of((2 * j + b) * CHUNK, CHUNK), CHUNK)
+                m.__dict__[f"both{piece}"][to, :] = total.astype(bf16)
+            return carry
+
+        lax.fori_loop(0, per, step, 0, unroll=4)
+        m.ready(f"both{piece}")
+
+
+def run_merge(keep_one, keep_two, arrived_one, arrived_two):
+    ins = {"keep_two": keep_two, "keep_one": keep_one}
+    near = {"arrived_one": arrived_one, "arrived_two": arrived_two}
+    both = launch(
+        merge_kernel,
+        {name: (array, "parts") for name, array in ins.items()} | {name: (array, "near") for name, array in near.items()},
+        {"both": ((128 * CHUNK, 128), bf16, "parts")},
+    )["both"]
+    return both.reshape(64, 2 * CHUNK, 128)
+
+
+def finish_kernel(m):
+    per = 64 // PIECES
+    total = None
+    for piece in range(PIECES):
+        m.need(f"spread{piece}")
+        part = m.__dict__[f"spread{piece}"]
+
+        def step(i, carry):
+            return carry + part[i].astype(f32)
+
+        total = lax.fori_loop(0, per, step, total if piece else jnp.zeros((2 * CHUNK, 128), f32), unroll=2)
+    m.total[...] = total
+    for b in range(2):
+        at = b * CHUNK
+        for name, first, count, width in (("qkv", 0, 3, 9), ("proj", 27, 3, 3), ("expand", 36, 3, 12), ("contract", 72, 12, 3)):
+            target = m.__dict__[f"{name}_{b}"]
+            for r in range(count):
+                for c in range(width):
+                    row = at + first + r * width + c
+                    target[r : r + 1, c * 128 : c * 128 + 128] = m.total[row : row + 1, :]
+        m.lines[:, b, :] = jnp.broadcast_to(m.total[at + 108 : at + 109, :], (128, 128))
+
+
+def run_finish(spread):
+    outs = {}
+    for b in range(2):
+        outs |= {f"qkv_{b}": ((3, 3 * D), f32, "near"), f"proj_{b}": ((3, D), f32, "near")}
+        outs |= {f"expand_{b}": ((3, FF), f32, "near"), f"contract_{b}": ((12, D), f32, "near")}
+    return launch(
+        finish_kernel,
+        {"spread": (spread, "parts")},
+        outs | {"lines": ((128, 2, 128), f32, "near")},
+        {"total": pltpu.VMEM((2 * CHUNK, 128), f32)},
+    )
+
+
 def passed_along(block, axis, distance):
     devices = range(lax.axis_size(axis))
     route = [((i - distance) % len(devices), i) for i in devices]
@@ -512,24 +597,9 @@
     return lax.ppermute(block, "wa", [(i, i ^ 1) for i in range(lax.axis_size("wa"))])
 
 
-def scattered(kept, arrived):
-    both = [
-        (a.astype(f32) + b.astype(f32)).astype(bf16).reshape(64, CHUNK, 128) for a, b in zip(kept, arrived)
-    ]
+def exchanged(both):
     groups = [[i for i in range(128) if i % 2 == side] for side in range(2)]
-    spread = lax.all_to_all(
-        jnp.concatenate(both, axis=1), AXES, 0, 0, axis_index_groups=groups, tiled=True
-    )
-    return jnp.sum(spread.astype(f32), axis=0)
-
-
-def weight_parts(chunk):
-    return (
-        chunk[0:27].reshape(3, 3 * D),
-        chunk[27:36].reshape(3, D),
-        chunk[36:72].reshape(3, FF),
-        chunk[72:108].reshape(12, D),
-    )
+    return lax.all_to_all(both, AXES, 0, 0, axis_index_groups=groups, tiled=True)
 
 
 def body(
@@ -545,27 +615,28 @@
     weights_one = far(qkv_one, proj_one, expand_one, contract_one)
     weights_two = far(qkv_two, proj_two, expand_two, contract_two)
     one = run_first_forward(x, table_one, weights_one)
-    up = rolled_along(upstream, 0, -1)
-    both = jnp.stack([rolled_along(to_grid(one["y"]), 0, -1), up])
-    both = rolled_along(rolled_along(both, 1, -1), 2, -1)
+    both = jnp.stack([to_grid(one["y"]), upstream])
+    for dim in range(3):
+        both = rolled_along(both, dim, -1)
     rolled, up = to_rows(both[0]), to_rows(both[1])
     two = run_second(rolled, up, table_two, weights_two)
-    sent = passed_along(edge_of(to_grid(two["gy"]), 0, WT // 2, 1), "ta", 1)
-    sums_two = run_weights(mine, two, up, two["gy"])
-    gy = rejoin(to_grid(sums_two["passed"]), 0, WT // 2, 1, sent)
-    gy = to_rows(rolled_along(rolled_along(gy, 1, 1), 2, 1))
-    arrived_two = swapped(lax.dynamic_update_slice(sums_two["give"], gy[:1, :128], (CHUNK - 1, 0)))
-    sums_one = run_first_backward(mine, gy, x, one, weights_one)
-    keep_one, keep_two, give_one, dx = sums_one["keep"], sums_two["keep"], sums_one["give"], sums_one["dx"]
-    total = scattered((keep_one, keep_two), (swapped(give_one), arrived_two))
-    first, second = total[:CHUNK], total[CHUNK:]
-    lines = jnp.concatenate([first[108:109], second[108:109]], axis=0)
-    tables = lax.all_to_all(jnp.broadcast_to(lines[None], (128, 2, 128)), AXES, 0, 0, tiled=True)
+    gy = rolled_along(to_grid(two["gy"]), 0, 1)
+    sent = passed_along(edge_of(gy, 1, WH // 2, 1), AXES[1], 1)
+    sums_two = run_weights(mine, two, up, to_rows(gy))
+    gy = rejoin(to_grid(sums_two["passed"]), 1, WH // 2, 1, sent)
+    gy = to_rows(rolled_along(gy, 2, 1))
+    sums_one = run_first_backward(mine, gy, x, one, weights_one, sums_two["give"])
+    dx = sums_one["dx"]
+    spread = exchanged(
+        run_merge(sums_one["keep"], sums_two["keep"], swapped(sums_one["give"]), swapped(sums_one["give_two"]))
+    )
+    done = run_finish(spread)
+    tables = lax.all_to_all(done["lines"], AXES, 0, 0, tiled=True)
 
     def table_of(which):
         return tables[:120, which].reshape(HEADS, TPAD)[:, :TABLE]
 
-    g1, g2 = weight_parts(first), weight_parts(second)
+    g1, g2 = ([done[f"{name}_{b}"] for name in ("qkv", "proj", "expand", "contract")] for b in range(2))
     return (
         to_grid(dx), g1[0], g1[1], table_of(0), g1[2], g1[3],
         g2[0], g2[1], table_of(1), g2[2], g2[3],

time: 185 us -> 168 us (0.908)
  blocking collectives: 0 us -> 55.2 us
  waiting for transfers between devices: 72.8 us -> 29.3 us
  starting transfers between devices: 46 us -> 25.5 us
  local copies, waits for them, and re-layouts: 12.6 us -> 4.44 us
  other arithmetic: 8.4 us -> 1.27 us
  Pallas kernels: 44.7 us -> 51.5 us
    all_to_all x0 -> x1, blocking collectives: none -> 55.2 us  [exchanged(): lax.all_to_all(both, AXES, 0, 0, axis_index_groups=groups, tiled=True)]
    all_to_all x2 -> x1, waiting for transfers between devices: 51.9 us -> 9.5 us  [body(): tables = lax.all_to_all(done['lines'], AXES, 0, 0, tiled=True)]
    ppermute x7 -> x6, starting transfers between devices: 25.5 us -> 14.3 us  [passed_along(): return lax.ppermute(block, axis, route)]
    all_to_all x2 -> x1, starting transfers between devices: 16.5 us -> 6.83 us  [body(): tables = lax.all_to_all(done['lines'], AXES, 0, 0, tiled=True)]
    pallas_call x4 -> x6, Pallas kernels: 44.7 us -> 51.5 us  [launch(): pl.pallas_call(wrapped, out_shape=[pltpu.HBM(shape, dtype) if space in ('...]
    reshape x8 -> x0, local copies, waits for them, and re-layouts: 4.9 us -> none  [the longest x2 1.24 us: weight_parts(): chunk[36:72].reshape(3, FF)]
    ppermute x7 -> x6, waiting for transfers between devices: 18.1 us -> 13.6 us  [passed_along(): return lax.ppermute(block, axis, route)]
    ppermute x2, waiting for transfers between devices: 2.82 us -> 6.15 us  [swapped(): lax.ppermute(block, 'wa', [(i, i ^ 1) for i in range(lax.axis_size('wa'))])]
  transfers between devices with their start and end apart: 11 -> 9, of which waited for: 9 -> 8; matrix products, arithmetic and copies ran while one was open for 5% -> 1% of each run, Pallas kernels for 10% -> 6%
where the time goes in v3:
time: 168 us
  blocking collectives  55.2 us (33%)
  Pallas kernels  51.5 us (31%)
  waiting for transfers between devices  29.3 us (17%)
  starting transfers between devices  25.5 us (15%)
  local copies, waits for them, and re-layouts  4.44 us (3%)
    all_to_all x1, blocking collectives, exchanged(): lax.all_to_all(both, AXES, 0, 0, axis_index_groups=groups, tiled=True)  55.2 us
    pallas_call x6, Pallas kernels, launch(): pl.pallas_call(wrapped, out_shape=[pltpu.HBM(shape, dtype) if space in ('...  51.5 us
    ppermute x6, starting transfers between devices, passed_along(): return lax.ppermute(block, axis, route)  14.3 us
    ppermute x6, waiting for transfers between devices, passed_along(): return lax.ppermute(block, axis, route)  13.6 us
    all_to_all x1, waiting for transfers between devices, body(): tables = lax.all_to_all(done['lines'], AXES, 0, 0, tiled=True)  9.5 us
    all_to_all x1, starting transfers between devices, body(): tables = lax.all_to_all(done['lines'], AXES, 0, 0, tiled=True)  6.83 us
    ppermute x2, waiting for transfers between devices, swapped(): lax.ppermute(block, 'wa', [(i, i ^ 1) for i in range(lax.axis_size('wa'))])  6.15 us
    ppermute x2, starting transfers between devices, swapped(): lax.ppermute(block, 'wa', [(i, i ^ 1) for i in range(lax.axis_size('wa'))])  4.35 us
  transfers between devices with their start and end apart: 9, of which 8 were waited for; matrix products, arithmetic and copies ran while one was open for 1% of the time, Pallas kernels for 6%

profile of v3, /device:TPU:1, one launch (start us, length us, event | category | flops | bytes accessed | tf_op | source)
XLA Modules:
  0.0 168.1 jit_solution(9545942600666512094)
XLA Ops:
  0.6 0.9 copy.31
  1.6 0.9 copy-done.1
  2.5 8.1 %shard_map.203 = (bf16[224,384]{1,0:T(8,128)(2,1)}, bf16[224,1152]{1,0:T(8,128)(2,1)}, bf16[12,224,224]{2,1,0:T(8,128)(2,1)}, bf16[224,384]{1,0:T(8,128)(2,1)}, ...) custom-call(bf16[224,384]{1,0:T(8,128)(2,1)S(1)} %bitcast.25, ...), custom_call_target="tpu_custom_call" | custom-call | tf_op jit(solution)/shard_map/pallas_call | solution.py:89
  11.0 3.7 %collective-permute-start = (bf16[2,2,7,7,384]{4,1,3,2,0:T(2,128)(2,1)S(1)}, bf16[2,2,7,7,384]{4,1,3,2,0:T(2,128)(2,1)S(1)}, u32[]{:S(2)}, u32[]{:S(2)}) collective-permute-start(bf16[2,2,7,7,384]{4,1,3,2,0:T(2,128)(2,1)S(1)} %get-tuple-element.83), channel_id=1, source_target_pairs={{64,0},{0,64},{65,1},{1,65},{66,2},{2,66},{67,3},{3,67},{68,4},{4,... | collective-permute-start | bytes 451592 | tf_op jit(solution)/shard_map/ppermute | solution.py:564
  14.6 3.2 %collective-permute-done = bf16[2,2,7,7,384]{4,1,3,2,0:T(2,128)(2,1)S(1)} collective-permute-done((bf16[2,2,7,7,384]{4,1,3,2,0:T(2,128)(2,1)S(1)}, bf16[2,2,7,7,384]{4,1,3,2,0:T(2,128)(2,1)S(1)}, u32[]{:S(2)}, u32[]{:S(2)}) %collective-permute-start) | collective-permute-done | bytes 150560 | tf_op jit(solution)/shard_map/ppermute | solution.py:564
  17.9 4.3 %collective-permute-start.1 = (bf16[2,4,3,7,384]{4,1,3,2,0:T(4,128)(2,1)S(1)}, bf16[2,4,3,7,384]{4,1,3,2,0:T(4,128)(2,1)S(1)}, u32[]{:S(2)}, u32[]{:S(2)}) collective-permute-start(bf16[2,4,3,7,384]{4,1,3,2,0:T(4,128)(2,1)S(1)} %pad_maximum_fusion.4), channel_id=1, source_target_pairs={{8,0},{16,8},{24,16},{32,24},{40,32},{48,40},{56,48},{0,56},{9,1},... | collective-permute-start | bytes 387080 | tf_op jit(solution)/shard_map/ppermute | solution.py:564
  22.4 1.7 %collective-permute-done.1 = bf16[2,4,3,7,384]{4,1,3,2,0:T(4,128)(2,1)S(1)} collective-permute-done((bf16[2,4,3,7,384]{4,1,3,2,0:T(4,128)(2,1)S(1)}, bf16[2,4,3,7,384]{4,1,3,2,0:T(4,128)(2,1)S(1)}, u32[]{:S(2)}, u32[]{:S(2)}) %collective-permute-start.1) | collective-permute-done | bytes 129056 | tf_op jit(solution)/shard_map/ppermute | solution.py:564
  24.2 2.4 %collective-permute-start.2 = (bf16[2,4,7,3,384]{4,1,3,2,0:T(4,128)(2,1)S(1)}, bf16[2,4,7,3,384]{4,1,3,2,0:T(4,128)(2,1)S(1)}, u32[]{:S(2)}, u32[]{:S(2)}) collective-permute-start(bf16[2,4,7,3,384]{4,1,3,2,0:T(4,128)(2,1)S(1)} %pad_maximum_fusion.3), channel_id=1, source_target_pairs={{1,0},{2,1},{3,2},{4,3},{5,4},{6,5},{7,6},{0,7},{9,8},{10,9},{11,1... | collective-permute-start | bytes 387080 | tf_op jit(solution)/shard_map/ppermute | solution.py:564
  26.7 4.0 %collective-permute-done.2 = bf16[2,4,7,3,384]{4,1,3,2,0:T(4,128)(2,1)S(1)} collective-permute-done((bf16[2,4,7,3,384]{4,1,3,2,0:T(4,128)(2,1)S(1)}, bf16[2,4,7,3,384]{4,1,3,2,0:T(4,128)(2,1)S(1)}, u32[]{:S(2)}, u32[]{:S(2)}) %collective-permute-start.2) | collective-permute-done | bytes 129056 | tf_op jit(solution)/shard_map/ppermute | solution.py:564
  31.2 12.3 %shard_map.204 = (bf16[224,384]{1,0:T(8,128)(2,1)}, bf16[224,384]{1,0:T(8,128)(2,1)}, bf16[224,384]{1,0:T(8,128)(2,1)}, bf16[224,1536]{1,0:T(8,128)(2,1)}, bf16[...) custom-call(bf16[224,384]{1,0:T(8,128)(2,1)S(1)} %bitcast.28, ...), custom_call_target="tpu_custom_call" | custom-call | tf_op jit(solution)/shard_map/pallas_call | solution.py:89
  43.5 2.5 %collective-permute-start.3 = (bf16[2,7,7,384]{3,2,1,0:T(8,128)(2,1)S(1)}, bf16[2,7,7,384]{3,2,1,0:T(8,128)(2,1)S(1)}, u32[]{:S(2)}, u32[]{:S(2)}) collective-permute-start(bf16[2,7,7,384]{3,2,1,0:T(8,128)(2,1)S(1)} %get-tuple-element.86), channel_id=1, source_target_pairs={{64,0},{0,64},{65,1},{1,65},{66,2},{2,66},{67,3},{3,67},{68,4},{4,... | collective-permute-start | bytes 225800 | tf_op jit(solution)/shard_map/ppermute | solution.py:564
  46.0 3.2 %collective-permute-done.3 = bf16[2,7,7,384]{3,2,1,0:T(8,128)(2,1)S(1)} collective-permute-done((bf16[2,7,7,384]{3,2,1,0:T(8,128)(2,1)S(1)}, bf16[2,7,7,384]{3,2,1,0:T(8,128)(2,1)S(1)}, u32[]{:S(2)}, u32[]{:S(2)}) %collective-permute-start.3) | collective-permute-done | bytes 75296 | tf_op jit(solution)/shard_map/ppermute | solution.py:564
  49.2 1.1 collective-permute-start.4
  50.4 9.9 %shard_map.205 = (bf16[7168,128]{1,0:T(8,128)(2,1)}, bf16[7168,128]{1,0:T(8,128)(2,1)}, bf16[224,384]{1,0:T(8,128)(2,1)S(1)}) custom-call(s32[1]{0:T(128)} %bitcast.refs_0_, bf16[224,384]{1,0:T(8,128)(2,1)S(1)} %bitcast.24, bf16[224,384]{1,0:T(8,128)(2,1)S(1)} %bitcast.27, bf16[224,384]{1,0:T(8,128)(2,1)} %get-tuple-element.47.refs_3_, ...), custom_call_target="tpu_custom_call" | custom-call | tf_op jit(solution)/shard_map/pallas_call | solution.py:89
  60.8 1.5 collective-permute-done.5
  62.5 14.5 %shard_map.206 = (bf16[224,384]{1,0:T(8,128)(2,1)S(1)}, bf16[7168,128]{1,0:T(8,128)(2,1)}, bf16[7168,128]{1,0:T(8,128)(2,1)}, bf16[7168,128]{1,0:T(8,128)(2,1)}) custom-call(s32[1]{0:T(128)} %bitcast.refs_0_, bf16[224,384]{1,0:T(8,128)(2,1)S(1)} %bitcast.29, bf16[224,384]{1,0:T(8,128)(2,1)S(1)} %bitcast.26, ...), custom_call_target="tpu_custom_call", output_to_operand_aliasing={{3}: (15, {})} | custom-call | tf_op jit(solution)/shard_map/pallas_call | solution.py:89
  77.0 4.3 %collective-permute-start.6 = (bf16[7168,128]{1,0:T(8,128)(2,1)}, bf16[7168,128]{1,0:T(8,128)(2,1)S(1)}, u32[]{:S(2)}, u32[]{:S(2)}) collective-permute-start(bf16[7168,128]{1,0:T(8,128)(2,1)} %get-tuple-element.68), channel_id=1, source_target_pairs={{0,1},{1,0},{2,3},{3,2},{4,5},{5,4},{6,7},{7,6},{8,9},{9,8},{10,11... | collective-permute-start | bytes 5505032 | tf_op jit(solution)/shard_map/ppermute | solution.py:597
  81.3 3.5 %collective-permute-done.6.refs_2_ = bf16[7168,128]{1,0:T(8,128)(2,1)S(1)} collective-permute-done((bf16[7168,128]{1,0:T(8,128)(2,1)}, bf16[7168,128]{1,0:T(8,128)(2,1)S(1)}, u32[]{:S(2)}, u32[]{:S(2)}) %collective-permute-start.6) | collective-permute-done | bytes 1835040 | tf_op jit(solution)/shard_map/ppermute | solution.py:597
  84.8 2.6 %collective-permute-done.7.refs_3_ = bf16[7168,128]{1,0:T(8,128)(2,1)S(1)} collective-permute-done((bf16[7168,128]{1,0:T(8,128)(2,1)}, bf16[7168,128]{1,0:T(8,128)(2,1)S(1)}, u32[]{:S(2)}, u32[]{:S(2)}) %collective-permute-start.7) | collective-permute-done | bytes 1835040 | tf_op jit(solution)/shard_map/ppermute | solution.py:597
  87.5 3.7 %shard_map.207 = bf16[14336,128]{1,0:T(8,128)(2,1)} custom-call(bf16[7168,128]{1,0:T(8,128)(2,1)} %get-tuple-element.66.refs_0_, bf16[7168,128]{1,0:T(8,128)(2,1)} %get-tuple-element.67.refs_1_, bf16[7168,128]{1,0:T(8,128)(2,1)S(1)} %collective-permute-done.6.refs_2_, bf16[7168,128]{1,0:T(8,128)(2,1)S(1)} %collective-permute-done.7.refs_3_), custom_call_target="tpu_custom_call" | custom-call | tf_op jit(solution)/shard_map/pallas_call | solution.py:89
  91.2 55.2 %all_to_all.10.refs_0_ = bf16[64,224,128]{2,1,0:T(8,128)(2,1)} all-to-all(bf16[64,224,128]{2,1,0:T(8,128)(2,1)} %bitcast.34), channel_id=1, replica_groups={{0,2,4,6,8,10,12,14,16,18,20,22,24,26,28,30,32,34,36,38,40,42,44,46,48,..., dimensions={0} | all-to-all | bytes 7340032 | tf_op jit(solution)/shard_map/all_to_all | solution.py:602
  146.4 3.0 %shard_map.208 = (f32[3,1152]{1,0:T(4,128)}, f32[3,384]{1,0:T(4,128)}, f32[3,1536]{1,0:T(4,128)}, f32[12,384]{1,0:T(8,128)}, f32[3,1152]{1,0:T(4,128)}, /*index=...) custom-call(bf16[64,224,128]{2,1,0:T(8,128)(2,1)} %all_to_all.10.refs_0_), custom_call_target="tpu_custom_call" | custom-call | tf_op jit(solution)/shard_map/pallas_call | solution.py:89
  149.4 6.8 %all-to-all-start.1 = ((f32[128,2,128]{2,1,0:T(2,128)}), f32[128,2,128]{2,1,0:T(2,128)S(1)}, u32[]{:S(2)}, u32[]{:S(2)}) async-start(f32[128,2,128]{2,1,0:T(2,128)} %get-tuple-element.72), calls=%async_computation.1 | async-start | bytes 262144 | tf_op jit(solution)/shard_map/all_to_all | solution.py:634
  157.0 9.5 %all-to-all-done.1 = f32[128,2,128]{2,1,0:T(2,128)S(1)} async-done(((f32[128,2,128]{2,1,0:T(2,128)}), f32[128,2,128]{2,1,0:T(2,128)S(1)}, u32[]{:S(2)}, u32[]{:S(2)}) %all-to-all-start.1) | async-done | bytes 131104 | tf_op jit(solution)/shard_map/all_to_all | solution.py:634
  (31 shorter events, 4.4 us)
Async XLA Ops:
  1.6 0.9 copy-start.1
  2.5 8.2 %copy-start.2 = (bf16[4,7,7,384]{3,0,2,1:T(4,128)(2,1)S(1)}, bf16[4,7,7,384]{3,0,2,1:T(4,128)(2,1)}, u32[]{:S(2)}) copy-start(bf16[4,7,7,384]{3,0,2,1:T(4,128)(2,1)} %param.13) | copy-start | bytes 451588
  11.0 6.8 %collective-permute-start = (bf16[2,2,7,7,384]{4,1,3,2,0:T(2,128)(2,1)S(1)}, bf16[2,2,7,7,384]{4,1,3,2,0:T(2,128)(2,1)S(1)}, u32[]{:S(2)}, u32[]{:S(2)}) collective-permute-start(bf16[2,2,7,7,384]{4,1,3,2,0:T(2,128)(2,1)S(1)} %get-tuple-element.83), channel_id=1, source_target_pairs={{64,0},{0,64},{65,1},{1,65},{66,2},{2,66},{67,3},{3,67},{68,4},{4,... | collective-permute-start | bytes 451592 | tf_op jit(solution)/shard_map/ppermute | solution.py:564
  17.8 13.4 %copy-start = (f32[12,1183]{1,0:T(8,128)S(1)}, f32[12,1183]{1,0:T(8,128)}, u32[]{:S(2)}) copy-start(f32[12,1183]{1,0:T(8,128)} %refs_2_.3) | copy-start | bytes 170356
  17.9 6.2 %collective-permute-start.1 = (bf16[2,4,3,7,384]{4,1,3,2,0:T(4,128)(2,1)S(1)}, bf16[2,4,3,7,384]{4,1,3,2,0:T(4,128)(2,1)S(1)}, u32[]{:S(2)}, u32[]{:S(2)}) collective-permute-start(bf16[2,4,3,7,384]{4,1,3,2,0:T(4,128)(2,1)S(1)} %pad_maximum_fusion.4), channel_id=1, source_target_pairs={{8,0},{16,8},{24,16},{32,24},{40,32},{48,40},{56,48},{0,56},{9,1},... | collective-permute-start | bytes 387080 | tf_op jit(solution)/shard_map/ppermute | solution.py:564
  24.2 6.6 %collective-permute-start.2 = (bf16[2,4,7,3,384]{4,1,3,2,0:T(4,128)(2,1)S(1)}, bf16[2,4,7,3,384]{4,1,3,2,0:T(4,128)(2,1)S(1)}, u32[]{:S(2)}, u32[]{:S(2)}) collective-permute-start(bf16[2,4,7,3,384]{4,1,3,2,0:T(4,128)(2,1)S(1)} %pad_maximum_fusion.3), channel_id=1, source_target_pairs={{1,0},{2,1},{3,2},{4,3},{5,4},{6,5},{7,6},{0,7},{9,8},{10,9},{11,1... | collective-permute-start | bytes 387080 | tf_op jit(solution)/shard_map/ppermute | solution.py:564
  43.5 5.7 %collective-permute-start.3 = (bf16[2,7,7,384]{3,2,1,0:T(8,128)(2,1)S(1)}, bf16[2,7,7,384]{3,2,1,0:T(8,128)(2,1)S(1)}, u32[]{:S(2)}, u32[]{:S(2)}) collective-permute-start(bf16[2,7,7,384]{3,2,1,0:T(8,128)(2,1)S(1)} %get-tuple-element.86), channel_id=1, source_target_pairs={{64,0},{0,64},{65,1},{1,65},{66,2},{2,66},{67,3},{3,67},{68,4},{4,... | collective-permute-start | bytes 225800 | tf_op jit(solution)/shard_map/ppermute | solution.py:564
  49.2 11.1 %collective-permute-start.4 = (bf16[4,3,7,384]{3,2,1,0:T(8,128)(2,1)S(1)}, bf16[4,3,7,384]{3,2,1,0:T(8,128)(2,1)S(1)}, u32[]{:S(2)}, u32[]{:S(2)}) collective-permute-start(bf16[4,3,7,384]{3,2,1,0:T(8,128)(2,1)S(1)} %fusion.12), channel_id=1, source_target_pairs={{56,0},{0,8},{8,16},{16,24},{24,32},{32,40},{40,48},{48,56},{57,1}... | collective-permute-start | bytes 193544 | tf_op jit(solution)/shard_map/ppermute | solution.py:564
  60.4 1.9 %collective-permute-start.5 = (bf16[4,7,3,384]{3,2,1,0:T(4,128)(2,1)S(1)}, bf16[4,7,3,384]{3,2,1,0:T(4,128)(2,1)S(1)}, u32[]{:S(2)}, u32[]{:S(2)}) collective-permute-start(bf16[4,7,3,384]{3,2,1,0:T(4,128)(2,1)S(1)} %fusion.11), channel_id=1, source_target_pairs={{7,0},{0,1},{1,2},{2,3},{3,4},{4,5},{5,6},{6,7},{15,8},{8,9},{9,10... | collective-permute-start | bytes 193544 | tf_op jit(solution)/shard_map/ppermute | solution.py:564
  77.0 7.9 %collective-permute-start.6 = (bf16[7168,128]{1,0:T(8,128)(2,1)}, bf16[7168,128]{1,0:T(8,128)(2,1)S(1)}, u32[]{:S(2)}, u32[]{:S(2)}) collective-permute-start(bf16[7168,128]{1,0:T(8,128)(2,1)} %get-tuple-element.68), channel_id=1, source_target_pairs={{0,1},{1,0},{2,3},{3,2},{4,5},{5,4},{6,7},{7,6},{8,9},{9,8},{10,11... | collective-permute-start | bytes 5505032 | tf_op jit(solution)/shard_map/ppermute | solution.py:597
  81.2 6.2 %collective-permute-start.7 = (bf16[7168,128]{1,0:T(8,128)(2,1)}, bf16[7168,128]{1,0:T(8,128)(2,1)S(1)}, u32[]{:S(2)}, u32[]{:S(2)}) collective-permute-start(bf16[7168,128]{1,0:T(8,128)(2,1)} %get-tuple-element.69), channel_id=1, source_target_pairs={{0,1},{1,0},{2,3},{3,2},{4,5},{5,4},{6,7},{7,6},{8,9},{9,8},{10,11... | collective-permute-start | bytes 5505032 | tf_op jit(solution)/shard_map/ppermute | solution.py:597
  149.4 17.1 %all-to-all-start.1 = ((f32[128,2,128]{2,1,0:T(2,128)}), f32[128,2,128]{2,1,0:T(2,128)S(1)}, u32[]{:S(2)}, u32[]{:S(2)}) async-start(f32[128,2,128]{2,1,0:T(2,128)} %get-tuple-element.72), calls=%async_computation.1 | async-start | bytes 262144 | tf_op jit(solution)/shard_map/all_to_all | solution.py:634

commit v4 on v3

--- a/solution.py
+++ b/solution.py
@@ -176,7 +176,7 @@
     for hj in range(WH):
         dy = jnp.zeros((HEADS * 8, 392), f32)
         for tj in range(WT):
-            z = ds_ref[:, tj * 56 + hj * 8 : tj * 56 + hj * 8 + 8, :].astype(f32).reshape(HEADS * 8, ROWS)
+            z = ds_ref[:, tj * 56 + hj * 8 : tj * 56 + hj * 8 + 8, :].reshape(HEADS * 8, ROWS)
             parts = []
             if tj < 3:
                 parts.append(jnp.zeros((HEADS * 8, (3 - tj) * 56), f32))
@@ -281,7 +281,7 @@
 
 
 def attention_and_feed(m, x):
-    m.need("wqkv")
+    m.need("table", "wqkv")
     build_bias(m.table, m.bias, m.wide)
     norm_into(x, m.n1)
     attention_forward(m.n1, m.wqkv, m.bias, m.qkv, m.p, m.turned, m.ctx)
@@ -349,7 +349,7 @@
 def first_backward(m):
     backward(m, m.x, m.gy, m.dx)
     m.need("n1", "ctx", "n2", "act")
-    weight_sums(m)
+    weight_sums(m, m.ds)
 
 
 def picker(per):
@@ -366,10 +366,12 @@
 def weights_kernel(m):
     m.passed[...] = m.carried[...]
     m.need("n1", "dqkv", "ctx", "dh", "n2", "de", "act", "ds")
-    weight_sums(m)
-
-
-def weight_sums(m):
+    for h in range(HEADS):
+        m.wide[h] = m.ds[h].astype(f32)
+    weight_sums(m, m.wide)
+
+
+def weight_sums(m, ds):
     f_ref = m.f
     pick = picker(3)
 
@@ -390,7 +392,7 @@
     pick = picker(12)
     for b in range(4):
         place(72, m.act[:, b * D : b * D + D], m.gy, pick, 12, b * 32)
-    lines = unsheared(table_pull(m.ds))
+    lines = unsheared(table_pull(ds))
     zero = jnp.zeros((128, 128), f32)
     for j in range(108, CHUNK):
         f_ref[pl.ds(j, 128, stride=CHUNK), :] = zero
@@ -428,7 +430,7 @@
 def run_first_forward(x, table, weights):
     return launch(
         first_forward,
-        {"x": (x, "near"), "table": (table, "near")} | weights,
+        {"x": (x, "near"), "table": (table, "far")} | weights,
         {
             "n1": rows(D, "far"), "qkv": rows(3 * D, "far"), "p": (SQUARE, bf16, "far"), "ctx": rows(D, "far"),
             "h": rows(D, "far"), "n2": rows(D, "far"), "act": rows(FF, "far"), "slope": rows(FF, "far"),
@@ -465,8 +467,9 @@
 def run_first_backward(mine, gy, x, kept, weights, give_two):
     return launch(
         first_backward,
-        {"mine": (mine, "flag"), "gy": (gy, "near"), "x": (x, "near"), "wc": weights["wc"]}
-        | {"slope": (kept["slope"], "far"), "we": weights["we"], "h": (kept["h"], "far"), "wp": weights["wp"]}
+        {"mine": (mine, "flag"), "gy": (gy, "near"), "x": (x, "near"), "wc": (weights["wc"][0], "near")}
+        | {"slope": (kept["slope"], "near"), "we": (weights["we"][0], "near"), "h": (kept["h"], "near")}
+        | {"wp": weights["wp"]}
         | {"qkv": (kept["qkv"], "far"), "p": (kept["p"], "far"), "wqkv": weights["wqkv"]}
         | {name: (kept[name], "far") for name in ("n1", "ctx", "n2", "act")}
         | {"give_two": (give_two, "pass")},
@@ -474,7 +477,7 @@
         {
             "turned": scr((D, ROWS), f32), "dctx": scr((ROWS, D), bf16), "big": scr((ROWS, D), f32),
             "dqkv": scr((ROWS, 3 * D), bf16), "dh": scr((ROWS, D), bf16), "de": scr((ROWS, FF), bf16),
-            "ds": scr(SQUARE, bf16), "f": scr((128 * CHUNK, 128), f32),
+            "ds": scr(SQUARE, f32), "f": scr((128 * CHUNK, 128), f32),
         },
     )
 
@@ -485,7 +488,7 @@
         {"mine": (mine, "flag"), "gy": (gy, "near"), "carried": (carried, "near")}
         | {name: (sums[name], "far") for name in ("n1", "ctx", "n2", "act", "dqkv", "dh", "de", "ds")},
         {"keep": HALF, "give": HALF, "passed": (carried.shape, carried.dtype, "near")},
-        {"f": scr((128 * CHUNK, 128), f32)},
+        {"f": scr((128 * CHUNK, 128), f32), "wide": scr(SQUARE, f32)},
     )
 
 
@@ -585,6 +588,34 @@
     return rejoin(grid, at, width, direction, moved)
 
 
+def rolled_twice(grid, direction):
+    first = grid.ndim - 4
+    sizes = [lax.axis_size(axis) for axis in AXES[:2]]
+    parts = {}
+    for bt in range(2):
+        for bh in range(2):
+            part = grid
+            for at, width, moves in ((first, WT // 2, bt), (first + 1, WH // 2, bh)):
+                extent = part.shape[at]
+                if moves:
+                    part = edge_of(part, at, width, direction)
+                elif direction < 0:
+                    part = lax.slice_in_dim(part, width, extent, axis=at)
+                else:
+                    part = lax.slice_in_dim(part, 0, extent - width, axis=at)
+            if bt or bh:
+                route = [
+                    (t * sizes[1] + h, (t + bt * direction) % sizes[0] * sizes[1] + (h + bh * direction) % sizes[1])
+                    for t in range(sizes[0])
+                    for h in range(sizes[1])
+                ]
+                part = lax.ppermute(part, AXES[:2], route)
+            parts[bt, bh] = part
+    order = (0, 1) if direction < 0 else (1, 0)
+    halves = [jnp.concatenate([parts[bt, bh] for bh in order], axis=first + 1) for bt in order]
+    return jnp.concatenate(halves, axis=first)
+
+
 def to_rows(grid):
     return jnp.pad(grid, ((0, 0), (0, 0), (0, 1), (0, 0))).reshape(ROWS, D)
 
@@ -616,15 +647,13 @@
     weights_two = far(qkv_two, proj_two, expand_two, contract_two)
     one = run_first_forward(x, table_one, weights_one)
     both = jnp.stack([to_grid(one["y"]), upstream])
-    for dim in range(3):
-        both = rolled_along(both, dim, -1)
+    both = rolled_along(rolled_twice(both, -1), 2, -1)
     rolled, up = to_rows(both[0]), to_rows(both[1])
-    two = run_second(rolled, up, table_two, weights_two)
-    gy = rolled_along(to_grid(two["gy"]), 0, 1)
-    sent = passed_along(edge_of(gy, 1, WH // 2, 1), AXES[1], 1)
+    two = run_second(rolled, up, table_two, {name: (w, "near") for name, (w, _) in weights_two.items()})
+    gy = rolled_twice(to_grid(two["gy"]), 1)
+    sent = passed_along(edge_of(gy, 2, WW // 2, 1), AXES[2], 1)
     sums_two = run_weights(mine, two, up, to_rows(gy))
-    gy = rejoin(to_grid(sums_two["passed"]), 1, WH // 2, 1, sent)
-    gy = to_rows(rolled_along(gy, 2, 1))
+    gy = to_rows(rejoin(to_grid(sums_two["passed"]), 2, WW // 2, 1, sent))
     sums_one = run_first_backward(mine, gy, x, one, weights_one, sums_two["give"])
     dx = sums_one["dx"]
     spread = exchanged(

time: 168 us -> 158 us (0.940)
  starting transfers between devices: 25.5 us -> 19.9 us
  Pallas kernels: 51.5 us -> 49.4 us
    ppermute x6 -> x2, starting transfers between devices: 14.3 us -> 3.69 us  [passed_along(): return lax.ppermute(block, axis, route)]
    ppermute x6 -> x2, waiting for transfers between devices: 13.6 us -> 3.77 us  [passed_along(): return lax.ppermute(block, axis, route)]
    ppermute x0 -> x6, waiting for transfers between devices: none -> 9.15 us  [rolled_twice(): part = lax.ppermute(part, AXES[:2], route)]
    ppermute x0 -> x6, starting transfers between devices: none -> 8.58 us  [rolled_twice(): part = lax.ppermute(part, AXES[:2], route)]
    ppermute x2, starting transfers between devices: 4.35 us -> 0.75 us  [swapped(): lax.ppermute(block, 'wa', [(i, i ^ 1) for i in range(lax.axis_size('wa'))])]
    pallas_call x6, Pallas kernels: 51.5 us -> 49.4 us  [launch(): pl.pallas_call(wrapped, out_shape=[pltpu.HBM(shape, dtype) if space in ('...]
  transfers between devices with their start and end apart: 9 -> 11, of which waited for: 8 -> 7; matrix products, arithmetic and copies ran while one was open for 1% -> 1% of each run, Pallas kernels for 6% -> 6%
where the time goes in v4:
time: 158 us; the launch traced here: 157 us
  blocking collectives  53.6 us (34%)
  Pallas kernels  49.4 us (31%)
  waiting for transfers between devices  28.6 us (18%)
  starting transfers between devices  19.9 us (13%)
  local copies, waits for them, and re-layouts  3.73 us (2%)
    all_to_all x1, blocking collectives, exchanged(): lax.all_to_all(both, AXES, 0, 0, axis_index_groups=groups, tiled=True)  53.6 us
    pallas_call x6, Pallas kernels, launch(): pl.pallas_call(wrapped, out_shape=[pltpu.HBM(shape, dtype) if space in ('...  49.4 us
    all_to_all x1, waiting for transfers between devices, body(): tables = lax.all_to_all(done['lines'], AXES, 0, 0, tiled=True)  9.5 us
    ppermute x6, waiting for transfers between devices, rolled_twice(): part = lax.ppermute(part, AXES[:2], route)  9.15 us
    ppermute x6, starting transfers between devices, rolled_twice(): part = lax.ppermute(part, AXES[:2], route)  8.58 us
    all_to_all x1, starting transfers between devices, body(): tables = lax.all_to_all(done['lines'], AXES, 0, 0, tiled=True)  6.9 us
    ppermute x2, waiting for transfers between devices, swapped(): lax.ppermute(block, 'wa', [(i, i ^ 1) for i in range(lax.axis_size('wa'))])  6.15 us
    ppermute x2, waiting for transfers between devices, passed_along(): return lax.ppermute(block, axis, route)  3.77 us
  transfers between devices with their start and end apart: 11, of which 7 were waited for; matrix products, arithmetic and copies ran while one was open for 1% of the time, Pallas kernels for 6%

profile of v4, /device:TPU:1, one launch (start us, length us, event | category | flops | bytes accessed | tf_op | source)
XLA Modules:
  0.0 157.4 jit_solution(9734834529864869812)
XLA Ops:
  0.6 0.9 copy.31
  1.6 8.2 %shard_map.203 = (bf16[224,384]{1,0:T(8,128)(2,1)}, bf16[224,1152]{1,0:T(8,128)(2,1)}, bf16[12,224,224]{2,1,0:T(8,128)(2,1)}, bf16[224,384]{1,0:T(8,128)(2,1)}, ...) custom-call(bf16[224,384]{1,0:T(8,128)(2,1)S(1)} %bitcast.25, ...), custom_call_target="tpu_custom_call" | custom-call | tf_op jit(solution)/shard_map/pallas_call | solution.py:89
  10.2 3.7 %collective-permute-start.1 = (bf16[2,2,4,7,384]{4,1,3,2,0:T(2,128)(2,1)S(1)}, bf16[2,2,4,7,384]{4,1,3,2,0:T(2,128)(2,1)S(1)}, u32[]{:S(2)}, u32[]{:S(2)}) collective-permute-start(bf16[2,2,4,7,384]{4,1,3,2,0:T(2,128)(2,1)S(1)} %get-tuple-element.84), channel_id=1, source_target_pairs={{0,64},{8,72},{16,80},{24,88},{32,96},{40,104},{48,112},{56,120},{... | collective-permute-start | bytes 258056 | tf_op jit(solution)/shard_map/ppermute | solution.py:612
  14.0 2.8 %collective-permute-start = (bf16[2,2,3,7,384]{4,1,3,2,0:T(2,128)(2,1)S(1)}, bf16[2,2,3,7,384]{4,1,3,2,0:T(2,128)(2,1)S(1)}, u32[]{:S(2)}, u32[]{:S(2)}) collective-permute-start(bf16[2,2,3,7,384]{4,1,3,2,0:T(2,128)(2,1)S(1)} %get-tuple-element.85), channel_id=1, source_target_pairs={{0,56},{8,0},{16,8},{24,16},{32,24},{40,32},{48,40},{56,48},{64,12... | collective-permute-start | bytes 193544 | tf_op jit(solution)/shard_map/ppermute | solution.py:612
  16.8 0.8 collective-permute-start.2
  18.1 3.0 %collective-permute-done.2 = bf16[2,2,3,7,384]{4,1,3,2,0:T(2,128)(2,1)S(1)} collective-permute-done((bf16[2,2,3,7,384]{4,1,3,2,0:T(2,128)(2,1)S(1)}, bf16[2,2,3,7,384]{4,1,3,2,0:T(2,128)(2,1)S(1)}, u32[]{:S(2)}, u32[]{:S(2)}) %collective-permute-start.2) | collective-permute-done | bytes 64544 | tf_op jit(solution)/shard_map/ppermute | solution.py:612
  21.2 2.4 %collective-permute-start.3 = (bf16[2,4,7,3,384]{4,1,3,2,0:T(4,128)(2,1)S(1)}, bf16[2,4,7,3,384]{4,1,3,2,0:T(4,128)(2,1)S(1)}, u32[]{:S(2)}, u32[]{:S(2)}) collective-permute-start(bf16[2,4,7,3,384]{4,1,3,2,0:T(4,128)(2,1)S(1)} %maximum_maximum_fusion.2), channel_id=1, source_target_pairs={{1,0},{2,1},{3,2},{4,3},{5,4},{6,5},{7,6},{0,7},{9,8},{10,9},{11,1... | collective-permute-start | bytes 387080 | tf_op jit(solution)/shard_map/ppermute | solution.py:567
  24.0 3.8 %collective-permute-done.3 = bf16[2,4,7,3,384]{4,1,3,2,0:T(4,128)(2,1)S(1)} collective-permute-done((bf16[2,4,7,3,384]{4,1,3,2,0:T(4,128)(2,1)S(1)}, bf16[2,4,7,3,384]{4,1,3,2,0:T(4,128)(2,1)S(1)}, u32[]{:S(2)}, u32[]{:S(2)}) %collective-permute-start.3) | collective-permute-done | bytes 129056 | tf_op jit(solution)/shard_map/ppermute | solution.py:567
  28.2 11.4 %shard_map.204 = (bf16[224,384]{1,0:T(8,128)(2,1)}, bf16[224,384]{1,0:T(8,128)(2,1)}, bf16[224,384]{1,0:T(8,128)(2,1)}, bf16[224,1536]{1,0:T(8,128)(2,1)}, bf16[...) custom-call(bf16[224,384]{1,0:T(8,128)(2,1)S(1)} %bitcast.27, ...), custom_call_target="tpu_custom_call" | custom-call | tf_op jit(solution)/shard_map/pallas_call | solution.py:89
  40.2 0.7 collective-permute-start.4
  40.9 5.7 %collective-permute-done.4 = bf16[2,3,7,384]{3,2,1,0:T(8,128)(2,1)S(1)} collective-permute-done((bf16[2,3,7,384]{3,2,1,0:T(8,128)(2,1)S(1)}, bf16[2,3,7,384]{3,2,1,0:T(8,128)(2,1)S(1)}, u32[]{:S(2)}, u32[]{:S(2)}) %collective-permute-start.4) | collective-permute-done | bytes 32288 | tf_op jit(solution)/shard_map/ppermute | solution.py:612
  46.7 1.3 collective-permute-start.7
  48.1 10.1 %shard_map.205 = (bf16[7168,128]{1,0:T(8,128)(2,1)}, bf16[7168,128]{1,0:T(8,128)(2,1)}, bf16[224,384]{1,0:T(8,128)(2,1)S(1)}) custom-call(s32[1]{0:T(128)} %bitcast.refs_0_, bf16[224,384]{1,0:T(8,128)(2,1)S(1)} %bitcast.24, bf16[224,384]{1,0:T(8,128)(2,1)S(1)} %bitcast.28, bf16[224,384]{1,0:T(8,128)(2,1)} %get-tuple-element.47.refs_3_, ...), custom_call_target="tpu_custom_call" | custom-call | tf_op jit(solution)/shard_map/pallas_call | solution.py:89
  58.3 13.1 %shard_map.206 = (bf16[224,384]{1,0:T(8,128)(2,1)S(1)}, bf16[7168,128]{1,0:T(8,128)(2,1)}, bf16[7168,128]{1,0:T(8,128)(2,1)}, bf16[7168,128]{1,0:T(8,128)(2,1)}) custom-call(s32[1]{0:T(128)} %bitcast.refs_0_, bf16[224,384]{1,0:T(8,128)(2,1)S(1)} %bitcast.29, bf16[224,384]{1,0:T(8,128)(2,1)S(1)} %bitcast.26, ...), custom_call_target="tpu_custom_call", output_to_operand_aliasing={{3}: (15, {})} | custom-call | tf_op jit(solution)/shard_map/pallas_call | solution.py:89
  71.4 0.7 collective-permute-start.8
  72.1 3.5 %collective-permute-done.8.refs_2_ = bf16[7168,128]{1,0:T(8,128)(2,1)S(1)} collective-permute-done((bf16[7168,128]{1,0:T(8,128)(2,1)}, bf16[7168,128]{1,0:T(8,128)(2,1)S(1)}, u32[]{:S(2)}, u32[]{:S(2)}) %collective-permute-start.8) | collective-permute-done | bytes 1835040 | tf_op jit(solution)/shard_map/ppermute | solution.py:628
  75.7 2.6 %collective-permute-done.9.refs_3_ = bf16[7168,128]{1,0:T(8,128)(2,1)S(1)} collective-permute-done((bf16[7168,128]{1,0:T(8,128)(2,1)}, bf16[7168,128]{1,0:T(8,128)(2,1)S(1)}, u32[]{:S(2)}, u32[]{:S(2)}) %collective-permute-start.9) | collective-permute-done | bytes 1835040 | tf_op jit(solution)/shard_map/ppermute | solution.py:628
  78.3 3.7 %shard_map.207 = bf16[14336,128]{1,0:T(8,128)(2,1)} custom-call(bf16[7168,128]{1,0:T(8,128)(2,1)} %get-tuple-element.66.refs_0_, bf16[7168,128]{1,0:T(8,128)(2,1)} %get-tuple-element.67.refs_1_, bf16[7168,128]{1,0:T(8,128)(2,1)S(1)} %collective-permute-done.8.refs_2_, bf16[7168,128]{1,0:T(8,128)(2,1)S(1)} %collective-permute-done.9.refs_3_), custom_call_target="tpu_custom_call" | custom-call | tf_op jit(solution)/shard_map/pallas_call | solution.py:89
  82.0 53.6 %all_to_all.10.refs_0_ = bf16[64,224,128]{2,1,0:T(8,128)(2,1)} all-to-all(bf16[64,224,128]{2,1,0:T(8,128)(2,1)} %bitcast.35), channel_id=1, replica_groups={{0,2,4,6,8,10,12,14,16,18,20,22,24,26,28,30,32,34,36,38,40,42,44,46,48,..., dimensions={0} | all-to-all | bytes 7340032 | tf_op jit(solution)/shard_map/all_to_all | solution.py:633
  135.7 3.0 %shard_map.208 = (f32[3,1152]{1,0:T(4,128)}, f32[3,384]{1,0:T(4,128)}, f32[3,1536]{1,0:T(4,128)}, f32[12,384]{1,0:T(8,128)}, f32[3,1152]{1,0:T(4,128)}, /*index=...) custom-call(bf16[64,224,128]{2,1,0:T(8,128)(2,1)} %all_to_all.10.refs_0_), custom_call_target="tpu_custom_call" | custom-call | tf_op jit(solution)/shard_map/pallas_call | solution.py:89
  138.7 6.9 %all-to-all-start.1 = ((f32[128,2,128]{2,1,0:T(2,128)}), f32[128,2,128]{2,1,0:T(2,128)S(1)}, u32[]{:S(2)}, u32[]{:S(2)}) async-start(f32[128,2,128]{2,1,0:T(2,128)} %get-tuple-element.72), calls=%async_computation.1 | async-start | bytes 262144 | tf_op jit(solution)/shard_map/all_to_all | solution.py:663
  145.6 0.7 copy.30
  146.3 9.5 %all-to-all-done.1 = f32[128,2,128]{2,1,0:T(2,128)S(1)} async-done(((f32[128,2,128]{2,1,0:T(2,128)}), f32[128,2,128]{2,1,0:T(2,128)S(1)}, u32[]{:S(2)}, u32[]{:S(2)}) %all-to-all-start.1) | async-done | bytes 131104 | tf_op jit(solution)/shard_map/all_to_all | solution.py:663
  156.2 0.6 reshape_squeeze.7
  (49 shorter events, 3.8 us)
Async XLA Ops:
  1.6 8.2 %copy-start.9 = (bf16[4,7,7,384]{3,0,2,1:T(4,128)(2,1)S(1)}, bf16[4,7,7,384]{3,0,2,1:T(4,128)(2,1)}, u32[]{:S(2)}) copy-start(bf16[4,7,7,384]{3,0,2,1:T(4,128)(2,1)} %param.13) | copy-start | bytes 451588
  10.1 18.0 %copy-start.2 = (bf16[384,1536]{1,0:T(8,128)(2,1)S(1)}, bf16[384,1536]{1,0:T(8,128)(2,1)}, u32[]{:S(2)}) copy-start(bf16[384,1536]{1,0:T(8,128)(2,1)} %refs_5_.4) | copy-start | bytes 3538948
  10.1 18.0 %copy-start.3 = (bf16[1536,384]{1,0:T(8,128)(2,1)S(1)}, bf16[1536,384]{1,0:T(8,128)(2,1)}, u32[]{:S(2)}) copy-start(bf16[1536,384]{1,0:T(8,128)(2,1)} %refs_6_.1) | copy-start | bytes 3538948
  10.2 18.0 %copy-start.4 = (bf16[384,1152]{1,0:T(8,128)(2,1)S(1)}, bf16[384,1152]{1,0:T(8,128)(2,1)}, u32[]{:S(2)}) copy-start(bf16[384,1152]{1,0:T(8,128)(2,1)} %refs_3_.4) | copy-start | bytes 2654212
  10.2 18.0 %copy-start.6 = (bf16[384,384]{1,0:T(8,128)(2,1)S(1)}, bf16[384,384]{1,0:T(8,128)(2,1)}, u32[]{:S(2)}) copy-start(bf16[384,384]{1,0:T(8,128)(2,1)} %refs_4_.3) | copy-start | bytes 884740
  10.2 18.0 %copy-start.8 = (f32[12,1183]{1,0:T(8,128)S(1)}, f32[12,1183]{1,0:T(8,128)}, u32[]{:S(2)}) copy-start(f32[12,1183]{1,0:T(8,128)} %refs_2_.3) | copy-start | bytes 170356
  10.2 10.9 %collective-permute-start.1 = (bf16[2,2,4,7,384]{4,1,3,2,0:T(2,128)(2,1)S(1)}, bf16[2,2,4,7,384]{4,1,3,2,0:T(2,128)(2,1)S(1)}, u32[]{:S(2)}, u32[]{:S(2)}) collective-permute-start(bf16[2,2,4,7,384]{4,1,3,2,0:T(2,128)(2,1)S(1)} %get-tuple-element.84), channel_id=1, source_target_pairs={{0,64},{8,72},{16,80},{24,88},{32,96},{40,104},{48,112},{56,120},{... | collective-permute-start | bytes 258056 | tf_op jit(solution)/shard_map/ppermute | solution.py:612
  14.0 4.2 %collective-permute-start = (bf16[2,2,3,7,384]{4,1,3,2,0:T(2,128)(2,1)S(1)}, bf16[2,2,3,7,384]{4,1,3,2,0:T(2,128)(2,1)S(1)}, u32[]{:S(2)}, u32[]{:S(2)}) collective-permute-start(bf16[2,2,3,7,384]{4,1,3,2,0:T(2,128)(2,1)S(1)} %get-tuple-element.85), channel_id=1, source_target_pairs={{0,56},{8,0},{16,8},{24,16},{32,24},{40,32},{48,40},{56,48},{64,12... | collective-permute-start | bytes 193544 | tf_op jit(solution)/shard_map/ppermute | solution.py:612
  16.8 4.3 %collective-permute-start.2 = (bf16[2,2,3,7,384]{4,1,3,2,0:T(2,128)(2,1)S(1)}, bf16[2,2,3,7,384]{4,1,3,2,0:T(2,128)(2,1)S(1)}, u32[]{:S(2)}, u32[]{:S(2)}) collective-permute-start(bf16[2,2,3,7,384]{4,1,3,2,0:T(2,128)(2,1)S(1)} %get-tuple-element.86), channel_id=1, source_target_pairs={{0,120},{8,64},{16,72},{24,80},{32,88},{40,96},{48,104},{56,112},{... | collective-permute-start | bytes 193544 | tf_op jit(solution)/shard_map/ppermute | solution.py:612
  21.2 6.6 %collective-permute-start.3 = (bf16[2,4,7,3,384]{4,1,3,2,0:T(4,128)(2,1)S(1)}, bf16[2,4,7,3,384]{4,1,3,2,0:T(4,128)(2,1)S(1)}, u32[]{:S(2)}, u32[]{:S(2)}) collective-permute-start(bf16[2,4,7,3,384]{4,1,3,2,0:T(4,128)(2,1)S(1)} %maximum_maximum_fusion.2), channel_id=1, source_target_pairs={{1,0},{2,1},{3,2},{4,3},{5,4},{6,5},{7,6},{0,7},{9,8},{10,9},{11,1... | collective-permute-start | bytes 387080 | tf_op jit(solution)/shard_map/ppermute | solution.py:567
  39.6 6.9 %collective-permute-start.5 = (bf16[2,4,7,384]{3,2,1,0:T(8,128)(2,1)S(1)}, bf16[2,4,7,384]{3,2,1,0:T(8,128)(2,1)S(1)}, u32[]{:S(2)}, u32[]{:S(2)}) collective-permute-start(bf16[2,4,7,384]{3,2,1,0:T(8,128)(2,1)S(1)} %get-tuple-element.89), channel_id=1, source_target_pairs={{0,64},{8,72},{16,80},{24,88},{32,96},{40,104},{48,112},{56,120},{... | collective-permute-start | bytes 129032 | tf_op jit(solution)/shard_map/ppermute | solution.py:612
  40.2 6.3 %collective-permute-start.4 = (bf16[2,3,7,384]{3,2,1,0:T(8,128)(2,1)S(1)}, bf16[2,3,7,384]{3,2,1,0:T(8,128)(2,1)S(1)}, u32[]{:S(2)}, u32[]{:S(2)}) collective-permute-start(bf16[2,3,7,384]{3,2,1,0:T(8,128)(2,1)S(1)} %get-tuple-element.87), channel_id=1, source_target_pairs={{0,72},{8,80},{16,88},{24,96},{32,104},{40,112},{48,120},{56,64},{... | collective-permute-start | bytes 96776 | tf_op jit(solution)/shard_map/ppermute | solution.py:612
  40.9 5.7 %collective-permute-start.6 = (bf16[2,3,7,384]{3,2,1,0:T(8,128)(2,1)S(1)}, bf16[2,3,7,384]{3,2,1,0:T(8,128)(2,1)S(1)}, u32[]{:S(2)}, u32[]{:S(2)}) collective-permute-start(bf16[2,3,7,384]{3,2,1,0:T(8,128)(2,1)S(1)} %get-tuple-element.88), channel_id=1, source_target_pairs={{0,8},{8,16},{16,24},{24,32},{32,40},{40,48},{48,56},{56,0},{64,72... | collective-permute-start | bytes 96776 | tf_op jit(solution)/shard_map/ppermute | solution.py:612
  46.7 11.5 %collective-permute-start.7 = (bf16[4,7,3,384]{3,2,1,0:T(4,128)(2,1)S(1)}, bf16[4,7,3,384]{3,2,1,0:T(4,128)(2,1)S(1)}, u32[]{:S(2)}, u32[]{:S(2)}) collective-permute-start(bf16[4,7,3,384]{3,2,1,0:T(4,128)(2,1)S(1)} %slice.115), channel_id=1, source_target_pairs={{7,0},{0,1},{1,2},{2,3},{3,4},{4,5},{5,6},{6,7},{15,8},{8,9},{9,10... | collective-permute-start | bytes 193544 | tf_op jit(solution)/shard_map/ppermute | solution.py:567
  48.0 10.3 %copy-start = (bf16[384,1536]{1,0:T(8,128)(2,1)S(1)}, bf16[384,1536]{1,0:T(8,128)(2,1)}, u32[]{:S(2)}) copy-start(bf16[384,1536]{1,0:T(8,128)(2,1)} %refs_5_.5) | copy-start | bytes 3538948
  48.0 10.3 %copy-start.1 = (bf16[1536,384]{1,0:T(8,128)(2,1)S(1)}, bf16[1536,384]{1,0:T(8,128)(2,1)}, u32[]{:S(2)}) copy-start(bf16[1536,384]{1,0:T(8,128)(2,1)} %refs_3_.5) | copy-start | bytes 3538948
  48.0 10.3 %copy-start.5 = (bf16[224,1536]{1,0:T(8,128)(2,1)S(1)}, bf16[224,1536]{1,0:T(8,128)(2,1)}, u32[]{:S(2)}) copy-start(bf16[224,1536]{1,0:T(8,128)(2,1)} %get-tuple-element.56.refs_4_) | copy-start | bytes 2064388
  48.1 10.3 %copy-start.7 = (bf16[224,384]{1,0:T(8,128)(2,1)S(1)}, bf16[224,384]{1,0:T(8,128)(2,1)}, u32[]{:S(2)}) copy-start(bf16[224,384]{1,0:T(8,128)(2,1)} %get-tuple-element.57.refs_6_) | copy-start | bytes 516100
  71.4 4.3 %collective-permute-start.8 = (bf16[7168,128]{1,0:T(8,128)(2,1)}, bf16[7168,128]{1,0:T(8,128)(2,1)S(1)}, u32[]{:S(2)}, u32[]{:S(2)}) collective-permute-start(bf16[7168,128]{1,0:T(8,128)(2,1)} %get-tuple-element.68), channel_id=1, source_target_pairs={{0,1},{1,0},{2,3},{3,2},{4,5},{5,4},{6,7},{7,6},{8,9},{9,8},{10,11... | collective-permute-start | bytes 5505032 | tf_op jit(solution)/shard_map/ppermute | solution.py:628
  72.1 6.2 %collective-permute-start.9 = (bf16[7168,128]{1,0:T(8,128)(2,1)}, bf16[7168,128]{1,0:T(8,128)(2,1)S(1)}, u32[]{:S(2)}, u32[]{:S(2)}) collective-permute-start(bf16[7168,128]{1,0:T(8,128)(2,1)} %get-tuple-element.69), channel_id=1, source_target_pairs={{0,1},{1,0},{2,3},{3,2},{4,5},{5,4},{6,7},{7,6},{8,9},{9,8},{10,11... | collective-permute-start | bytes 5505032 | tf_op jit(solution)/shard_map/ppermute | solution.py:628
  138.7 17.1 %all-to-all-start.1 = ((f32[128,2,128]{2,1,0:T(2,128)}), f32[128,2,128]{2,1,0:T(2,128)S(1)}, u32[]{:S(2)}, u32[]{:S(2)}) async-start(f32[128,2,128]{2,1,0:T(2,128)} %get-tuple-element.72), calls=%async_computation.1 | async-start | bytes 262144 | tf_op jit(solution)/shard_map/all_to_all | solution.py:663

commit v5 on v4

--- a/solution.py
+++ b/solution.py
@@ -464,15 +464,14 @@
 HALF = ((64 * CHUNK, 128), bf16, "far")
 
 
-def run_first_backward(mine, gy, x, kept, weights, give_two):
+def run_first_backward(mine, gy, x, kept, weights):
     return launch(
         first_backward,
         {"mine": (mine, "flag"), "gy": (gy, "near"), "x": (x, "near"), "wc": (weights["wc"][0], "near")}
         | {"slope": (kept["slope"], "near"), "we": (weights["we"][0], "near"), "h": (kept["h"], "near")}
         | {"wp": weights["wp"]}
         | {"qkv": (kept["qkv"], "far"), "p": (kept["p"], "far"), "wqkv": weights["wqkv"]}
-        | {name: (kept[name], "far") for name in ("n1", "ctx", "n2", "act")}
-        | {"give_two": (give_two, "pass")},
+        | {name: (kept[name], "far") for name in ("n1", "ctx", "n2", "act")},
         {"dx": rows(D, "near"), "keep": HALF, "give": HALF},
         {
             "turned": scr((D, ROWS), f32), "dctx": scr((ROWS, D), bf16), "big": scr((ROWS, D), f32),
@@ -545,7 +544,31 @@
                 for c in range(width):
                     row = at + first + r * width + c
                     target[r : r + 1, c * 128 : c * 128 + 128] = m.total[row : row + 1, :]
-        m.lines[:, b, :] = jnp.broadcast_to(m.total[at + 108 : at + 109, :], (128, 128))
+
+
+def lines_kernel(spread, lines_ref, near_ref, sems):
+    copies = [
+        pltpu.make_async_copy(spread.at[:, pl.ds(b * CHUNK + 96, 16), :], near_ref.at[b], sems.at[b]) for b in range(2)
+    ]
+    for copy in copies:
+        copy.start()
+    for b, copy in enumerate(copies):
+        copy.wait()
+        total = jnp.zeros((16, 128), f32)
+        for i in range(64):
+            total = total + near_ref[b, i].astype(f32)
+        lines_ref[:, b, :] = jnp.broadcast_to(total[12:13], (128, 128))
+
+
+def run_lines(spread):
+    return pl.pallas_call(
+        lines_kernel,
+        out_shape=jax.ShapeDtypeStruct((128, 2, 128), f32),
+        in_specs=[pl.BlockSpec(memory_space=pltpu.HBM)],
+        out_specs=pl.BlockSpec(memory_space=pltpu.VMEM),
+        scratch_shapes=[pltpu.VMEM((2, 64, 16, 128), bf16), pltpu.SemaphoreType.DMA((2,))],
+        compiler_params=pltpu.CompilerParams(vmem_limit_bytes=VMEM_LIMIT),
+    )(pltpu.with_memory_space_constraint(spread, pltpu.HBM))
 
 
 def run_finish(spread):
@@ -556,7 +579,7 @@
     return launch(
         finish_kernel,
         {"spread": (spread, "parts")},
-        outs | {"lines": ((128, 2, 128), f32, "near")},
+        outs,
         {"total": pltpu.VMEM((2 * CHUNK, 128), f32)},
     )
 
@@ -654,13 +677,14 @@
     sent = passed_along(edge_of(gy, 2, WW // 2, 1), AXES[2], 1)
     sums_two = run_weights(mine, two, up, to_rows(gy))
     gy = to_rows(rejoin(to_grid(sums_two["passed"]), 2, WW // 2, 1, sent))
-    sums_one = run_first_backward(mine, gy, x, one, weights_one, sums_two["give"])
+    arrived_two = swapped(sums_two["give"])
+    sums_one = run_first_backward(mine, gy, x, one, weights_one)
     dx = sums_one["dx"]
     spread = exchanged(
-        run_merge(sums_one["keep"], sums_two["keep"], swapped(sums_one["give"]), swapped(sums_one["give_two"]))
-    )
+        run_merge(sums_one["keep"], sums_two["keep"], swapped(sums_one["give"]), arrived_two)
+    )
+    tables = lax.all_to_all(run_lines(spread), AXES, 0, 0, tiled=True)
     done = run_finish(spread)
-    tables = lax.all_to_all(done["lines"], AXES, 0, 0, tiled=True)
 
     def table_of(which):
         return tables[:120, which].reshape(HEADS, TPAD)[:, :TABLE]

time: 158 us -> 154 us (0.975)
  waiting for transfers between devices: 28.6 us -> 23.4 us
  Pallas kernels: 49.4 us -> 51.1 us
    all_to_all x1, waiting for transfers between devices: 9.5 us -> 6.58 us  [body(): tables = lax.all_to_all(run_lines(spread), AXES, 0, 0, tiled=True)]
    ppermute x2, waiting for transfers between devices: 6.15 us -> 3.96 us  [swapped(): lax.ppermute(block, 'wa', [(i, i ^ 1) for i in range(lax.axis_size('wa'))])]
    pallas_call x0 -> x1, Pallas kernels: none -> 1.82 us  [run_lines(): pl.pallas_call(lines_kernel, out_shape=jax.ShapeDtypeStruct((128, 2, 128)...]
  transfers between devices with their start and end apart: 11 -> 11, of which waited for: 7 -> 6; matrix products, arithmetic and copies ran while one was open for 1% -> 1% of each run, Pallas kernels for 6% -> 17%
where the time goes in v5:
time: 154 us
  blocking collectives  53.3 us (35%)
  Pallas kernels  51.1 us (33%)
  waiting for transfers between devices  23.4 us (15%)
  starting transfers between devices  19.9 us (13%)
  local copies, waits for them, and re-layouts  3.73 us (2%)
    all_to_all x1, blocking collectives, exchanged(): lax.all_to_all(both, AXES, 0, 0, axis_index_groups=groups, tiled=True)  53.3 us
    pallas_call x6, Pallas kernels, launch(): pl.pallas_call(wrapped, out_shape=[pltpu.HBM(shape, dtype) if space in ('...  49.3 us
    ppermute x6, waiting for transfers between devices, rolled_twice(): part = lax.ppermute(part, AXES[:2], route)  9.13 us
    ppermute x6, starting transfers between devices, rolled_twice(): part = lax.ppermute(part, AXES[:2], route)  8.59 us
    all_to_all x1, starting transfers between devices, body(): tables = lax.all_to_all(run_lines(spread), AXES, 0, 0, tiled=True)  6.83 us
    all_to_all x1, waiting for transfers between devices, body(): tables = lax.all_to_all(run_lines(spread), AXES, 0, 0, tiled=True)  6.58 us
    ppermute x2, waiting for transfers between devices, swapped(): lax.ppermute(block, 'wa', [(i, i ^ 1) for i in range(lax.axis_size('wa'))])  3.96 us
    ppermute x2, waiting for transfers between devices, passed_along(): return lax.ppermute(block, axis, route)  3.76 us
  transfers between devices with their start and end apart: 11, of which 6 were waited for; matrix products, arithmetic and copies ran while one was open for 1% of the time, Pallas kernels for 17%

profile of v5, /device:TPU:1, one launch (start us, length us, event | category | flops | bytes accessed | tf_op | source)
XLA Modules:
  0.0 153.7 jit_solution(3331091249182202800)
XLA Ops:
  0.6 0.9 copy.30
  1.6 8.1 %shard_map.203 = (bf16[224,384]{1,0:T(8,128)(2,1)}, bf16[224,1152]{1,0:T(8,128)(2,1)}, bf16[12,224,224]{2,1,0:T(8,128)(2,1)}, bf16[224,384]{1,0:T(8,128)(2,1)}, ...) custom-call(bf16[224,384]{1,0:T(8,128)(2,1)S(1)} %bitcast.23, ...), custom_call_target="tpu_custom_call" | custom-call | tf_op jit(solution)/shard_map/pallas_call | solution.py:89
  10.2 3.7 %collective-permute-start.1 = (bf16[2,2,4,7,384]{4,1,3,2,0:T(2,128)(2,1)S(1)}, bf16[2,2,4,7,384]{4,1,3,2,0:T(2,128)(2,1)S(1)}, u32[]{:S(2)}, u32[]{:S(2)}) collective-permute-start(bf16[2,2,4,7,384]{4,1,3,2,0:T(2,128)(2,1)S(1)} %get-tuple-element.80), channel_id=1, source_target_pairs={{0,64},{8,72},{16,80},{24,88},{32,96},{40,104},{48,112},{56,120},{... | collective-permute-start | bytes 258056 | tf_op jit(solution)/shard_map/ppermute | solution.py:635
  13.9 2.8 %collective-permute-start = (bf16[2,2,3,7,384]{4,1,3,2,0:T(2,128)(2,1)S(1)}, bf16[2,2,3,7,384]{4,1,3,2,0:T(2,128)(2,1)S(1)}, u32[]{:S(2)}, u32[]{:S(2)}) collective-permute-start(bf16[2,2,3,7,384]{4,1,3,2,0:T(2,128)(2,1)S(1)} %get-tuple-element.81), channel_id=1, source_target_pairs={{0,56},{8,0},{16,8},{24,16},{32,24},{40,32},{48,40},{56,48},{64,12... | collective-permute-start | bytes 193544 | tf_op jit(solution)/shard_map/ppermute | solution.py:635
  16.8 0.8 collective-permute-start.2
  18.1 3.0 %collective-permute-done.2 = bf16[2,2,3,7,384]{4,1,3,2,0:T(2,128)(2,1)S(1)} collective-permute-done((bf16[2,2,3,7,384]{4,1,3,2,0:T(2,128)(2,1)S(1)}, bf16[2,2,3,7,384]{4,1,3,2,0:T(2,128)(2,1)S(1)}, u32[]{:S(2)}, u32[]{:S(2)}) %collective-permute-start.2) | collective-permute-done | bytes 64544 | tf_op jit(solution)/shard_map/ppermute | solution.py:635
  21.2 2.4 %collective-permute-start.3 = (bf16[2,4,7,3,384]{4,1,3,2,0:T(4,128)(2,1)S(1)}, bf16[2,4,7,3,384]{4,1,3,2,0:T(4,128)(2,1)S(1)}, u32[]{:S(2)}, u32[]{:S(2)}) collective-permute-start(bf16[2,4,7,3,384]{4,1,3,2,0:T(4,128)(2,1)S(1)} %maximum_maximum_fusion.2), channel_id=1, source_target_pairs={{1,0},{2,1},{3,2},{4,3},{5,4},{6,5},{7,6},{0,7},{9,8},{10,9},{11,1... | collective-permute-start | bytes 387080 | tf_op jit(solution)/shard_map/ppermute | solution.py:590
  24.1 3.8 %collective-permute-done.3 = bf16[2,4,7,3,384]{4,1,3,2,0:T(4,128)(2,1)S(1)} collective-permute-done((bf16[2,4,7,3,384]{4,1,3,2,0:T(4,128)(2,1)S(1)}, bf16[2,4,7,3,384]{4,1,3,2,0:T(4,128)(2,1)S(1)}, u32[]{:S(2)}, u32[]{:S(2)}) %collective-permute-start.3) | collective-permute-done | bytes 129056 | tf_op jit(solution)/shard_map/ppermute | solution.py:590
  28.2 11.4 %shard_map.204 = (bf16[224,384]{1,0:T(8,128)(2,1)}, bf16[224,384]{1,0:T(8,128)(2,1)}, bf16[224,384]{1,0:T(8,128)(2,1)}, bf16[224,1536]{1,0:T(8,128)(2,1)}, bf16[...) custom-call(bf16[224,384]{1,0:T(8,128)(2,1)S(1)} %bitcast.28, ...), custom_call_target="tpu_custom_call" | custom-call | tf_op jit(solution)/shard_map/pallas_call | solution.py:89
  40.3 0.7 collective-permute-start.4
  40.9 5.6 %collective-permute-done.4 = bf16[2,3,7,384]{3,2,1,0:T(8,128)(2,1)S(1)} collective-permute-done((bf16[2,3,7,384]{3,2,1,0:T(8,128)(2,1)S(1)}, bf16[2,3,7,384]{3,2,1,0:T(8,128)(2,1)S(1)}, u32[]{:S(2)}, u32[]{:S(2)}) %collective-permute-start.4) | collective-permute-done | bytes 32288 | tf_op jit(solution)/shard_map/ppermute | solution.py:635
  46.7 1.3 collective-permute-start.7
  48.1 10.1 %shard_map.205 = (bf16[7168,128]{1,0:T(8,128)(2,1)}, bf16[7168,128]{1,0:T(8,128)(2,1)}, bf16[224,384]{1,0:T(8,128)(2,1)S(1)}) custom-call(s32[1]{0:T(128)} %bitcast.refs_0_, bf16[224,384]{1,0:T(8,128)(2,1)S(1)} %bitcast.26, bf16[224,384]{1,0:T(8,128)(2,1)S(1)} %bitcast.29, bf16[224,384]{1,0:T(8,128)(2,1)} %get-tuple-element.45.refs_3_, ...), custom_call_target="tpu_custom_call" | custom-call | tf_op jit(solution)/shard_map/pallas_call | solution.py:89
  58.2 0.7 collective-permute-start.9
  59.0 13.0 %shard_map.206 = (bf16[224,384]{1,0:T(8,128)(2,1)S(1)}, bf16[7168,128]{1,0:T(8,128)(2,1)}, bf16[7168,128]{1,0:T(8,128)(2,1)}) custom-call(s32[1]{0:T(128)} %bitcast.refs_0_, bf16[224,384]{1,0:T(8,128)(2,1)S(1)} %bitcast.27, bf16[224,384]{1,0:T(8,128)(2,1)S(1)} %bitcast.24, bf16[1536,384]{1,0:T(8,128)(2,1)S(1)} %copy-done.1, bf16[224,1536]{1,0:T(8,128)(2,1)S(1)} %copy-done.5, ...), custom_call_target="tpu_custom_call" | custom-call | tf_op jit(solution)/shard_map/pallas_call | solution.py:89
  72.2 4.0 %collective-permute-done.8.refs_2_ = bf16[7168,128]{1,0:T(8,128)(2,1)S(1)} collective-permute-done((bf16[7168,128]{1,0:T(8,128)(2,1)}, bf16[7168,128]{1,0:T(8,128)(2,1)S(1)}, u32[]{:S(2)}, u32[]{:S(2)}) %collective-permute-start.8) | collective-permute-done | bytes 1835040 | tf_op jit(solution)/shard_map/ppermute | solution.py:651
  76.1 3.7 %shard_map.207 = bf16[14336,128]{1,0:T(8,128)(2,1)} custom-call(bf16[7168,128]{1,0:T(8,128)(2,1)} %get-tuple-element.63.refs_0_, bf16[7168,128]{1,0:T(8,128)(2,1)} %get-tuple-element.64.refs_1_, bf16[7168,128]{1,0:T(8,128)(2,1)S(1)} %collective-permute-done.8.refs_2_, bf16[7168,128]{1,0:T(8,128)(2,1)S(1)} %collective-permute-done.9.refs_3_), custom_call_target="tpu_custom_call" | custom-call | tf_op jit(solution)/shard_map/pallas_call | solution.py:89
  79.9 53.3 %all_to_all.10.refs_0_.spread = bf16[64,224,128]{2,1,0:T(8,128)(2,1)} all-to-all(bf16[64,224,128]{2,1,0:T(8,128)(2,1)} %bitcast.35), channel_id=1, replica_groups={{0,2,4,6,8,10,12,14,16,18,20,22,24,26,28,30,32,34,36,38,40,42,44,46,48,..., dimensions={0} | all-to-all | bytes 7340032 | tf_op jit(solution)/shard_map/all_to_all | solution.py:656
  133.2 1.8 %shard_map.209 = f32[128,2,128]{2,1,0:T(2,128)} custom-call(bf16[64,224,128]{2,1,0:T(8,128)(2,1)} %all_to_all.10.refs_0_.spread), custom_call_target="tpu_custom_call" | custom-call | tf_op jit(solution)/shard_map/pallas_call | solution.py:564
  135.0 6.8 %all-to-all-start.1 = ((f32[128,2,128]{2,1,0:T(2,128)}), f32[128,2,128]{2,1,0:T(2,128)S(1)}, u32[]{:S(2)}, u32[]{:S(2)}) async-start(f32[128,2,128]{2,1,0:T(2,128)} %shard_map.209), calls=%async_computation.1 | async-start | bytes 262144 | tf_op jit(solution)/shard_map/all_to_all | solution.py:686
  141.9 0.7 copy.29
  142.6 2.9 %shard_map.208 = (f32[3,1152]{1,0:T(4,128)}, f32[3,384]{1,0:T(4,128)}, f32[3,1536]{1,0:T(4,128)}, f32[12,384]{1,0:T(8,128)}, f32[3,1152]{1,0:T(4,128)}, /*index=...) custom-call(bf16[64,224,128]{2,1,0:T(8,128)(2,1)} %all_to_all.10.refs_0_.spread), custom_call_target="tpu_custom_call" | custom-call | tf_op jit(solution)/shard_map/pallas_call | solution.py:89
  145.5 6.6 %all-to-all-done.1 = f32[128,2,128]{2,1,0:T(2,128)S(1)} async-done(((f32[128,2,128]{2,1,0:T(2,128)}), f32[128,2,128]{2,1,0:T(2,128)S(1)}, u32[]{:S(2)}, u32[]{:S(2)}) %all-to-all-start.1) | async-done | bytes 131104 | tf_op jit(solution)/shard_map/all_to_all | solution.py:686
  152.4 0.6 reshape_squeeze.7
  (50 shorter events, 3.8 us)
Async XLA Ops:
  1.6 8.2 %copy-start.9 = (bf16[4,7,7,384]{3,0,2,1:T(4,128)(2,1)S(1)}, bf16[4,7,7,384]{3,0,2,1:T(4,128)(2,1)}, u32[]{:S(2)}) copy-start(bf16[4,7,7,384]{3,0,2,1:T(4,128)(2,1)} %param.13) | copy-start | bytes 451588
  10.1 18.1 %copy-start.2 = (bf16[384,1536]{1,0:T(8,128)(2,1)S(1)}, bf16[384,1536]{1,0:T(8,128)(2,1)}, u32[]{:S(2)}) copy-start(bf16[384,1536]{1,0:T(8,128)(2,1)} %refs_5_.4) | copy-start | bytes 3538948
  10.1 18.1 %copy-start.3 = (bf16[1536,384]{1,0:T(8,128)(2,1)S(1)}, bf16[1536,384]{1,0:T(8,128)(2,1)}, u32[]{:S(2)}) copy-start(bf16[1536,384]{1,0:T(8,128)(2,1)} %refs_6_.1) | copy-start | bytes 3538948
  10.1 18.0 %copy-start.4 = (bf16[384,1152]{1,0:T(8,128)(2,1)S(1)}, bf16[384,1152]{1,0:T(8,128)(2,1)}, u32[]{:S(2)}) copy-start(bf16[384,1152]{1,0:T(8,128)(2,1)} %refs_3_.4) | copy-start | bytes 2654212
  10.2 18.0 %copy-start.6 = (bf16[384,384]{1,0:T(8,128)(2,1)S(1)}, bf16[384,384]{1,0:T(8,128)(2,1)}, u32[]{:S(2)}) copy-start(bf16[384,384]{1,0:T(8,128)(2,1)} %refs_4_.3) | copy-start | bytes 884740
  10.2 18.0 %copy-start.8 = (f32[12,1183]{1,0:T(8,128)S(1)}, f32[12,1183]{1,0:T(8,128)}, u32[]{:S(2)}) copy-start(f32[12,1183]{1,0:T(8,128)} %refs_2_.3) | copy-start | bytes 170356
  10.2 10.9 %collective-permute-start.1 = (bf16[2,2,4,7,384]{4,1,3,2,0:T(2,128)(2,1)S(1)}, bf16[2,2,4,7,384]{4,1,3,2,0:T(2,128)(2,1)S(1)}, u32[]{:S(2)}, u32[]{:S(2)}) collective-permute-start(bf16[2,2,4,7,384]{4,1,3,2,0:T(2,128)(2,1)S(1)} %get-tuple-element.80), channel_id=1, source_target_pairs={{0,64},{8,72},{16,80},{24,88},{32,96},{40,104},{48,112},{56,120},{... | collective-permute-start | bytes 258056 | tf_op jit(solution)/shard_map/ppermute | solution.py:635
  13.9 4.2 %collective-permute-start = (bf16[2,2,3,7,384]{4,1,3,2,0:T(2,128)(2,1)S(1)}, bf16[2,2,3,7,384]{4,1,3,2,0:T(2,128)(2,1)S(1)}, u32[]{:S(2)}, u32[]{:S(2)}) collective-permute-start(bf16[2,2,3,7,384]{4,1,3,2,0:T(2,128)(2,1)S(1)} %get-tuple-element.81), channel_id=1, source_target_pairs={{0,56},{8,0},{16,8},{24,16},{32,24},{40,32},{48,40},{56,48},{64,12... | collective-permute-start | bytes 193544 | tf_op jit(solution)/shard_map/ppermute | solution.py:635
  16.8 4.3 %collective-permute-start.2 = (bf16[2,2,3,7,384]{4,1,3,2,0:T(2,128)(2,1)S(1)}, bf16[2,2,3,7,384]{4,1,3,2,0:T(2,128)(2,1)S(1)}, u32[]{:S(2)}, u32[]{:S(2)}) collective-permute-start(bf16[2,2,3,7,384]{4,1,3,2,0:T(2,128)(2,1)S(1)} %get-tuple-element.82), channel_id=1, source_target_pairs={{0,120},{8,64},{16,72},{24,80},{32,88},{40,96},{48,104},{56,112},{... | collective-permute-start | bytes 193544 | tf_op jit(solution)/shard_map/ppermute | solution.py:635
  21.2 6.6 %collective-permute-start.3 = (bf16[2,4,7,3,384]{4,1,3,2,0:T(4,128)(2,1)S(1)}, bf16[2,4,7,3,384]{4,1,3,2,0:T(4,128)(2,1)S(1)}, u32[]{:S(2)}, u32[]{:S(2)}) collective-permute-start(bf16[2,4,7,3,384]{4,1,3,2,0:T(4,128)(2,1)S(1)} %maximum_maximum_fusion.2), channel_id=1, source_target_pairs={{1,0},{2,1},{3,2},{4,3},{5,4},{6,5},{7,6},{0,7},{9,8},{10,9},{11,1... | collective-permute-start | bytes 387080 | tf_op jit(solution)/shard_map/ppermute | solution.py:590
  39.7 6.9 %collective-permute-start.5 = (bf16[2,4,7,384]{3,2,1,0:T(8,128)(2,1)S(1)}, bf16[2,4,7,384]{3,2,1,0:T(8,128)(2,1)S(1)}, u32[]{:S(2)}, u32[]{:S(2)}) collective-permute-start(bf16[2,4,7,384]{3,2,1,0:T(8,128)(2,1)S(1)} %get-tuple-element.85), channel_id=1, source_target_pairs={{0,64},{8,72},{16,80},{24,88},{32,96},{40,104},{48,112},{56,120},{... | collective-permute-start | bytes 129032 | tf_op jit(solution)/shard_map/ppermute | solution.py:635
  40.3 6.3 %collective-permute-start.4 = (bf16[2,3,7,384]{3,2,1,0:T(8,128)(2,1)S(1)}, bf16[2,3,7,384]{3,2,1,0:T(8,128)(2,1)S(1)}, u32[]{:S(2)}, u32[]{:S(2)}) collective-permute-start(bf16[2,3,7,384]{3,2,1,0:T(8,128)(2,1)S(1)} %get-tuple-element.83), channel_id=1, source_target_pairs={{0,72},{8,80},{16,88},{24,96},{32,104},{40,112},{48,120},{56,64},{... | collective-permute-start | bytes 96776 | tf_op jit(solution)/shard_map/ppermute | solution.py:635
  40.9 5.6 %collective-permute-start.6 = (bf16[2,3,7,384]{3,2,1,0:T(8,128)(2,1)S(1)}, bf16[2,3,7,384]{3,2,1,0:T(8,128)(2,1)S(1)}, u32[]{:S(2)}, u32[]{:S(2)}) collective-permute-start(bf16[2,3,7,384]{3,2,1,0:T(8,128)(2,1)S(1)} %get-tuple-element.84), channel_id=1, source_target_pairs={{0,8},{8,16},{16,24},{24,32},{32,40},{40,48},{48,56},{56,0},{64,72... | collective-permute-start | bytes 96776 | tf_op jit(solution)/shard_map/ppermute | solution.py:635
  46.7 12.2 %collective-permute-start.7 = (bf16[4,7,3,384]{3,2,1,0:T(4,128)(2,1)S(1)}, bf16[4,7,3,384]{3,2,1,0:T(4,128)(2,1)S(1)}, u32[]{:S(2)}, u32[]{:S(2)}) collective-permute-start(bf16[4,7,3,384]{3,2,1,0:T(4,128)(2,1)S(1)} %slice.115), channel_id=1, source_target_pairs={{7,0},{0,1},{1,2},{2,3},{3,4},{4,5},{5,6},{6,7},{15,8},{8,9},{9,10... | collective-permute-start | bytes 193544 | tf_op jit(solution)/shard_map/ppermute | solution.py:590
  48.1 10.9 %copy-start = (bf16[384,1536]{1,0:T(8,128)(2,1)S(1)}, bf16[384,1536]{1,0:T(8,128)(2,1)}, u32[]{:S(2)}) copy-start(bf16[384,1536]{1,0:T(8,128)(2,1)} %refs_5_.5) | copy-start | bytes 3538948
  48.1 10.9 %copy-start.1 = (bf16[1536,384]{1,0:T(8,128)(2,1)S(1)}, bf16[1536,384]{1,0:T(8,128)(2,1)}, u32[]{:S(2)}) copy-start(bf16[1536,384]{1,0:T(8,128)(2,1)} %refs_3_.5) | copy-start | bytes 3538948
  48.1 10.9 %copy-start.5 = (bf16[224,1536]{1,0:T(8,128)(2,1)S(1)}, bf16[224,1536]{1,0:T(8,128)(2,1)}, u32[]{:S(2)}) copy-start(bf16[224,1536]{1,0:T(8,128)(2,1)} %get-tuple-element.54.refs_4_) | copy-start | bytes 2064388
  48.1 10.9 %copy-start.7 = (bf16[224,384]{1,0:T(8,128)(2,1)S(1)}, bf16[224,384]{1,0:T(8,128)(2,1)}, u32[]{:S(2)}) copy-start(bf16[224,384]{1,0:T(8,128)(2,1)} %get-tuple-element.55.refs_6_) | copy-start | bytes 516100
  58.2 14.0 %collective-permute-start.9 = (bf16[7168,128]{1,0:T(8,128)(2,1)}, bf16[7168,128]{1,0:T(8,128)(2,1)S(1)}, u32[]{:S(2)}, u32[]{:S(2)}) collective-permute-start(bf16[7168,128]{1,0:T(8,128)(2,1)} %get-tuple-element.66), channel_id=1, source_target_pairs={{0,1},{1,0},{2,3},{3,2},{4,5},{5,4},{6,7},{7,6},{8,9},{9,8},{10,11... | collective-permute-start | bytes 5505032 | tf_op jit(solution)/shard_map/ppermute | solution.py:651
  72.1 4.1 %collective-permute-start.8 = (bf16[7168,128]{1,0:T(8,128)(2,1)}, bf16[7168,128]{1,0:T(8,128)(2,1)S(1)}, u32[]{:S(2)}, u32[]{:S(2)}) collective-permute-start(bf16[7168,128]{1,0:T(8,128)(2,1)} %get-tuple-element.65), channel_id=1, source_target_pairs={{0,1},{1,0},{2,3},{3,2},{4,5},{5,4},{6,7},{7,6},{8,9},{9,8},{10,11... | collective-permute-start | bytes 5505032 | tf_op jit(solution)/shard_map/ppermute | solution.py:651
  135.0 17.1 %all-to-all-start.1 = ((f32[128,2,128]{2,1,0:T(2,128)}), f32[128,2,128]{2,1,0:T(2,128)S(1)}, u32[]{:S(2)}, u32[]{:S(2)}) async-start(f32[128,2,128]{2,1,0:T(2,128)} %shard_map.209), calls=%async_computation.1 | async-start | bytes 262144 | tf_op jit(solution)/shard_map/all_to_all | solution.py:686

commit v6 on v5

--- a/solution.py
+++ b/solution.py
@@ -469,8 +469,8 @@
         first_backward,
         {"mine": (mine, "flag"), "gy": (gy, "near"), "x": (x, "near"), "wc": (weights["wc"][0], "near")}
         | {"slope": (kept["slope"], "near"), "we": (weights["we"][0], "near"), "h": (kept["h"], "near")}
-        | {"wp": weights["wp"]}
-        | {"qkv": (kept["qkv"], "far"), "p": (kept["p"], "far"), "wqkv": weights["wqkv"]}
+        | {"wp": (weights["wp"][0], "near"), "wqkv": (weights["wqkv"][0], "near")}
+        | {"qkv": (kept["qkv"], "near"), "p": (kept["p"], "near")}
         | {name: (kept[name], "far") for name in ("n1", "ctx", "n2", "act")},
         {"dx": rows(D, "near"), "keep": HALF, "give": HALF},
         {

time: 154 us -> 154 us (level)
  no operation moved by 1% of the time
where the time goes in v6:
time: 154 us; the launch traced here: 153 us
  blocking collectives  53.3 us (35%)
  Pallas kernels  50.6 us (33%)
  waiting for transfers between devices  23.4 us (15%)
  starting transfers between devices  19.9 us (13%)
  local copies, waits for them, and re-layouts  3.75 us (2%)
    all_to_all x1, blocking collectives, exchanged(): lax.all_to_all(both, AXES, 0, 0, axis_index_groups=groups, tiled=True)  53.3 us
    pallas_call x6, Pallas kernels, launch(): pl.pallas_call(wrapped, out_shape=[pltpu.HBM(shape, dtype) if space in ('...  48.8 us
    ppermute x6, waiting for transfers between devices, rolled_twice(): part = lax.ppermute(part, AXES[:2], route)  9.13 us
    ppermute x6, starting transfers between devices, rolled_twice(): part = lax.ppermute(part, AXES[:2], route)  8.59 us
    all_to_all x1, starting transfers between devices, body(): tables = lax.all_to_all(run_lines(spread), AXES, 0, 0, tiled=True)  6.83 us
    all_to_all x1, waiting for transfers between devices, body(): tables = lax.all_to_all(run_lines(spread), AXES, 0, 0, tiled=True)  6.58 us
    ppermute x2, waiting for transfers between devices, swapped(): lax.ppermute(block, 'wa', [(i, i ^ 1) for i in range(lax.axis_size('wa'))])  3.97 us
    ppermute x2, waiting for transfers between devices, passed_along(): return lax.ppermute(block, axis, route)  3.76 us
  transfers between devices with their start and end apart: 11, of which 6 were waited for; matrix products, arithmetic and copies ran while one was open for 1% of the time, Pallas kernels for 17%

profile of v6, /device:TPU:1, one launch (start us, length us, event | category | flops | bytes accessed | tf_op | source)
XLA Modules:
  0.0 153.3 jit_solution(5388105104898684274)
XLA Ops:
  0.6 0.9 copy.30
  1.6 8.1 %shard_map.203 = (bf16[224,384]{1,0:T(8,128)(2,1)}, bf16[224,1152]{1,0:T(8,128)(2,1)}, bf16[12,224,224]{2,1,0:T(8,128)(2,1)}, bf16[224,384]{1,0:T(8,128)(2,1)}, ...) custom-call(bf16[224,384]{1,0:T(8,128)(2,1)S(1)} %bitcast.23, ...), custom_call_target="tpu_custom_call" | custom-call | tf_op jit(solution)/shard_map/pallas_call | solution.py:89
  10.2 3.7 %collective-permute-start.1 = (bf16[2,2,4,7,384]{4,1,3,2,0:T(2,128)(2,1)S(1)}, bf16[2,2,4,7,384]{4,1,3,2,0:T(2,128)(2,1)S(1)}, u32[]{:S(2)}, u32[]{:S(2)}) collective-permute-start(bf16[2,2,4,7,384]{4,1,3,2,0:T(2,128)(2,1)S(1)} %get-tuple-element.80), channel_id=1, source_target_pairs={{0,64},{8,72},{16,80},{24,88},{32,96},{40,104},{48,112},{56,120},{... | collective-permute-start | bytes 258056 | tf_op jit(solution)/shard_map/ppermute | solution.py:635
  13.9 2.8 %collective-permute-start = (bf16[2,2,3,7,384]{4,1,3,2,0:T(2,128)(2,1)S(1)}, bf16[2,2,3,7,384]{4,1,3,2,0:T(2,128)(2,1)S(1)}, u32[]{:S(2)}, u32[]{:S(2)}) collective-permute-start(bf16[2,2,3,7,384]{4,1,3,2,0:T(2,128)(2,1)S(1)} %get-tuple-element.81), channel_id=1, source_target_pairs={{0,56},{8,0},{16,8},{24,16},{32,24},{40,32},{48,40},{56,48},{64,12... | collective-permute-start | bytes 193544 | tf_op jit(solution)/shard_map/ppermute | solution.py:635
  16.8 0.8 collective-permute-start.2
  18.1 3.0 %collective-permute-done.2 = bf16[2,2,3,7,384]{4,1,3,2,0:T(2,128)(2,1)S(1)} collective-permute-done((bf16[2,2,3,7,384]{4,1,3,2,0:T(2,128)(2,1)S(1)}, bf16[2,2,3,7,384]{4,1,3,2,0:T(2,128)(2,1)S(1)}, u32[]{:S(2)}, u32[]{:S(2)}) %collective-permute-start.2) | collective-permute-done | bytes 64544 | tf_op jit(solution)/shard_map/ppermute | solution.py:635
  21.2 2.4 %collective-permute-start.3 = (bf16[2,4,7,3,384]{4,1,3,2,0:T(4,128)(2,1)S(1)}, bf16[2,4,7,3,384]{4,1,3,2,0:T(4,128)(2,1)S(1)}, u32[]{:S(2)}, u32[]{:S(2)}) collective-permute-start(bf16[2,4,7,3,384]{4,1,3,2,0:T(4,128)(2,1)S(1)} %maximum_maximum_fusion.2), channel_id=1, source_target_pairs={{1,0},{2,1},{3,2},{4,3},{5,4},{6,5},{7,6},{0,7},{9,8},{10,9},{11,1... | collective-permute-start | bytes 387080 | tf_op jit(solution)/shard_map/ppermute | solution.py:590
  24.1 3.8 %collective-permute-done.3 = bf16[2,4,7,3,384]{4,1,3,2,0:T(4,128)(2,1)S(1)} collective-permute-done((bf16[2,4,7,3,384]{4,1,3,2,0:T(4,128)(2,1)S(1)}, bf16[2,4,7,3,384]{4,1,3,2,0:T(4,128)(2,1)S(1)}, u32[]{:S(2)}, u32[]{:S(2)}) %collective-permute-start.3) | collective-permute-done | bytes 129056 | tf_op jit(solution)/shard_map/ppermute | solution.py:590
  28.2 11.4 %shard_map.204 = (bf16[224,384]{1,0:T(8,128)(2,1)}, bf16[224,384]{1,0:T(8,128)(2,1)}, bf16[224,384]{1,0:T(8,128)(2,1)}, bf16[224,1536]{1,0:T(8,128)(2,1)}, bf16[...) custom-call(bf16[224,384]{1,0:T(8,128)(2,1)S(1)} %bitcast.28, ...), custom_call_target="tpu_custom_call" | custom-call | tf_op jit(solution)/shard_map/pallas_call | solution.py:89
  40.3 0.7 collective-permute-start.4
  41.0 5.6 %collective-permute-done.4 = bf16[2,3,7,384]{3,2,1,0:T(8,128)(2,1)S(1)} collective-permute-done((bf16[2,3,7,384]{3,2,1,0:T(8,128)(2,1)S(1)}, bf16[2,3,7,384]{3,2,1,0:T(8,128)(2,1)S(1)}, u32[]{:S(2)}, u32[]{:S(2)}) %collective-permute-start.4) | collective-permute-done | bytes 32288 | tf_op jit(solution)/shard_map/ppermute | solution.py:635
  46.7 1.3 collective-permute-start.7
  48.1 10.1 %shard_map.205 = (bf16[7168,128]{1,0:T(8,128)(2,1)}, bf16[7168,128]{1,0:T(8,128)(2,1)}, bf16[224,384]{1,0:T(8,128)(2,1)S(1)}) custom-call(s32[1]{0:T(128)} %bitcast.refs_0_, bf16[224,384]{1,0:T(8,128)(2,1)S(1)} %bitcast.26, bf16[224,384]{1,0:T(8,128)(2,1)S(1)} %bitcast.29, bf16[224,384]{1,0:T(8,128)(2,1)} %get-tuple-element.45.refs_3_, ...), custom_call_target="tpu_custom_call" | custom-call | tf_op jit(solution)/shard_map/pallas_call | solution.py:89
  58.2 0.7 collective-permute-start.9
  59.1 12.5 %shard_map.206 = (bf16[224,384]{1,0:T(8,128)(2,1)S(1)}, bf16[7168,128]{1,0:T(8,128)(2,1)}, bf16[7168,128]{1,0:T(8,128)(2,1)}) custom-call(s32[1]{0:T(128)} %bitcast.refs_0_, bf16[224,384]{1,0:T(8,128)(2,1)S(1)} %bitcast.27, bf16[224,384]{1,0:T(8,128)(2,1)S(1)} %bitcast.24, bf16[1536,384]{1,0:T(8,128)(2,1)S(1)} %copy-done.1, bf16[224,1536]{1,0:T(8,128)(2,1)S(1)} %copy-done.8, ...), custom_call_target="tpu_custom_call" | custom-call | tf_op jit(solution)/shard_map/pallas_call | solution.py:89
  71.7 4.0 %collective-permute-done.8.refs_2_ = bf16[7168,128]{1,0:T(8,128)(2,1)S(1)} collective-permute-done((bf16[7168,128]{1,0:T(8,128)(2,1)}, bf16[7168,128]{1,0:T(8,128)(2,1)S(1)}, u32[]{:S(2)}, u32[]{:S(2)}) %collective-permute-start.8) | collective-permute-done | bytes 1835040 | tf_op jit(solution)/shard_map/ppermute | solution.py:651
  75.7 3.8 %shard_map.207 = bf16[14336,128]{1,0:T(8,128)(2,1)} custom-call(bf16[7168,128]{1,0:T(8,128)(2,1)} %get-tuple-element.63.refs_0_, bf16[7168,128]{1,0:T(8,128)(2,1)} %get-tuple-element.64.refs_1_, bf16[7168,128]{1,0:T(8,128)(2,1)S(1)} %collective-permute-done.8.refs_2_, bf16[7168,128]{1,0:T(8,128)(2,1)S(1)} %collective-permute-done.9.refs_3_), custom_call_target="tpu_custom_call" | custom-call | tf_op jit(solution)/shard_map/pallas_call | solution.py:89
  79.5 53.3 %all_to_all.10.refs_0_.spread = bf16[64,224,128]{2,1,0:T(8,128)(2,1)} all-to-all(bf16[64,224,128]{2,1,0:T(8,128)(2,1)} %bitcast.35), channel_id=1, replica_groups={{0,2,4,6,8,10,12,14,16,18,20,22,24,26,28,30,32,34,36,38,40,42,44,46,48,..., dimensions={0} | all-to-all | bytes 7340032 | tf_op jit(solution)/shard_map/all_to_all | solution.py:656
  132.8 1.8 %shard_map.209 = f32[128,2,128]{2,1,0:T(2,128)} custom-call(bf16[64,224,128]{2,1,0:T(8,128)(2,1)} %all_to_all.10.refs_0_.spread), custom_call_target="tpu_custom_call" | custom-call | tf_op jit(solution)/shard_map/pallas_call | solution.py:564
  134.6 6.8 %all-to-all-start.1 = ((f32[128,2,128]{2,1,0:T(2,128)}), f32[128,2,128]{2,1,0:T(2,128)S(1)}, u32[]{:S(2)}, u32[]{:S(2)}) async-start(f32[128,2,128]{2,1,0:T(2,128)} %shard_map.209), calls=%async_computation.1 | async-start | bytes 262144 | tf_op jit(solution)/shard_map/all_to_all | solution.py:686
  141.4 0.7 copy.29
  142.2 2.9 %shard_map.208 = (f32[3,1152]{1,0:T(4,128)}, f32[3,384]{1,0:T(4,128)}, f32[3,1536]{1,0:T(4,128)}, f32[12,384]{1,0:T(8,128)}, f32[3,1152]{1,0:T(4,128)}, /*index=...) custom-call(bf16[64,224,128]{2,1,0:T(8,128)(2,1)} %all_to_all.10.refs_0_.spread), custom_call_target="tpu_custom_call" | custom-call | tf_op jit(solution)/shard_map/pallas_call | solution.py:89
  145.1 6.6 %all-to-all-done.1 = f32[128,2,128]{2,1,0:T(2,128)S(1)} async-done(((f32[128,2,128]{2,1,0:T(2,128)}), f32[128,2,128]{2,1,0:T(2,128)S(1)}, u32[]{:S(2)}, u32[]{:S(2)}) %all-to-all-start.1) | async-done | bytes 131104 | tf_op jit(solution)/shard_map/all_to_all | solution.py:686
  152.0 0.6 reshape_squeeze.7
  (58 shorter events, 3.8 us)
Async XLA Ops:
  10.1 18.1 %copy-start.4 = (bf16[384,1536]{1,0:T(8,128)(2,1)S(1)}, bf16[384,1536]{1,0:T(8,128)(2,1)}, u32[]{:S(2)}) copy-start(bf16[384,1536]{1,0:T(8,128)(2,1)} %refs_5_.4) | copy-start | bytes 3538948
  10.1 18.1 %copy-start.5 = (bf16[1536,384]{1,0:T(8,128)(2,1)S(1)}, bf16[1536,384]{1,0:T(8,128)(2,1)}, u32[]{:S(2)}) copy-start(bf16[1536,384]{1,0:T(8,128)(2,1)} %refs_6_.1) | copy-start | bytes 3538948
  10.1 18.0 %copy-start.7 = (bf16[384,1152]{1,0:T(8,128)(2,1)S(1)}, bf16[384,1152]{1,0:T(8,128)(2,1)}, u32[]{:S(2)}) copy-start(bf16[384,1152]{1,0:T(8,128)(2,1)} %refs_3_.4) | copy-start | bytes 2654212
  10.2 18.0 %copy-start.10 = (bf16[384,384]{1,0:T(8,128)(2,1)S(1)}, bf16[384,384]{1,0:T(8,128)(2,1)}, u32[]{:S(2)}) copy-start(bf16[384,384]{1,0:T(8,128)(2,1)} %refs_4_.3) | copy-start | bytes 884740
  10.2 18.0 %copy-start.12 = (f32[12,1183]{1,0:T(8,128)S(1)}, f32[12,1183]{1,0:T(8,128)}, u32[]{:S(2)}) copy-start(f32[12,1183]{1,0:T(8,128)} %refs_2_.3) | copy-start | bytes 170356
  10.2 10.9 %collective-permute-start.1 = (bf16[2,2,4,7,384]{4,1,3,2,0:T(2,128)(2,1)S(1)}, bf16[2,2,4,7,384]{4,1,3,2,0:T(2,128)(2,1)S(1)}, u32[]{:S(2)}, u32[]{:S(2)}) collective-permute-start(bf16[2,2,4,7,384]{4,1,3,2,0:T(2,128)(2,1)S(1)} %get-tuple-element.80), channel_id=1, source_target_pairs={{0,64},{8,72},{16,80},{24,88},{32,96},{40,104},{48,112},{56,120},{... | collective-permute-start | bytes 258056 | tf_op jit(solution)/shard_map/ppermute | solution.py:635
  13.9 4.2 %collective-permute-start = (bf16[2,2,3,7,384]{4,1,3,2,0:T(2,128)(2,1)S(1)}, bf16[2,2,3,7,384]{4,1,3,2,0:T(2,128)(2,1)S(1)}, u32[]{:S(2)}, u32[]{:S(2)}) collective-permute-start(bf16[2,2,3,7,384]{4,1,3,2,0:T(2,128)(2,1)S(1)} %get-tuple-element.81), channel_id=1, source_target_pairs={{0,56},{8,0},{16,8},{24,16},{32,24},{40,32},{48,40},{56,48},{64,12... | collective-permute-start | bytes 193544 | tf_op jit(solution)/shard_map/ppermute | solution.py:635
  16.8 4.3 %collective-permute-start.2 = (bf16[2,2,3,7,384]{4,1,3,2,0:T(2,128)(2,1)S(1)}, bf16[2,2,3,7,384]{4,1,3,2,0:T(2,128)(2,1)S(1)}, u32[]{:S(2)}, u32[]{:S(2)}) collective-permute-start(bf16[2,2,3,7,384]{4,1,3,2,0:T(2,128)(2,1)S(1)} %get-tuple-element.82), channel_id=1, source_target_pairs={{0,120},{8,64},{16,72},{24,80},{32,88},{40,96},{48,104},{56,112},{... | collective-permute-start | bytes 193544 | tf_op jit(solution)/shard_map/ppermute | solution.py:635
  21.2 6.6 %collective-permute-start.3 = (bf16[2,4,7,3,384]{4,1,3,2,0:T(4,128)(2,1)S(1)}, bf16[2,4,7,3,384]{4,1,3,2,0:T(4,128)(2,1)S(1)}, u32[]{:S(2)}, u32[]{:S(2)}) collective-permute-start(bf16[2,4,7,3,384]{4,1,3,2,0:T(4,128)(2,1)S(1)} %maximum_maximum_fusion.2), channel_id=1, source_target_pairs={{1,0},{2,1},{3,2},{4,3},{5,4},{6,5},{7,6},{0,7},{9,8},{10,9},{11,1... | collective-permute-start | bytes 387080 | tf_op jit(solution)/shard_map/ppermute | solution.py:590
  28.2 30.8 %copy-start.9 = (bf16[224,1152]{1,0:T(8,128)(2,1)S(1)}, bf16[224,1152]{1,0:T(8,128)(2,1)}, u32[]{:S(2)}) copy-start(bf16[224,1152]{1,0:T(8,128)(2,1)} %get-tuple-element.56.refs_9_) | copy-start | bytes 1548292
  39.7 6.9 %collective-permute-start.5 = (bf16[2,4,7,384]{3,2,1,0:T(8,128)(2,1)S(1)}, bf16[2,4,7,384]{3,2,1,0:T(8,128)(2,1)S(1)}, u32[]{:S(2)}, u32[]{:S(2)}) collective-permute-start(bf16[2,4,7,384]{3,2,1,0:T(8,128)(2,1)S(1)} %get-tuple-element.85), channel_id=1, source_target_pairs={{0,64},{8,72},{16,80},{24,88},{32,96},{40,104},{48,112},{56,120},{... | collective-permute-start | bytes 129032 | tf_op jit(solution)/shard_map/ppermute | solution.py:635
  40.3 18.8 %copy-start.11 = (bf16[224,384]{1,0:T(8,128)(2,1)S(1)}, bf16[224,384]{1,0:T(8,128)(2,1)}, u32[]{:S(2)}) copy-start(bf16[224,384]{1,0:T(8,128)(2,1)} %get-tuple-element.55.refs_6_) | copy-start | bytes 516100
  40.3 6.3 %collective-permute-start.4 = (bf16[2,3,7,384]{3,2,1,0:T(8,128)(2,1)S(1)}, bf16[2,3,7,384]{3,2,1,0:T(8,128)(2,1)S(1)}, u32[]{:S(2)}, u32[]{:S(2)}) collective-permute-start(bf16[2,3,7,384]{3,2,1,0:T(8,128)(2,1)S(1)} %get-tuple-element.83), channel_id=1, source_target_pairs={{0,72},{8,80},{16,88},{24,96},{32,104},{40,112},{48,120},{56,64},{... | collective-permute-start | bytes 96776 | tf_op jit(solution)/shard_map/ppermute | solution.py:635
  41.0 5.6 %collective-permute-start.6 = (bf16[2,3,7,384]{3,2,1,0:T(8,128)(2,1)S(1)}, bf16[2,3,7,384]{3,2,1,0:T(8,128)(2,1)S(1)}, u32[]{:S(2)}, u32[]{:S(2)}) collective-permute-start(bf16[2,3,7,384]{3,2,1,0:T(8,128)(2,1)S(1)} %get-tuple-element.84), channel_id=1, source_target_pairs={{0,8},{8,16},{16,24},{24,32},{32,40},{40,48},{48,56},{56,0},{64,72... | collective-permute-start | bytes 96776 | tf_op jit(solution)/shard_map/ppermute | solution.py:635
  46.6 12.4 %copy-start.8 = (bf16[224,1536]{1,0:T(8,128)(2,1)S(1)}, bf16[224,1536]{1,0:T(8,128)(2,1)}, u32[]{:S(2)}) copy-start(bf16[224,1536]{1,0:T(8,128)(2,1)} %get-tuple-element.54.refs_4_) | copy-start | bytes 2064388
  46.7 12.2 %collective-permute-start.7 = (bf16[4,7,3,384]{3,2,1,0:T(4,128)(2,1)S(1)}, bf16[4,7,3,384]{3,2,1,0:T(4,128)(2,1)S(1)}, u32[]{:S(2)}, u32[]{:S(2)}) collective-permute-start(bf16[4,7,3,384]{3,2,1,0:T(4,128)(2,1)S(1)} %slice.115), channel_id=1, source_target_pairs={{7,0},{0,1},{1,2},{2,3},{3,4},{4,5},{5,6},{6,7},{15,8},{8,9},{9,10... | collective-permute-start | bytes 193544 | tf_op jit(solution)/shard_map/ppermute | solution.py:590
  48.0 11.0 %copy-start.6 = (bf16[384,384]{1,0:T(8,128)(2,1)S(1)}, bf16[384,384]{1,0:T(8,128)(2,1)}, u32[]{:S(2)}) copy-start(bf16[384,384]{1,0:T(8,128)(2,1)} %refs_7_.1) | copy-start | bytes 884740
  48.1 11.0 %copy-start = (bf16[384,1536]{1,0:T(8,128)(2,1)S(1)}, bf16[384,1536]{1,0:T(8,128)(2,1)}, u32[]{:S(2)}) copy-start(bf16[384,1536]{1,0:T(8,128)(2,1)} %refs_5_.5) | copy-start | bytes 3538948
  48.1 11.0 %copy-start.1 = (bf16[1536,384]{1,0:T(8,128)(2,1)S(1)}, bf16[1536,384]{1,0:T(8,128)(2,1)}, u32[]{:S(2)}) copy-start(bf16[1536,384]{1,0:T(8,128)(2,1)} %refs_3_.5) | copy-start | bytes 3538948
  48.1 11.0 %copy-start.2 = (bf16[384,1152]{1,0:T(8,128)(2,1)S(1)}, bf16[384,1152]{1,0:T(8,128)(2,1)}, u32[]{:S(2)}) copy-start(bf16[384,1152]{1,0:T(8,128)(2,1)} %refs_8_.1) | copy-start | bytes 2654212
  48.1 11.0 %copy-start.3 = (bf16[12,224,224]{2,1,0:T(8,128)(2,1)S(1)}, bf16[12,224,224]{2,1,0:T(8,128)(2,1)}, u32[]{:S(2)}) copy-start(bf16[12,224,224]{2,1,0:T(8,128)(2,1)} %get-tuple-element.57.refs_10_) | copy-start | bytes 3612676
  58.2 13.4 %collective-permute-start.9 = (bf16[7168,128]{1,0:T(8,128)(2,1)}, bf16[7168,128]{1,0:T(8,128)(2,1)S(1)}, u32[]{:S(2)}, u32[]{:S(2)}) collective-permute-start(bf16[7168,128]{1,0:T(8,128)(2,1)} %get-tuple-element.66), channel_id=1, source_target_pairs={{0,1},{1,0},{2,3},{3,2},{4,5},{5,4},{6,7},{7,6},{8,9},{9,8},{10,11... | collective-permute-start | bytes 5505032 | tf_op jit(solution)/shard_map/ppermute | solution.py:651
  71.6 4.1 %collective-permute-start.8 = (bf16[7168,128]{1,0:T(8,128)(2,1)}, bf16[7168,128]{1,0:T(8,128)(2,1)S(1)}, u32[]{:S(2)}, u32[]{:S(2)}) collective-permute-start(bf16[7168,128]{1,0:T(8,128)(2,1)} %get-tuple-element.65), channel_id=1, source_target_pairs={{0,1},{1,0},{2,3},{3,2},{4,5},{5,4},{6,7},{7,6},{8,9},{9,8},{10,11... | collective-permute-start | bytes 5505032 | tf_op jit(solution)/shard_map/ppermute | solution.py:651
  134.6 17.1 %all-to-all-start.1 = ((f32[128,2,128]{2,1,0:T(2,128)}), f32[128,2,128]{2,1,0:T(2,128)S(1)}, u32[]{:S(2)}, u32[]{:S(2)}) async-start(f32[128,2,128]{2,1,0:T(2,128)} %shard_map.209), calls=%async_computation.1 | async-start | bytes 262144 | tf_op jit(solution)/shard_map/all_to_all | solution.py:686
  (1 other events, 8.2 us)
